TPU v7x, 32 devices: a whole 2x2x4 slice. The times are simulated.
32 devices in a mesh: panel: 4 (over x, core), obs: 8 (over z, y).
Axes of the slice: x: 2, y: 2, z: 4, core: 2. Of those that a mesh axis runs over, the one named last changes fastest.
Arguments:
- les_rows: bfloat16 [4096, 2, 128], P(('panel', 'obs')), may hold values from -6 to 6
- les_dest: int32 [4096, 1], P(('panel', 'obs')), may hold values from 0 to 31; in each aligned block of 128 rows (0 to 127, 128 to 255, ...) at most 8 rows name the same one
- loading_weight: bfloat16 [8192, 1024], P('panel', 'obs'), may hold values from -0.09375 to 0.09375
- thickness_weight: bfloat16 [8192, 1024], P('panel', 'obs'), may hold values from -0.09375 to 0.09375
- delays: int32 [16, 8], P('panel', 'obs'), may hold values from 0 to 64
Outputs:
- acoustic_pressure: float32 [128, 1024], P('panel', 'obs')
Inputs may be any that keep to these rules, and one draw needn't show every extreme that they name: `les_dest`: in the aligned blocks of 128 rows of one LES owner, no destination is named by more than 8 rows, a bound that some block reaches; every destination is named by some row.
All inputs are finite; a program needn't handle non-finite values.
Results may differ from a plain program's by a relative error of at most 0.0018.
Values may be sent and summed in bfloat16 or wider, within the bound.
No kernel may reach another device: no remote copies, remote signals or barrier semaphores. Data moves between devices by JAX's collectives and lax.ppermute only.
A program may use at most 64 MiB of HBM per device.

v0:
```python
import jax
import jax.numpy as jnp
from jax import lax
from jax.sharding import PartitionSpec as P

PBLK = 512


def owner_ranks(dest_block, count):
    onehot = (dest_block[:, :, None] == jnp.arange(count, dtype=jnp.int32)[None, None, :]).astype(
        jnp.int32
    )
    earlier = jnp.cumsum(onehot, axis=1) - onehot
    return jnp.sum(earlier * onehot, axis=2)


def delay_block(block, delay):
    steps = block.shape[0]
    padded = jnp.concatenate([jnp.zeros_like(block), block], axis=0)
    start = steps - delay
    return lax.dynamic_slice_in_dim(padded, start, steps, 0)


def shift_time(values, delay_row):
    steps = values.shape[0]
    blocks = delay_row.shape[0]
    shaped = values.reshape(steps, blocks, -1)
    moved = jax.vmap(delay_block, in_axes=(1, 0), out_axes=1)(shaped, delay_row)
    return moved.reshape(steps, -1)


def per_device(les_rows, les_dest, loading_weight, thickness_weight, delays):
    n_panel = lax.axis_size("panel")
    n_obs = lax.axis_size("obs")
    count = n_panel * n_obs
    rows_dev = les_rows.shape[0]
    steps = les_rows.shape[2]
    cap = 2 * rows_dev // count
    dest = les_dest[:, 0]
    rank = owner_ranks(dest.reshape(1, rows_dev), count)[0]
    position = dest * cap + rank
    buffer = jnp.zeros((count * cap, 2, steps), les_rows.dtype).at[position].set(les_rows)
    arrived = lax.all_to_all(
        buffer.reshape(count, cap, 2, steps),
        ("panel", "obs"),
        split_axis=0,
        concat_axis=0,
        tiled=True,
    )
    local = arrived.reshape(count * cap, 2, steps)
    group = lax.all_gather(local, "obs", axis=0, tiled=True)
    velocity = group[:, 1, :].astype(jnp.float32)
    padded = jnp.pad(velocity, ((0, 0), (1, 1)))
    rate = ((padded[:, 2:] - padded[:, :-2]) * 0.5).astype(jnp.bfloat16)
    pressure_src = group[:, 0, :]
    nblocks = group.shape[0] // PBLK
    width = loading_weight.shape[1]
    press_blocks = pressure_src.reshape(nblocks, PBLK, steps)
    rate_blocks = rate.reshape(nblocks, PBLK, steps)
    load_blocks = loading_weight.reshape(nblocks, PBLK, width)
    thick_blocks = thickness_weight.reshape(nblocks, PBLK, width)

    def one_block(total, inputs):
        press_b, rate_b, load_b, thick_b, delay_b = inputs
        dims = (((0,), (0,)), ((), ()))
        term = lax.dot_general(press_b, load_b, dims, preferred_element_type=jnp.float32)
        term = term + lax.dot_general(rate_b, thick_b, dims, preferred_element_type=jnp.float32)
        return (total + shift_time(term, delay_b), None)

    start = jnp.zeros((steps, width), jnp.float32)
    partial_sum, unused = lax.scan(
        one_block, start, (press_blocks, rate_blocks, load_blocks, thick_blocks, delays)
    )
    return lax.psum_scatter(partial_sum, "panel", scatter_dimension=0, tiled=True)


def solution(mesh):
    placed = (
        P(("panel", "obs"), None, None),
        P(("panel", "obs"), None),
        P("panel", "obs"),
        P("panel", "obs"),
        P("panel", "obs"),
    )
    return jax.shard_map(
        per_device, mesh=mesh, in_specs=placed, out_specs=P("panel", "obs"), check_vma=False
    )
```

profile of v0, /device:TPU:0, one launch (start us, length us, event | category | flops | bytes accessed | tf_op | source)
XLA Modules:
  0.0 119.4 jit_solution(9557809047722529191)
XLA Ops:
  6.5 0.0 all-gather.2.cloned.1.call-start
  6.5 0.7 fusion.16
  7.3 0.2 reduce_window_sum.11
  7.5 0.8 select_reduce_fusion
  8.3 0.7 fusion.17
  9.0 0.1 broadcast_in_dim.15
  9.0 9.7 %scatter_fusion = bf16[256,2,128]{2,1,0:T(2,128)(2,1)S(1)} fusion(bf16[256,2,128]{2,1,0:T(2,128)(2,1)S(1)} %broadcast_in_dim.15, s32[128]{0:T(128)S(1)} %fusion.17, bf16[128,2,128]{2,1,0:T(2,128)(2,1)} %param.7), kind=kCustom, calls=%fused_computation | custom fusion | bytes 197120 | tf_op jit(solution)/shard_map/scatter | solution.py:42
  18.8 14.8 %all_to_all.5 = bf16[32,8,2,128]{3,2,1,0:T(2,128)(2,1)S(1)} all-to-all(bf16[32,8,2,128]{3,2,1,0:T(2,128)(2,1)S(1)} %bitcast.58), channel_id=1, replica_groups=mesh['panel'=4,'obs'=8] {'panel','obs'}, dimensions={0} | all-to-all | bytes 262144 | tf_op jit(solution)/shard_map/all_to_all | solution.py:43
  33.6 0.7 copy.6
  34.3 0.0 all-gather.2.cloned.1.call-update
  34.3 0.0 reduce-scatter.2.cloned.1.call-start
  34.4 38.1 %all-gather.2.cloned.1.call-done = bf16[2048,2,128]{2,0,1:T(8,128)(2,1)} async-done(((bf16[256,2,128]{2,0,1:T(8,128)(2,1)}), bf16[2048,2,128]{2,0,1:T(8,128)(2,1)}) %all-gather.2.cloned.1.call-update) | async-done | bytes 1048592 | tf_op jit(solution)/shard_map/all_gather | solution.py:51
  72.5 1.3 %slice_bitcast_fusion = (bf16[2048,128]{1,0:T(8,128)(2,1)S(1)}, bf16[2048,1,128]{2,0,1:T(8,128)(2,1)S(1)}) fusion(bf16[2048,2,128]{2,0,1:T(8,128)(2,1)} %all-gather.2.cloned.1.call-done), kind=kLoop, calls=%fused_computation.22 | loop fusion | bytes 2097152 | tf_op jit(solution)/shard_map/convert_element_type | solution.py:52
  73.8 0.0 copy-start.1
  73.8 0.3 pad_convert_fusion
  74.2 0.3 fusion.15
  74.5 0.0 copy-done.1
  74.5 19.1 %while.14 = (s32[]{:T(128)}, f32[128,128]{1,0:T(8,128)S(1)}, bf16[4,512,128]{2,1,0:T(8,128)(2,1)S(1)}, bf16[4,512,128]{2,1,0:T(8,128)(2,1)}, bf16[4,512,128]{2,1...) while((s32[]{:T(128)}, f32[128,128]{1,0:T(8,128)S(1)}, ...), condition=%wide.region_4.5_spmd.clone, body=%wide.region_3.4_spmd.clone.sunk | while | flops 33603588 | bytes 919725 | solution.py:71
  74.5 0.7 fusion.31
  76.9 1.1 fusion.32
  78.1 1.1 fusion.33
  79.2 0.1 fusion.34
  79.3 0.7 fusion.31
  81.7 1.1 fusion.32
  82.8 1.1 fusion.33
  84.0 0.1 fusion.34
  84.1 0.7 fusion.31
  86.5 1.1 fusion.32
  87.6 1.1 fusion.33
  88.8 0.1 fusion.34
  88.8 0.7 fusion.31
  91.2 1.1 fusion.32
  92.4 1.1 fusion.33
  93.5 0.1 fusion.34
  93.6 0.0 copy-start
  93.6 0.6 copy-done
  94.2 0.0 reduce-scatter.2.cloned.1.call-update
  94.2 18.3 %reduce-scatter.2.cloned.1.call-done = f32[32,128]{1,0:T(8,128)} async-done(((f32[128,128]{1,0:T(8,128)}), f32[32,128]{1,0:T(8,128)}) %reduce-scatter.2.cloned.1.call-update) | async-done | bytes 16400 | tf_op jit(solution)/shard_map/reduce_scatter | solution.py:74
  (1 shorter events, 0.0 us)
Async XLA Ops:
  6.5 66.0 %all-gather.2.cloned.1.call-start = ((), (), s32[]{:S(2)}) async-start(), calls=%async_computation.2 | async-start | bytes 1179648 | tf_op jit(solution)/shard_map/all_gather | solution.py:51
  34.3 78.3 %reduce-scatter.2.cloned.1.call-start = ((), (), s32[]{:S(2)}) async-start(), calls=%async_computation.3 | async-start | bytes 81920 | tf_op jit(solution)/shard_map/reduce_scatter | solution.py:74
  73.8 0.7 copy-start.1
  93.6 0.6 copy-start
Sparse Core Ops, SparseCore 0:
  34.4 38.0 all-gather.1
  94.4 18.1 reduce-scatter.1
where the time goes:
time: 120 us; the launch traced here: 119 us
  waiting for transfers between devices  56.5 us (47%)
  blocking collectives  14.8 us (12%)
  between operations  13.5 us (11%)
  local copies, waits for them, and re-layouts  12.4 us (10%)
  matrix products  9.07 us (8%)
  loops' own time  7.18 us (6%)
  other arithmetic  5.91 us (5%)
    all_gather x1, waiting for transfers between devices, per_device(): group = lax.all_gather(local, 'obs', axis=0, tiled=True)  38.1 us
    reduce_scatter x1, waiting for transfers between devices, per_device(): lax.psum_scatter(partial_sum, 'panel', scatter_dimension=0, tiled=True)  18.3 us
    all_to_all x1, blocking collectives, per_device(): lax.all_to_all(buffer.reshape(count, cap, 2, steps), ('panel', 'obs'), sp...  14.8 us
    scatter x1, local copies, waits for them, and re-layouts, per_device(): jnp.zeros((count * cap, 2, steps), les_rows.dtype).at[position]  9.74 us
    another operation x1, loops' own time, per_device(): lax.scan(one_block, start, (press_blocks, rate_blocks, load_blocks, thick...  7.18 us
    dot_general x4, matrix products, one_block(): lax.dot_general(rate_b, thick_b, dims, preferred_element_type=jnp.float32)  4.54 us
    dot_general x4, matrix products, one_block(): lax.dot_general(press_b, load_b, dims, preferred_element_type=jnp.float32)  4.53 us
    sub x4, other arithmetic, delay_block(): start = steps - delay  2.6 us
  transfers between devices with their start and end apart: 2, of which 2 were waited for; matrix products, arithmetic and copies ran while one was open for 0% of the time, Pallas kernels for 0%

commit v1 on v0

v1 whole, which is shorter than its diff:
```python
import functools

import jax
import jax.numpy as jnp
from jax import lax
from jax.experimental import pallas as pl
from jax.experimental.pallas import tpu as pltpu
from jax.sharding import PartitionSpec as P

PBLK = 512
EXTRA = 16
VMEM_LIMIT = 48 * 1024 * 1024


def dot(a, b):
    return lax.dot_general(a, b, (((1,), (0,)), ((), ())), preferred_element_type=jnp.float32)


def slot_kernel(n_panel, n_obs, cap, a_ref, b_ref, ya_ref, yb_ref, out_ref, slots_ref):
    count = n_panel * n_obs
    me_p = lax.axis_index("panel")
    me_o = lax.axis_index("obs")
    rows = a_ref.shape[0] // (n_obs // 4) - EXTRA
    steps = a_ref.shape[1] // 2
    per = 16 // cap
    half = n_obs // 4
    r0 = lax.broadcasted_iota(jnp.int32, (rows, rows), 0)
    r1 = lax.broadcasted_iota(jnp.int32, (rows, rows), 1)
    earlier = (r0 < r1).astype(jnp.bfloat16)
    t0 = lax.broadcasted_iota(jnp.int32, (steps, steps), 0)
    t1 = lax.broadcasted_iota(jnp.int32, (steps, steps), 1)
    slope = jnp.where(t0 == t1 + 1, 0.5, jnp.where(t0 == t1 - 1, -0.5, 0.0)).astype(jnp.bfloat16)
    dest_ids = lax.broadcasted_iota(jnp.int32, (count, rows), 0)
    slot_ids = lax.broadcasted_iota(jnp.int32, (count * 16, per * rows), 0)
    for quad in range(n_obs // per):
        values, places = [], []
        for i in range(per):
            j = quad * per + i
            k, y = j // 2, j % 2
            ref = ((a_ref, ya_ref), (b_ref, yb_ref))[k // half][y]
            base = (k % half) * (rows + EXTRA)
            dest = ref[base + rows : base + rows + EXTRA, 0:rows].astype(jnp.float32)[0:1]
            dest = dest.astype(jnp.int32)
            onehot = dest_ids == dest
            before = dot(onehot.astype(jnp.bfloat16), earlier)
            rank = jnp.sum(jnp.where(onehot, before, 0.0), axis=0, keepdims=True).astype(jnp.int32)
            within = ((me_o % per) ^ i) * cap + rank
            places.append((dest ^ (me_p * n_obs)) * 16 + within)
            rate = dot(ref[base : base + rows, steps:], slope).astype(jnp.bfloat16)
            values.append(jnp.concatenate([ref[base : base + rows, 0:steps], rate], axis=1))
        value = jnp.concatenate(values, axis=0)
        place = jnp.concatenate(places, axis=1)
        pick = (slot_ids == place).astype(jnp.bfloat16)
        got = dot(pick, value).astype(jnp.bfloat16)
        start = pl.multiple_of(((me_o // per) ^ quad) * 16, 16)
        slots_ref[:, pl.ds(start, 16), :] = got.reshape(count, 16, 2 * steps)
    for k in range(out_ref.shape[0]):
        block = slots_ref[2 * k : 2 * k + 2].reshape(2 * n_obs * cap, 2 * steps)
        out_ref[k, :, 0 : 2 * n_obs * cap] = block[:, 0:steps].T
        out_ref[k, :, 2 * n_obs * cap :] = block[:, steps:].T


def add_term(acc_ref, source, weights, delay):
    steps = source.shape[0]
    acc_ref[pl.ds(delay, steps), :] += dot(source, weights)


def near_kernel(n_obs, s_ref, load_ref, thick_ref, delay_ref, c_ref, out_ref, acc_ref):
    me_p = lax.axis_index("panel")
    steps = out_ref.shape[0]
    nblocks = n_obs // 2
    acc_ref[...] = jnp.zeros_like(acc_ref)
    width = load_ref.shape[2]
    for b in range(nblocks):
        weights = jnp.concatenate(
            [ref[2 * b + i, me_p] for ref in (load_ref, thick_ref) for i in range(2)], axis=0
        )
        add_term(acc_ref, s_ref[b], weights, delay_ref[b, 0])
    piece_terms(nblocks, width, s_ref, nblocks, c_ref, acc_ref)
    out_ref[...] = acc_ref[0:steps]


def piece_terms(nblocks, width, s_ref, first, w_ref, acc_ref):
    depth = 2 * width * nblocks
    delays = w_ref[2 * depth : 2 * depth + EXTRA, :].astype(jnp.float32)[0:1].astype(jnp.int32)
    for b in range(nblocks):
        lo, hi = 2 * width * b, 2 * width * (b + 1)
        weights = jnp.concatenate([w_ref[lo:hi], w_ref[depth + lo : depth + hi]], axis=0)
        add_term(acc_ref, s_ref[first + b], weights, delays[0, b])


def far_kernel(n_panel, n_obs, width, s_ref, near_ref, x_ref, xc_ref, *refs):
    outs, acc_ref = refs[:n_panel], refs[n_panel]
    me_p = lax.axis_index("panel")
    steps = near_ref.shape[0]
    nblocks = n_obs // 2
    acc_ref[0:steps] = near_ref[...]
    acc_ref[steps:] = jnp.zeros_like(acc_ref[steps:])
    piece_terms(nblocks, width, s_ref, 2 * nblocks, x_ref, acc_ref)
    piece_terms(nblocks, width, s_ref, 3 * nblocks, xc_ref, acc_ref)
    share = steps // n_panel
    for k in range(n_panel):
        start = pl.multiple_of((me_p ^ k) * share, share)
        outs[k][...] = acc_ref[pl.ds(start, share), :]


def per_device(les_rows, les_dest, loading_weight, thickness_weight, delays):
    n_panel = lax.axis_size("panel")
    n_obs = lax.axis_size("obs")
    count = n_panel * n_obs
    rows, _, steps = les_rows.shape
    cap = 2 * rows // count
    observers = loading_weight.shape[1]
    width = n_obs * cap
    nblocks = n_obs // 2
    me_p = lax.axis_index("panel")
    params = pltpu.CompilerParams(vmem_limit_bytes=VMEM_LIMIT)
    vmem = pl.BlockSpec(memory_space=pltpu.VMEM)
    smem = pl.BlockSpec(memory_space=pltpu.SMEM)

    def along_panel(value, k):
        return lax.ppermute(value, "panel", [(i, i ^ k) for i in range(n_panel)])

    def along_obs(value, k):
        return lax.ppermute(value, "obs", [(i, i ^ k) for i in range(n_obs)])

    load = loading_weight.reshape(n_obs, n_panel, width, observers)
    thick = thickness_weight.reshape(n_obs, n_panel, width, observers)
    delay_rows = jnp.pad(
        delays.reshape(1, nblocks).astype(jnp.bfloat16),
        ((0, EXTRA - 1), (0, observers - nblocks)),
    )

    def piece(k):
        parts = [
            lax.dynamic_index_in_dim(w, me_p ^ k, 1, False).reshape(n_obs * width, observers)
            for w in (load, thick)
        ]
        return along_panel(jnp.concatenate(parts + [delay_rows], axis=0), k)

    from_x, from_xc, from_c = piece(2), piece(3), piece(1)

    dest_rows = jnp.pad(
        les_dest.reshape(1, rows).astype(jnp.bfloat16), ((0, EXTRA - 1), (0, 2 * steps - rows))
    )
    message = jnp.concatenate([les_rows.reshape(rows, 2 * steps), dest_rows], axis=0)
    column = [message] + [along_obs(message, 2 * k) for k in range(1, n_obs // 2)]
    a = jnp.concatenate(column[: n_obs // 4], axis=0)
    b = jnp.concatenate(column[n_obs // 4 :], axis=0)
    ya, yb = along_obs(a, 1), along_obs(b, 1)

    sources = pl.pallas_call(
        functools.partial(slot_kernel, n_panel, n_obs, cap),
        out_shape=jax.ShapeDtypeStruct((count // 2, steps, 4 * width), jnp.bfloat16),
        in_specs=[vmem] * 4,
        out_specs=vmem,
        scratch_shapes=[pltpu.VMEM((count, width, 2 * steps), jnp.bfloat16)],
        compiler_params=params,
    )(a, b, ya, yb)
    acc = pltpu.VMEM((2 * steps, observers), jnp.float32)
    near = pl.pallas_call(
        functools.partial(near_kernel, n_obs),
        out_shape=jax.ShapeDtypeStruct((steps, observers), jnp.float32),
        in_specs=[vmem, vmem, vmem, smem, vmem],
        out_specs=vmem,
        scratch_shapes=[acc],
        compiler_params=params,
    )(sources, load, thick, delays, from_c)
    share = jax.ShapeDtypeStruct((steps // n_panel, observers), jnp.float32)
    shares = pl.pallas_call(
        functools.partial(far_kernel, n_panel, n_obs, width),
        out_shape=[share] * n_panel,
        in_specs=[vmem] * 4,
        out_specs=[vmem] * n_panel,
        scratch_shapes=[acc],
        compiler_params=params,
    )(sources, near, from_x, from_xc)
    total = shares[0]
    for k in (2, 3, 1):
        total = total + along_panel(shares[k], k)
    return total


def solution(mesh):
    placed = (
        P(("panel", "obs"), None, None),
        P(("panel", "obs"), None),
        P("panel", "obs"),
        P("panel", "obs"),
        P("panel", "obs"),
    )
    return jax.shard_map(
        per_device, mesh=mesh, in_specs=placed, out_specs=P("panel", "obs"), check_vma=False
    )
```

time: 120 us -> 28.9 us (0.24)
  waiting for transfers between devices: 56.5 us -> 11 us
  blocking collectives: 14.8 us -> 0 us
  between operations: 13.5 us -> 0.13 us
  starting transfers between devices: 0.04 us -> 11.6 us
  local copies, waits for them, and re-layouts: 12.4 us -> 2.92 us
  matrix products: 9.07 us -> 0 us
  loops' own time: 7.18 us -> 0 us
  other arithmetic: 5.91 us -> 0.69 us
  Pallas kernels: 0 us -> 2.33 us
    all_gather x1 -> x0, waiting for transfers between devices: 38.1 us -> none  [per_device(): group = lax.all_gather(local, 'obs', axis=0, tiled=True)]
    reduce_scatter x1 -> x0, waiting for transfers between devices: 18.3 us -> none  [per_device(): lax.psum_scatter(partial_sum, 'panel', scatter_dimension=0, tiled=True)]
    all_to_all x1 -> x0, blocking collectives: 14.8 us -> none  [per_device(): lax.all_to_all(buffer.reshape(count, cap, 2, steps), ('panel', 'obs'), sp...]
    ppermute x0 -> x11, starting transfers between devices: none -> 11.6 us  [the longest x5 7.77 us: along_obs(): return lax.ppermute(value, 'obs', [(i, i ^ k) for i in range(n_obs)])]
    ppermute x0 -> x11, waiting for transfers between devices: none -> 11 us  [the longest x5 8.22 us: along_obs(): return lax.ppermute(value, 'obs', [(i, i ^ k) for i in range(n_obs)])]
    scatter x1 -> x0, local copies, waits for them, and re-layouts: 9.74 us -> none  [per_device(): jnp.zeros((count * cap, 2, steps), les_rows.dtype).at[position]]
    dot_general x8 -> x0, matrix products: 9.07 us -> none  [the longest x4 4.54 us: one_block(): lax.dot_general(rate_b, thick_b, dims, preferred_element_type=jnp.float32)]
    another operation x1 -> x0, loops' own time: 7.18 us -> none  [per_device(): lax.scan(one_block, start, (press_blocks, rate_blocks, load_blocks, thick...]
  transfers between devices with their start and end apart: 2 -> 11, of which waited for: 2 -> 5; matrix products, arithmetic and copies ran while one was open for 0% -> 5% of each run, Pallas kernels for 0% -> 7%
where the time goes in v1:
time: 28.9 us; the launch traced here: 28.7 us
  starting transfers between devices  11.6 us (40%)
  waiting for transfers between devices  11 us (38%)
  local copies, waits for them, and re-layouts  2.92 us (10%)
  Pallas kernels  2.33 us (8%)
  other arithmetic  0.69 us (2%)
    ppermute x5, waiting for transfers between devices, along_obs(): return lax.ppermute(value, 'obs', [(i, i ^ k) for i in range(n_obs)])  8.22 us
    ppermute x5, starting transfers between devices, along_obs(): return lax.ppermute(value, 'obs', [(i, i ^ k) for i in range(n_obs)])  7.77 us
    ppermute x6, starting transfers between devices, along_panel(): return lax.ppermute(value, 'panel', [(i, i ^ k) for i in range(n_panel)])  3.87 us
    ppermute x6, waiting for transfers between devices, along_panel(): return lax.ppermute(value, 'panel', [(i, i ^ k) for i in range(n_panel)])  2.78 us
    unnamed x11, local copies, waits for them, and re-layouts  1.63 us
    dynamic_slice x1, local copies, waits for them, and re-layouts, piece(): lax.dynamic_index_in_dim(w, me_p ^ k, 1, False)  1.28 us
    pallas_call x1, Pallas kernels, per_device(): pl.pallas_call(functools.partial(slot_kernel, n_panel, n_obs, cap), out_s...  1.13 us
    pallas_call x1, Pallas kernels, per_device(): pl.pallas_call(functools.partial(near_kernel, n_obs), out_shape=jax.Shape...  0.89 us
  transfers between devices with their start and end apart: 11, of which 5 were waited for; matrix products, arithmetic and copies ran while one was open for 5% of the time, Pallas kernels for 7%

profile of v1, /device:TPU:0, one launch (start us, length us, event | category | flops | bytes accessed | tf_op | source)
XLA Modules:
  0.0 28.7 jit_solution(9069657089415978516)
XLA Ops:
  0.0 0.0 copy-start.3
  0.0 0.9 %copy.9 = bf16[16,8,2,128]{3,1,2,0:T(8,128)(2,1)S(1)} copy(bf16[16,8,2,128]{3,2,1,0:T(2,128)(2,1)} %bitcast.28) | data formatting | bytes 131072
  0.9 0.0 copy-done.3
  0.9 4.1 %collective-permute-start.1 = (bf16[144,256]{1,0:T(8,128)(2,1)S(1)}, bf16[144,256]{1,0:T(8,128)(2,1)S(1)}, u32[]{:S(2)}, u32[]{:S(2)}) collective-permute-start(bf16[144,256]{1,0:T(8,128)(2,1)S(1)} %pad_maximum_fusion.1), channel_id=1, source_target_pairs={{0,4},{1,5},{2,6},{3,7},{4,0},{5,1},{6,2},{7,3},{8,12},{9,13},{10,... | collective-permute-start | bytes 221192 | tf_op jit(solution)/shard_map/ppermute | solution.py:125
  5.0 1.3 %collective-permute-start.2 = (bf16[144,256]{1,0:T(8,128)(2,1)S(1)}, bf16[144,256]{1,0:T(8,128)(2,1)S(1)}, u32[]{:S(2)}, u32[]{:S(2)}) collective-permute-start(bf16[144,256]{1,0:T(8,128)(2,1)S(1)} %pad_maximum_fusion.1), channel_id=1, source_target_pairs={{0,6},{1,7},{2,4},{3,5},{4,2},{5,3},{6,0},{7,1},{8,14},{9,15},{10,... | collective-permute-start | bytes 221192 | tf_op jit(solution)/shard_map/ppermute | solution.py:125
  6.4 0.2 collective-permute-start
  6.6 0.0 copy-start.2
  6.6 0.7 %copy-done.2 = s32[4,1]{0,1:T(1,128)S(1)} copy-done((s32[4,1]{0,1:T(1,128)S(1)}, s32[4,1]{0,1:T(1,128)}, u32[]{:S(2)}) %copy-start.2) | copy-done | bytes 40
  7.3 1.3 %constant_dynamic-slice_fusion = (bf16[8,1,64,128]{3,2,1,0:T(8,128)(2,1)S(1)}, bf16[8,1,64,128]{3,2,1,0:T(8,128)(2,1)S(1)}, bf16[8,1,64,128]{3,2,1,0:T(8,128)(2,...) fusion(bf16[8,4,64,128]{3,2,1,0:T(8,128)(2,1)} %bitcast.18, ...), kind=kLoop, calls=%fused_computation.11 | loop fusion | bytes 1572876 | tf_op jit(solution)/shard_map/jit(dynamic_index_in_dim)/dynamic_slice | solution.py:136
  8.5 0.1 fusion.3
  8.6 0.1 collective-permute-start.5
  8.7 1.6 %collective-permute-start.6 = (bf16[1040,128]{1,0:T(8,128)(2,1)S(1)}, bf16[1040,128]{1,0:T(8,128)(2,1)S(1)}, u32[]{:S(2)}, u32[]{:S(2)}) collective-permute-start(bf16[1040,128]{1,0:T(8,128)(2,1)S(1)} %get-tuple-element.21), channel_id=1, source_target_pairs={{0,16},{8,24},{16,0},{24,8},{1,17},{9,25},{17,1},{25,9},{2,18},{10... | collective-permute-start | bytes 798728 | tf_op jit(solution)/shard_map/ppermute | solution.py:122
  10.2 0.0 collective-permute-done.1
  10.3 0.3 %collective-permute-start.7 = (bf16[1040,128]{1,0:T(8,128)(2,1)S(1)}, bf16[1040,128]{1,0:T(8,128)(2,1)S(1)}, u32[]{:S(2)}, u32[]{:S(2)}) collective-permute-start(bf16[1040,128]{1,0:T(8,128)(2,1)S(1)} %get-tuple-element.19), channel_id=1, source_target_pairs={{0,24},{8,16},{16,8},{24,0},{1,25},{9,17},{17,9},{25,1},{2,26},{10... | collective-permute-start | bytes 798728 | tf_op jit(solution)/shard_map/ppermute | solution.py:122
  10.6 0.9 %collective-permute-done.2 = bf16[144,256]{1,0:T(8,128)(2,1)S(1)} collective-permute-done((bf16[144,256]{1,0:T(8,128)(2,1)S(1)}, bf16[144,256]{1,0:T(8,128)(2,1)S(1)}, u32[]{:S(2)}, u32[]{:S(2)}) %collective-permute-start.2) | collective-permute-done | bytes 73760 | tf_op jit(solution)/shard_map/ppermute | solution.py:125
  11.5 1.5 %collective-permute-start.4 = (bf16[288,256]{1,0:T(8,128)(2,1)S(1)}, bf16[288,256]{1,0:T(8,128)(2,1)S(1)}, u32[]{:S(2)}, u32[]{:S(2)}) collective-permute-start(bf16[288,256]{1,0:T(8,128)(2,1)S(1)} %constant_dynamic-update-slice_fusion.b_ref), channel_id=1, source_target_pairs={{0,1},{1,0},{2,3},{3,2},{4,5},{5,4},{6,7},{7,6},{8,9},{9,8},{10,11... | collective-permute-start | bytes 442376 | tf_op jit(solution)/shard_map/ppermute | solution.py:125
  13.0 0.0 collective-permute-done
  13.0 0.6 %collective-permute-start.3 = (bf16[288,256]{1,0:T(8,128)(2,1)S(1)}, bf16[288,256]{1,0:T(8,128)(2,1)S(1)}, u32[]{:S(2)}, u32[]{:S(2)}) collective-permute-start(bf16[288,256]{1,0:T(8,128)(2,1)S(1)} %pad_maximum_fusion.a_ref), channel_id=1, source_target_pairs={{0,1},{1,0},{2,3},{3,2},{4,5},{5,4},{6,7},{7,6},{8,9},{9,8},{10,11... | collective-permute-start | bytes 442376 | tf_op jit(solution)/shard_map/ppermute | solution.py:125
  13.6 0.1 copy.6.delay_ref
  13.7 0.0 copy-start
  13.7 0.0 copy-start.1
  13.7 4.4 %collective-permute-done.4.yb_ref = bf16[288,256]{1,0:T(8,128)(2,1)S(1)} collective-permute-done((bf16[288,256]{1,0:T(8,128)(2,1)S(1)}, bf16[288,256]{1,0:T(8,128)(2,1)S(1)}, u32[]{:S(2)}, u32[]{:S(2)}) %collective-permute-start.4) | collective-permute-done | bytes 147488 | tf_op jit(solution)/shard_map/ppermute | solution.py:125
  18.1 2.9 %collective-permute-done.3.ya_ref = bf16[288,256]{1,0:T(8,128)(2,1)S(1)} collective-permute-done((bf16[288,256]{1,0:T(8,128)(2,1)S(1)}, bf16[288,256]{1,0:T(8,128)(2,1)S(1)}, u32[]{:S(2)}, u32[]{:S(2)}) %collective-permute-start.3) | collective-permute-done | bytes 147488 | tf_op jit(solution)/shard_map/ppermute | solution.py:125
  21.0 1.1 %shard_map.55.s_ref = bf16[16,128,256]{2,1,0:T(8,128)(2,1)S(1)} custom-call(bf16[288,256]{1,0:T(8,128)(2,1)S(1)} %pad_maximum_fusion.a_ref, bf16[288,256]{1,0:T(8,128)(2,1)S(1)} %constant_dynamic-update-slice_fusion.b_ref, bf16[288,256]{1,0:T(8,128)(2,1)S(1)} %collective-permute-done.3.ya_ref, bf16[288,256]{1,0:T(8,128)(2,1)S(1)} %collective-permute-done.4.yb_ref), custom_call_target="tpu_custom_call" | custom-call | tf_op jit(solution)/shard_map/pallas_call | solution.py:152
  22.1 0.0 collective-permute-done.5.c_ref
  22.1 0.0 copy-done
  22.1 0.0 copy-done.1
  22.2 0.9 %shard_map.56.near_ref = f32[128,128]{1,0:T(8,128)S(1)} custom-call(bf16[16,128,256]{2,1,0:T(8,128)(2,1)S(1)} %shard_map.55.s_ref, bf16[8,4,64,128]{3,2,1,0:T(8,128)(2,1)S(1)} %bitcast.17, bf16[8,4,64,128]{3,2,1,0:T(8,128)(2,1)S(1)} %bitcast.19, s32[4,1]{1,0:T(4,128)S(1)} %copy.6.delay_ref, bf16[1040,128]{1,0:T(8,128)(2,1)S(1)} %collective-permute-done.5.c_ref), custom_call_target="tpu_custom_call" | custom-call | tf_op jit(solution)/shard_map/pallas_call | solution.py:161
  23.0 0.0 collective-permute-done.6.x_ref
  23.1 0.0 collective-permute-done.7.xc_ref
  23.1 0.3 %shard_map.57 = (f32[32,128]{1,0:T(8,128)S(1)}, f32[32,128]{1,0:T(8,128)S(1)}, f32[32,128]{1,0:T(8,128)S(1)}, f32[32,128]{1,0:T(8,128)S(1)}) custom-call(bf16[16,128,256]{2,1,0:T(8,128)(2,1)S(1)} %shard_map.55.s_ref, f32[128,128]{1,0:T(8,128)S(1)} %shard_map.56.near_ref, bf16[1040,128]{1,0:T(8,128)(2,1)S(1)} %collective-permute-done.6.x_ref, ...), custom_call_target="tpu_custom_call" | custom-call | tf_op jit(solution)/shard_map/pallas_call | solution.py:170
  23.4 0.1 collective-permute-start.10
  23.5 1.4 %collective-permute-start.8 = (f32[32,128]{1,0:T(8,128)S(1)}, f32[32,128]{1,0:T(8,128)S(1)}, u32[]{:S(2)}, u32[]{:S(2)}) collective-permute-start(f32[32,128]{1,0:T(8,128)S(1)} %get-tuple-element.10), channel_id=1, source_target_pairs={{0,16},{8,24},{16,0},{24,8},{1,17},{9,25},{17,1},{25,9},{2,18},{10... | collective-permute-start | bytes 49160 | tf_op jit(solution)/shard_map/ppermute | solution.py:122
  24.9 0.4 %collective-permute-start.9 = (f32[32,128]{1,0:T(8,128)S(1)}, f32[32,128]{1,0:T(8,128)S(1)}, u32[]{:S(2)}, u32[]{:S(2)}) collective-permute-start(f32[32,128]{1,0:T(8,128)S(1)} %get-tuple-element.11), channel_id=1, source_target_pairs={{0,24},{8,16},{16,8},{24,0},{1,25},{9,17},{17,9},{25,1},{2,26},{10... | collective-permute-start | bytes 49160 | tf_op jit(solution)/shard_map/ppermute | solution.py:122
  25.3 0.0 collective-permute-done.10
  25.3 1.9 %collective-permute-done.8 = f32[32,128]{1,0:T(8,128)S(1)} collective-permute-done((f32[32,128]{1,0:T(8,128)S(1)}, f32[32,128]{1,0:T(8,128)S(1)}, u32[]{:S(2)}, u32[]{:S(2)}) %collective-permute-start.8) | collective-permute-done | bytes 16416 | tf_op jit(solution)/shard_map/ppermute | solution.py:122
  27.3 0.8 %collective-permute-done.9 = f32[32,128]{1,0:T(8,128)S(1)} collective-permute-done((f32[32,128]{1,0:T(8,128)S(1)}, f32[32,128]{1,0:T(8,128)S(1)}, u32[]{:S(2)}, u32[]{:S(2)}) %collective-permute-start.9) | collective-permute-done | bytes 16416 | tf_op jit(solution)/shard_map/ppermute | solution.py:122
  28.1 0.6 %add_add_fusion = f32[32,128]{1,0:T(8,128)} fusion(f32[32,128]{1,0:T(8,128)S(1)} %collective-permute-done.10, f32[32,128]{1,0:T(8,128)S(1)} %collective-permute-done.9, f32[32,128]{1,0:T(8,128)S(1)} %get-tuple-element.9, f32[32,128]{1,0:T(8,128)S(1)} %collective-permute-done.8), kind=kLoop, calls=%fused_computation.8 | loop fusion | flops 12288 | bytes 81920 | tf_op jit(solution)/shard_map/add | solution.py:180
  (7 shorter events, 0.0 us)
Async XLA Ops:
  0.0 0.9 %copy-start.3 = (s32[128,1]{0,1:T(1,128)S(1)}, s32[128,1]{0,1:T(1,128)}, u32[]{:S(2)}) copy-start(s32[128,1]{0,1:T(1,128)} %param.6) | copy-start | bytes 1540
  0.9 9.3 %collective-permute-start.1 = (bf16[144,256]{1,0:T(8,128)(2,1)S(1)}, bf16[144,256]{1,0:T(8,128)(2,1)S(1)}, u32[]{:S(2)}, u32[]{:S(2)}) collective-permute-start(bf16[144,256]{1,0:T(8,128)(2,1)S(1)} %pad_maximum_fusion.1), channel_id=1, source_target_pairs={{0,4},{1,5},{2,6},{3,7},{4,0},{5,1},{6,2},{7,3},{8,12},{9,13},{10,... | collective-permute-start | bytes 221192 | tf_op jit(solution)/shard_map/ppermute | solution.py:125
  5.0 6.5 %collective-permute-start.2 = (bf16[144,256]{1,0:T(8,128)(2,1)S(1)}, bf16[144,256]{1,0:T(8,128)(2,1)S(1)}, u32[]{:S(2)}, u32[]{:S(2)}) collective-permute-start(bf16[144,256]{1,0:T(8,128)(2,1)S(1)} %pad_maximum_fusion.1), channel_id=1, source_target_pairs={{0,6},{1,7},{2,4},{3,5},{4,2},{5,3},{6,0},{7,1},{8,14},{9,15},{10,... | collective-permute-start | bytes 221192 | tf_op jit(solution)/shard_map/ppermute | solution.py:125
  6.4 6.7 %collective-permute-start = (bf16[144,256]{1,0:T(8,128)(2,1)S(1)}, bf16[144,256]{1,0:T(8,128)(2,1)S(1)}, u32[]{:S(2)}, u32[]{:S(2)}) collective-permute-start(bf16[144,256]{1,0:T(8,128)(2,1)S(1)} %pad_maximum_fusion.1), channel_id=1, source_target_pairs={{0,2},{1,3},{2,0},{3,1},{4,6},{5,7},{6,4},{7,5},{8,10},{9,11},{10,... | collective-permute-start | bytes 221192 | tf_op jit(solution)/shard_map/ppermute | solution.py:125
  6.6 0.7 %copy-start.2 = (s32[4,1]{0,1:T(1,128)S(1)}, s32[4,1]{0,1:T(1,128)}, u32[]{:S(2)}) copy-start(s32[4,1]{0,1:T(1,128)} %param.9) | copy-start | bytes 52
  8.6 13.5 %collective-permute-start.5 = (bf16[1040,128]{1,0:T(8,128)(2,1)S(1)}, bf16[1040,128]{1,0:T(8,128)(2,1)S(1)}, u32[]{:S(2)}, u32[]{:S(2)}) collective-permute-start(bf16[1040,128]{1,0:T(8,128)(2,1)S(1)} %get-tuple-element.20), channel_id=1, source_target_pairs={{0,8},{8,0},{16,24},{24,16},{1,9},{9,1},{17,25},{25,17},{2,10},{10... | collective-permute-start | bytes 798728 | tf_op jit(solution)/shard_map/ppermute | solution.py:122
  8.7 14.4 %collective-permute-start.6 = (bf16[1040,128]{1,0:T(8,128)(2,1)S(1)}, bf16[1040,128]{1,0:T(8,128)(2,1)S(1)}, u32[]{:S(2)}, u32[]{:S(2)}) collective-permute-start(bf16[1040,128]{1,0:T(8,128)(2,1)S(1)} %get-tuple-element.21), channel_id=1, source_target_pairs={{0,16},{8,24},{16,0},{24,8},{1,17},{9,25},{17,1},{25,9},{2,18},{10... | collective-permute-start | bytes 798728 | tf_op jit(solution)/shard_map/ppermute | solution.py:122
  10.3 12.8 %collective-permute-start.7 = (bf16[1040,128]{1,0:T(8,128)(2,1)S(1)}, bf16[1040,128]{1,0:T(8,128)(2,1)S(1)}, u32[]{:S(2)}, u32[]{:S(2)}) collective-permute-start(bf16[1040,128]{1,0:T(8,128)(2,1)S(1)} %get-tuple-element.19), channel_id=1, source_target_pairs={{0,24},{8,16},{16,8},{24,0},{1,25},{9,17},{17,9},{25,1},{2,26},{10... | collective-permute-start | bytes 798728 | tf_op jit(solution)/shard_map/ppermute | solution.py:122
  11.5 6.6 %collective-permute-start.4 = (bf16[288,256]{1,0:T(8,128)(2,1)S(1)}, bf16[288,256]{1,0:T(8,128)(2,1)S(1)}, u32[]{:S(2)}, u32[]{:S(2)}) collective-permute-start(bf16[288,256]{1,0:T(8,128)(2,1)S(1)} %constant_dynamic-update-slice_fusion.b_ref), channel_id=1, source_target_pairs={{0,1},{1,0},{2,3},{3,2},{4,5},{5,4},{6,7},{7,6},{8,9},{9,8},{10,11... | collective-permute-start | bytes 442376 | tf_op jit(solution)/shard_map/ppermute | solution.py:125
  13.0 7.9 %collective-permute-start.3 = (bf16[288,256]{1,0:T(8,128)(2,1)S(1)}, bf16[288,256]{1,0:T(8,128)(2,1)S(1)}, u32[]{:S(2)}, u32[]{:S(2)}) collective-permute-start(bf16[288,256]{1,0:T(8,128)(2,1)S(1)} %pad_maximum_fusion.a_ref), channel_id=1, source_target_pairs={{0,1},{1,0},{2,3},{3,2},{4,5},{5,4},{6,7},{7,6},{8,9},{9,8},{10,11... | collective-permute-start | bytes 442376 | tf_op jit(solution)/shard_map/ppermute | solution.py:125
  13.7 8.4 %copy-start = (bf16[2048,128]{1,0:T(8,128)(2,1)S(1)}, bf16[2048,128]{1,0:T(8,128)(2,1)}, u32[]{:S(2)}) copy-start(bf16[2048,128]{1,0:T(8,128)(2,1)} %param.7) | copy-start | bytes 1572868
  13.7 8.4 %copy-start.1 = (bf16[2048,128]{1,0:T(8,128)(2,1)S(1)}, bf16[2048,128]{1,0:T(8,128)(2,1)}, u32[]{:S(2)}) copy-start(bf16[2048,128]{1,0:T(8,128)(2,1)} %param.8) | copy-start | bytes 1572868
  23.4 1.9 %collective-permute-start.10 = (f32[32,128]{1,0:T(8,128)S(1)}, f32[32,128]{1,0:T(8,128)S(1)}, u32[]{:S(2)}, u32[]{:S(2)}) collective-permute-start(f32[32,128]{1,0:T(8,128)S(1)} %get-tuple-element.12), channel_id=1, source_target_pairs={{0,8},{8,0},{16,24},{24,16},{1,9},{9,1},{17,25},{25,17},{2,10},{10... | collective-permute-start | bytes 49160 | tf_op jit(solution)/shard_map/ppermute | solution.py:122
  23.5 3.8 %collective-permute-start.8 = (f32[32,128]{1,0:T(8,128)S(1)}, f32[32,128]{1,0:T(8,128)S(1)}, u32[]{:S(2)}, u32[]{:S(2)}) collective-permute-start(f32[32,128]{1,0:T(8,128)S(1)} %get-tuple-element.10), channel_id=1, source_target_pairs={{0,16},{8,24},{16,0},{24,8},{1,17},{9,25},{17,1},{25,9},{2,18},{10... | collective-permute-start | bytes 49160 | tf_op jit(solution)/shard_map/ppermute | solution.py:122
  24.9 3.2 %collective-permute-start.9 = (f32[32,128]{1,0:T(8,128)S(1)}, f32[32,128]{1,0:T(8,128)S(1)}, u32[]{:S(2)}, u32[]{:S(2)}) collective-permute-start(f32[32,128]{1,0:T(8,128)S(1)} %get-tuple-element.11), channel_id=1, source_target_pairs={{0,24},{8,16},{16,8},{24,0},{1,25},{9,17},{17,9},{25,1},{2,26},{10... | collective-permute-start | bytes 49160 | tf_op jit(solution)/shard_map/ppermute | solution.py:122

commit v2 on v1

v2 whole, which is shorter than its diff:
```python
import functools

import jax
import jax.numpy as jnp
from jax import lax
from jax.experimental import pallas as pl
from jax.experimental.pallas import tpu as pltpu
from jax.sharding import PartitionSpec as P

PBLK = 512
PACK_ORDER = (2, 3, 1, 0)
EXTRA = 16
VMEM_LIMIT = 48 * 1024 * 1024


def dot(a, b):
    return lax.dot_general(a, b, (((1,), (0,)), ((), ())), preferred_element_type=jnp.float32)


def pack_kernel(n_panel, n_obs, cap, rows_ref, dest_ref, delay_ref, load_ref, thick_ref, *refs):
    message_ref, pieces = refs[0], refs[1 : 1 + n_panel]
    rows_in, dest_in, delay_in, sems, few = refs[1 + n_panel :]
    count = n_panel * n_obs
    me_p = lax.axis_index("panel")
    width = n_obs * cap
    depth = n_obs * width
    small = [
        pltpu.make_async_copy(src, dst, few.at[i])
        for i, (src, dst) in enumerate(((rows_ref, rows_in), (dest_ref, dest_in), (delay_ref, delay_in)))
    ]
    for copy in small:
        copy.start()
    copies = []
    for k in PACK_ORDER:
        for i, ref in enumerate((load_ref, thick_ref)):
            there = pieces[k].at[pl.ds(i * depth, depth)].reshape(n_obs, width, ref.shape[3])
            copies.append(pltpu.make_async_copy(ref.at[:, me_p ^ k], there, sems.at[k, i]))
            copies[-1].start()
    rows, steps = rows_ref.shape[0] // 2, rows_ref.shape[1]
    nblocks = delay_ref.shape[1]
    for copy in small:
        copy.wait()
    lane = lax.broadcasted_iota(jnp.int32, (EXTRA, load_ref.shape[3]), 1)
    late = jnp.zeros(lane.shape, jnp.int32)
    for b in range(nblocks):
        late = jnp.where(lane == b, delay_in[0, b], late)
    for k in range(n_panel):
        pieces[k][2 * depth : 2 * depth + EXTRA, :] = late.astype(jnp.float32).astype(jnp.bfloat16)
    r0 = lax.broadcasted_iota(jnp.int32, (rows, 2 * rows), 0)
    r1 = lax.broadcasted_iota(jnp.int32, (rows, 2 * rows), 1)
    value = rows_in[...]
    pressure = dot((r1 == 2 * r0).astype(jnp.bfloat16), value).astype(jnp.bfloat16)
    velocity = dot((r1 == 2 * r0 + 1).astype(jnp.bfloat16), value).astype(jnp.bfloat16)
    t0 = lax.broadcasted_iota(jnp.int32, (steps, steps), 0)
    t1 = lax.broadcasted_iota(jnp.int32, (steps, steps), 1)
    slope = jnp.where(t0 == t1 + 1, 0.5, jnp.where(t0 == t1 - 1, -0.5, 0.0)).astype(jnp.bfloat16)
    message_ref[0:rows, 0:steps] = pressure
    message_ref[0:rows, steps:] = dot(velocity, slope).astype(jnp.bfloat16)
    dest = dest_in[...]
    onehot = lax.broadcasted_iota(jnp.int32, (count, rows), 0) == dest
    q0 = lax.broadcasted_iota(jnp.int32, (rows, rows), 0)
    q1 = lax.broadcasted_iota(jnp.int32, (rows, rows), 1)
    before = dot(onehot.astype(jnp.bfloat16), (q0 < q1).astype(jnp.bfloat16))
    rank = jnp.sum(jnp.where(onehot, before, 0.0), axis=0, keepdims=True)
    tail = jnp.zeros((EXTRA, steps), jnp.float32)
    message_ref[rows:, 0:steps] = (tail + dest.astype(jnp.float32)).astype(jnp.bfloat16)
    message_ref[rows:, steps:] = (tail + rank).astype(jnp.bfloat16)
    for copy in copies:
        copy.wait()


def slot_kernel(n_panel, n_obs, cap, a_ref, b_ref, ya_ref, yb_ref, gate_ref, out_ref, slots_ref):
    count = n_panel * n_obs
    me_p = lax.axis_index("panel")
    me_o = lax.axis_index("obs")
    rows = a_ref.shape[0] // (n_obs // 4) - EXTRA
    steps = a_ref.shape[1] // 2
    per = 16 // cap
    slot_ids = lax.broadcasted_iota(jnp.int32, (count * 16, per * rows), 0)
    for quad in range(n_obs // per):
        values, places = [], []
        for i in range(per):
            j = quad * per + i
            ref = (a_ref, ya_ref, b_ref, yb_ref)[j % 4]
            base = (j // 4) * (rows + EXTRA)
            tail = ref[base + rows : base + rows + EXTRA, :].astype(jnp.float32)[0:1].astype(jnp.int32)
            dest, rank = tail[:, 0:rows], tail[:, steps : steps + rows]
            within = ((me_o % per) ^ i) * cap + rank
            places.append((dest ^ (me_p * n_obs)) * 16 + within)
            values.append(ref[base : base + rows, :])
        value = jnp.concatenate(values, axis=0)
        place = jnp.concatenate(places, axis=1)
        pick = (slot_ids == place).astype(jnp.bfloat16)
        got = dot(pick, value).astype(jnp.bfloat16)
        start = pl.multiple_of(((me_o // per) ^ quad) * 16, 16)
        slots_ref[:, pl.ds(start, 16), :] = got.reshape(count, 16, 2 * steps)
    for k in range(out_ref.shape[0]):
        block = slots_ref[2 * k : 2 * k + 2].reshape(2 * n_obs * cap, 2 * steps)
        out_ref[k, :, 0 : 2 * n_obs * cap] = block[:, 0:steps].T
        out_ref[k, :, 2 * n_obs * cap :] = block[:, steps:].T


def add_term(acc_ref, source, weights, delay):
    steps = source.shape[0]
    acc_ref[pl.ds(delay, steps), :] += dot(source, weights)


def late_kernel(depth, x_ref, xc_ref, out_ref):
    for i, ref in enumerate((x_ref, xc_ref)):
        out_ref[8 * i : 8 * i + 8] = ref[depth : depth + EXTRA, :].astype(jnp.float32)[0:8].astype(jnp.int32)


def near_kernel(n_obs, width, s_ref, own_ref, c_ref, out_ref, acc_ref):
    steps = out_ref.shape[0]
    nblocks = n_obs // 2
    acc_ref[...] = jnp.zeros_like(acc_ref)
    piece_terms(nblocks, width, s_ref, 0, own_ref, acc_ref)
    piece_terms(nblocks, width, s_ref, nblocks, c_ref, acc_ref)
    out_ref[...] = acc_ref[0:steps]


def piece_terms(nblocks, width, s_ref, first, w_ref, acc_ref):
    depth = 2 * width * nblocks
    delays = w_ref[2 * depth : 2 * depth + EXTRA, :].astype(jnp.float32)[0:1].astype(jnp.int32)
    for b in range(nblocks):
        lo, hi = 2 * width * b, 2 * width * (b + 1)
        weights = jnp.concatenate([w_ref[lo:hi], w_ref[depth + lo : depth + hi]], axis=0)
        add_term(acc_ref, s_ref[first + b], weights, delays[0, b])


def far_kernel(n_panel, n_obs, width, s_ref, near_ref, x_ref, xc_ref, *refs):
    outs, acc_ref = refs[:n_panel], refs[n_panel]
    me_p = lax.axis_index("panel")
    steps = near_ref.shape[0]
    nblocks = n_obs // 2
    acc_ref[0:steps] = near_ref[...]
    acc_ref[steps:] = jnp.zeros_like(acc_ref[steps:])
    piece_terms(nblocks, width, s_ref, 2 * nblocks, x_ref, acc_ref)
    piece_terms(nblocks, width, s_ref, 3 * nblocks, xc_ref, acc_ref)
    share = steps // n_panel
    for k in range(n_panel):
        start = pl.multiple_of((me_p ^ k) * share, share)
        outs[k][...] = acc_ref[pl.ds(start, share), :]


def per_device(les_rows, les_dest, loading_weight, thickness_weight, delays):
    n_panel = lax.axis_size("panel")
    n_obs = lax.axis_size("obs")
    count = n_panel * n_obs
    rows, _, steps = les_rows.shape
    cap = 2 * rows // count
    observers = loading_weight.shape[1]
    width = n_obs * cap
    nblocks = n_obs // 2
    params = pltpu.CompilerParams(vmem_limit_bytes=VMEM_LIMIT)
    vmem = pl.BlockSpec(memory_space=pltpu.VMEM)
    hbm = pl.BlockSpec(memory_space=pltpu.HBM)

    def along_panel(value, k):
        return lax.ppermute(value, "panel", [(i, i ^ k) for i in range(n_panel)])

    def along_obs(value, k):
        return lax.ppermute(value, "obs", [(i, i ^ k) for i in range(n_obs)])

    load = loading_weight.reshape(n_obs, n_panel, width, observers)
    thick = thickness_weight.reshape(n_obs, n_panel, width, observers)
    piece = jax.ShapeDtypeStruct((2 * n_obs * width + EXTRA, observers), jnp.bfloat16)
    message, own, to_c, to_x, to_xc = pl.pallas_call(
        functools.partial(pack_kernel, n_panel, n_obs, cap),
        out_shape=[jax.ShapeDtypeStruct((rows + EXTRA, 2 * steps), jnp.bfloat16)] + [piece] * n_panel,
        in_specs=[hbm] * 5,
        out_specs=[vmem] * (1 + n_panel),
        scratch_shapes=[
            pltpu.VMEM((2 * rows, steps), jnp.bfloat16),
            pltpu.VMEM((1, rows), jnp.int32),
            pltpu.SMEM((1, nblocks), jnp.int32),
            pltpu.SemaphoreType.DMA((n_panel, 2)),
            pltpu.SemaphoreType.DMA((3,)),
        ],
        compiler_params=params,
    )(
        *(
            pltpu.with_memory_space_constraint(value, pltpu.HBM)
            for value in (
                les_rows.reshape(2 * rows, steps),
                les_dest.reshape(1, rows),
                delays.reshape(1, nblocks),
                load,
                thick,
            )
        )
    )
    from_x, from_xc, from_c = along_panel(to_x, 2), along_panel(to_xc, 3), along_panel(to_c, 1)
    a = jnp.concatenate([message] + [along_obs(message, k) for k in range(4, n_obs, 4)], axis=0)
    a, from_c = lax.optimization_barrier((a, from_c))
    b, ya, yb = along_obs(a, 2), along_obs(a, 1), along_obs(a, 3)

    late = pl.pallas_call(
        functools.partial(late_kernel, 2 * n_obs * width),
        out_shape=jax.ShapeDtypeStruct((16, observers), jnp.int32),
        in_specs=[vmem] * 2,
        out_specs=vmem,
        compiler_params=params,
        cost_estimate=pl.CostEstimate(flops=10**0, bytes_accessed=0, transcendentals=0),
    )(from_x, from_xc)

    sources = pl.pallas_call(
        functools.partial(slot_kernel, n_panel, n_obs, cap),
        out_shape=jax.ShapeDtypeStruct((count // 2, steps, 4 * width), jnp.bfloat16),
        in_specs=[vmem] * 5,
        out_specs=vmem,
        scratch_shapes=[pltpu.VMEM((count, width, 2 * steps), jnp.bfloat16)],
        compiler_params=params,
    )(a, b, ya, yb, late)
    acc = pltpu.VMEM((2 * steps, observers), jnp.float32)
    near = pl.pallas_call(
        functools.partial(near_kernel, n_obs, width),
        out_shape=jax.ShapeDtypeStruct((steps, observers), jnp.float32),
        in_specs=[vmem] * 3,
        out_specs=vmem,
        scratch_shapes=[acc],
        compiler_params=params,
    )(sources, own, from_c)
    share = jax.ShapeDtypeStruct((steps // n_panel, observers), jnp.float32)
    shares = pl.pallas_call(
        functools.partial(far_kernel, n_panel, n_obs, width),
        out_shape=[share] * n_panel,
        in_specs=[vmem] * 4,
        out_specs=[vmem] * n_panel,
        scratch_shapes=[acc],
        compiler_params=params,
    )(sources, near, from_x, from_xc)
    total = shares[0]
    for k in (2, 3, 1):
        total = total + along_panel(shares[k], k)
    return total


def solution(mesh):
    placed = (
        P(("panel", "obs"), None, None),
        P(("panel", "obs"), None),
        P("panel", "obs"),
        P("panel", "obs"),
        P("panel", "obs"),
    )
    return jax.shard_map(
        per_device, mesh=mesh, in_specs=placed, out_specs=P("panel", "obs"), check_vma=False
    )
```

time: 28.9 us -> 26.8 us (0.927)
  local copies, waits for them, and re-layouts: 2.92 us -> 0 us
  waiting for transfers between devices: 11 us -> 11.7 us
  Pallas kernels: 2.33 us -> 2.86 us
    ppermute x6, waiting for transfers between devices: 2.78 us -> 7.99 us  [along_panel(): return lax.ppermute(value, 'panel', [(i, i ^ k) for i in range(n_panel)])]
    ppermute x5 -> x4, waiting for transfers between devices: 8.22 us -> 3.71 us  [along_obs(): return lax.ppermute(value, 'obs', [(i, i ^ k) for i in range(n_obs)])]
    unnamed x11 -> x0, local copies, waits for them, and re-layouts: 1.63 us -> none
    dynamic_slice x1 -> x0, local copies, waits for them, and re-layouts: 1.28 us -> none  [piece(): lax.dynamic_index_in_dim(w, me_p ^ k, 1, False)]
    pallas_call x1 -> x3, Pallas kernels: 0.89 us -> 1.74 us  [the longest x1 1.43 us: per_device(): pl.pallas_call(functools.partial(pack_kernel, n_panel, n_obs, cap), out_s...]
    ppermute x5 -> x4, starting transfers between devices: 7.77 us -> 7.22 us  [along_obs(): return lax.ppermute(value, 'obs', [(i, i ^ k) for i in range(n_obs)])]
    ppermute x6, starting transfers between devices: 3.87 us -> 4.26 us  [along_panel(): return lax.ppermute(value, 'panel', [(i, i ^ k) for i in range(n_panel)])]
    pallas_call x1, Pallas kernels: 1.13 us -> 0.81 us  [per_device(): pl.pallas_call(functools.partial(slot_kernel, n_panel, n_obs, cap), out_s...]
  transfers between devices with their start and end apart: 11 -> 10, of which waited for: 5 -> 6; matrix products, arithmetic and copies ran while one was open for 5% -> 0% of each run, Pallas kernels for 7% -> 0%
where the time goes in v2:
time: 26.8 us; the launch traced here: 26.7 us
  waiting for transfers between devices  11.7 us (44%)
  starting transfers between devices  11.5 us (43%)
  Pallas kernels  2.86 us (11%)
  other arithmetic  0.62 us (2%)
    ppermute x6, waiting for transfers between devices, along_panel(): return lax.ppermute(value, 'panel', [(i, i ^ k) for i in range(n_panel)])  7.99 us
    ppermute x4, starting transfers between devices, along_obs(): return lax.ppermute(value, 'obs', [(i, i ^ k) for i in range(n_obs)])  7.22 us
    ppermute x6, starting transfers between devices, along_panel(): return lax.ppermute(value, 'panel', [(i, i ^ k) for i in range(n_panel)])  4.26 us
    ppermute x4, waiting for transfers between devices, along_obs(): return lax.ppermute(value, 'obs', [(i, i ^ k) for i in range(n_obs)])  3.71 us
    pallas_call x1, Pallas kernels, per_device(): pl.pallas_call(functools.partial(pack_kernel, n_panel, n_obs, cap), out_s...  1.43 us
    pallas_call x1, Pallas kernels, per_device(): pl.pallas_call(functools.partial(slot_kernel, n_panel, n_obs, cap), out_s...  0.81 us
    add x1, other arithmetic, per_device(): total = total + along_panel(shares[k], k)  0.61 us
  transfers between devices with their start and end apart: 10, of which 6 were waited for; matrix products, arithmetic and copies ran while one was open for 0% of the time, Pallas kernels for 0%

profile of v2, /device:TPU:0, one launch (start us, length us, event | category | flops | bytes accessed | tf_op | source)
XLA Modules:
  0.0 26.7 jit_solution(4498718795650623257)
XLA Ops:
  0.0 1.4 %shard_map.55 = (bf16[144,256]{1,0:T(8,128)(2,1)S(1)}, bf16[1040,128]{1,0:T(8,128)(2,1)S(1)}, bf16[1040,128]{1,0:T(8,128)(2,1)S(1)}, bf16[1040,128]{1,0:T(8,128)(2,1)S(1)}, bf16[1040,128]{1,0:T(8,128)(2,1)S(1)}) custom-call(bf16[256,128]{1,0:T(8,128)(2,1)} %bitcast.7, s32[1,128]{1,0:T(1,128)} %bitcast.8, s32[1,4]{1,0:T(1,128)} %bitcast.9, ...), custom_call_target="tpu_custom_call" | custom-call | tf_op jit(solution)/shard_map/pallas_call | solution.py:168
  1.4 0.5 %collective-permute-start.1 = (bf16[1040,128]{1,0:T(8,128)(2,1)S(1)}, bf16[1040,128]{1,0:T(8,128)(2,1)S(1)}, u32[]{:S(2)}, u32[]{:S(2)}) collective-permute-start(bf16[1040,128]{1,0:T(8,128)(2,1)S(1)} %get-tuple-element.17), channel_id=1, source_target_pairs={{0,8},{8,0},{16,24},{24,16},{1,9},{9,1},{17,25},{25,17},{2,10},{10... | collective-permute-start | bytes 798728 | tf_op jit(solution)/shard_map/ppermute | solution.py:160
  2.0 3.7 %collective-permute-start = (bf16[144,256]{1,0:T(8,128)(2,1)S(1)}, bf16[144,256]{1,0:T(8,128)(2,1)S(1)}, u32[]{:S(2)}, u32[]{:S(2)}) collective-permute-start(bf16[144,256]{1,0:T(8,128)(2,1)S(1)} %get-tuple-element.16), channel_id=1, source_target_pairs={{0,4},{1,5},{2,6},{3,7},{4,0},{5,1},{6,2},{7,3},{8,12},{9,13},{10,... | collective-permute-start | bytes 221192 | tf_op jit(solution)/shard_map/ppermute | solution.py:163
  5.6 1.5 %collective-permute-start.5 = (bf16[1040,128]{1,0:T(8,128)(2,1)S(1)}, bf16[1040,128]{1,0:T(8,128)(2,1)S(1)}, u32[]{:S(2)}, u32[]{:S(2)}) collective-permute-start(bf16[1040,128]{1,0:T(8,128)(2,1)S(1)} %get-tuple-element.19), channel_id=1, source_target_pairs={{0,16},{8,24},{16,0},{24,8},{1,17},{9,25},{17,1},{25,9},{2,18},{10... | collective-permute-start | bytes 798728 | tf_op jit(solution)/shard_map/ppermute | solution.py:160
  7.1 0.0 collective-permute-start.6
  7.1 2.9 %collective-permute-done = bf16[144,256]{1,0:T(8,128)(2,1)S(1)} collective-permute-done((bf16[144,256]{1,0:T(8,128)(2,1)S(1)}, bf16[144,256]{1,0:T(8,128)(2,1)S(1)}, u32[]{:S(2)}, u32[]{:S(2)}) %collective-permute-start) | collective-permute-done | bytes 73760 | tf_op jit(solution)/shard_map/ppermute | solution.py:163
  10.1 0.0 collective-permute-done.1.c_ref
  10.1 1.8 %collective-permute-start.4 = (bf16[288,256]{1,0:T(8,128)(2,1)S(1)}, bf16[288,256]{1,0:T(8,128)(2,1)S(1)}, u32[]{:S(2)}, u32[]{:S(2)}) collective-permute-start(bf16[288,256]{1,0:T(8,128)(2,1)S(1)} %pad_maximum_fusion.a_ref), channel_id=1, source_target_pairs={{0,3},{1,2},{2,1},{3,0},{4,7},{5,6},{6,5},{7,4},{8,11},{9,10},{10,... | collective-permute-start | bytes 442376 | tf_op jit(solution)/shard_map/ppermute | solution.py:163
  11.9 0.5 %collective-permute-start.3 = (bf16[288,256]{1,0:T(8,128)(2,1)S(1)}, bf16[288,256]{1,0:T(8,128)(2,1)S(1)}, u32[]{:S(2)}, u32[]{:S(2)}) collective-permute-start(bf16[288,256]{1,0:T(8,128)(2,1)S(1)} %pad_maximum_fusion.a_ref), channel_id=1, source_target_pairs={{0,1},{1,0},{2,3},{3,2},{4,5},{5,4},{6,7},{7,6},{8,9},{9,8},{10,11... | collective-permute-start | bytes 442376 | tf_op jit(solution)/shard_map/ppermute | solution.py:163
  12.4 1.3 %collective-permute-start.2 = (bf16[288,256]{1,0:T(8,128)(2,1)S(1)}, bf16[288,256]{1,0:T(8,128)(2,1)S(1)}, u32[]{:S(2)}, u32[]{:S(2)}) collective-permute-start(bf16[288,256]{1,0:T(8,128)(2,1)S(1)} %pad_maximum_fusion.a_ref), channel_id=1, source_target_pairs={{0,2},{1,3},{2,0},{3,1},{4,6},{5,7},{6,4},{7,5},{8,10},{9,11},{10,... | collective-permute-start | bytes 442376 | tf_op jit(solution)/shard_map/ppermute | solution.py:163
  13.6 1.2 %collective-permute-done.5.x_ref = bf16[1040,128]{1,0:T(8,128)(2,1)S(1)} collective-permute-done((bf16[1040,128]{1,0:T(8,128)(2,1)S(1)}, bf16[1040,128]{1,0:T(8,128)(2,1)S(1)}, u32[]{:S(2)}, u32[]{:S(2)}) %collective-permute-start.5) | collective-permute-done | bytes 266272 | tf_op jit(solution)/shard_map/ppermute | solution.py:160
  14.9 4.2 %collective-permute-done.6.xc_ref = bf16[1040,128]{1,0:T(8,128)(2,1)S(1)} collective-permute-done((bf16[1040,128]{1,0:T(8,128)(2,1)S(1)}, bf16[1040,128]{1,0:T(8,128)(2,1)S(1)}, u32[]{:S(2)}, u32[]{:S(2)}) %collective-permute-start.6) | collective-permute-done | bytes 266272 | tf_op jit(solution)/shard_map/ppermute | solution.py:160
  19.0 0.0 collective-permute-done.4.yb_ref
  19.0 0.8 %collective-permute-done.3.ya_ref = bf16[288,256]{1,0:T(8,128)(2,1)S(1)} collective-permute-done((bf16[288,256]{1,0:T(8,128)(2,1)S(1)}, bf16[288,256]{1,0:T(8,128)(2,1)S(1)}, u32[]{:S(2)}, u32[]{:S(2)}) %collective-permute-start.3) | collective-permute-done | bytes 147488 | tf_op jit(solution)/shard_map/ppermute | solution.py:163
  19.8 0.0 collective-permute-done.2.b_ref
  19.8 0.8 %shard_map.57.s_ref = bf16[16,128,256]{2,1,0:T(8,128)(2,1)S(1)} custom-call(bf16[288,256]{1,0:T(8,128)(2,1)S(1)} %pad_maximum_fusion.a_ref, bf16[288,256]{1,0:T(8,128)(2,1)S(1)} %collective-permute-done.2.b_ref, bf16[288,256]{1,0:T(8,128)(2,1)S(1)} %collective-permute-done.3.ya_ref, bf16[288,256]{1,0:T(8,128)(2,1)S(1)} %collective-permute-done.4.yb_ref, ...), custom_call_target="tpu_custom_call" | custom-call | tf_op jit(solution)/shard_map/pallas_call | solution.py:207
  20.6 0.3 %shard_map.58.near_ref = f32[128,128]{1,0:T(8,128)S(1)} custom-call(bf16[16,128,256]{2,1,0:T(8,128)(2,1)S(1)} %shard_map.57.s_ref, bf16[1040,128]{1,0:T(8,128)(2,1)S(1)} %get-tuple-element.21.own_ref, bf16[1040,128]{1,0:T(8,128)(2,1)S(1)} %collective-permute-done.1.c_ref), custom_call_target="tpu_custom_call" | custom-call | tf_op jit(solution)/shard_map/pallas_call | solution.py:216
  20.9 0.3 %shard_map.59 = (f32[32,128]{1,0:T(8,128)S(1)}, f32[32,128]{1,0:T(8,128)S(1)}, f32[32,128]{1,0:T(8,128)S(1)}, f32[32,128]{1,0:T(8,128)S(1)}) custom-call(bf16[16,128,256]{2,1,0:T(8,128)(2,1)S(1)} %shard_map.57.s_ref, f32[128,128]{1,0:T(8,128)S(1)} %shard_map.58.near_ref, bf16[1040,128]{1,0:T(8,128)(2,1)S(1)} %collective-permute-done.5.x_ref, ...), custom_call_target="tpu_custom_call" | custom-call | tf_op jit(solution)/shard_map/pallas_call | solution.py:225
  21.3 1.5 %collective-permute-start.7 = (f32[32,128]{1,0:T(8,128)S(1)}, f32[32,128]{1,0:T(8,128)S(1)}, u32[]{:S(2)}, u32[]{:S(2)}) collective-permute-start(f32[32,128]{1,0:T(8,128)S(1)} %get-tuple-element.24), channel_id=1, source_target_pairs={{0,16},{8,24},{16,0},{24,8},{1,17},{9,25},{17,1},{25,9},{2,18},{10... | collective-permute-start | bytes 49160 | tf_op jit(solution)/shard_map/ppermute | solution.py:160
  22.8 0.0 collective-permute-start.8
  22.8 0.6 %collective-permute-start.9 = (f32[32,128]{1,0:T(8,128)S(1)}, f32[32,128]{1,0:T(8,128)S(1)}, u32[]{:S(2)}, u32[]{:S(2)}) collective-permute-start(f32[32,128]{1,0:T(8,128)S(1)} %get-tuple-element.26), channel_id=1, source_target_pairs={{0,8},{8,0},{16,24},{24,16},{1,9},{9,1},{17,25},{25,17},{2,10},{10... | collective-permute-start | bytes 49160 | tf_op jit(solution)/shard_map/ppermute | solution.py:160
  23.5 1.6 %collective-permute-done.7 = f32[32,128]{1,0:T(8,128)S(1)} collective-permute-done((f32[32,128]{1,0:T(8,128)S(1)}, f32[32,128]{1,0:T(8,128)S(1)}, u32[]{:S(2)}, u32[]{:S(2)}) %collective-permute-start.7) | collective-permute-done | bytes 16416 | tf_op jit(solution)/shard_map/ppermute | solution.py:160
  25.1 1.0 %collective-permute-done.8 = f32[32,128]{1,0:T(8,128)S(1)} collective-permute-done((f32[32,128]{1,0:T(8,128)S(1)}, f32[32,128]{1,0:T(8,128)S(1)}, u32[]{:S(2)}, u32[]{:S(2)}) %collective-permute-start.8) | collective-permute-done | bytes 16416 | tf_op jit(solution)/shard_map/ppermute | solution.py:160
  26.1 0.0 collective-permute-done.9
  26.1 0.6 %add_add_fusion = f32[32,128]{1,0:T(8,128)} fusion(f32[32,128]{1,0:T(8,128)S(1)} %collective-permute-done.9, f32[32,128]{1,0:T(8,128)S(1)} %collective-permute-done.8, f32[32,128]{1,0:T(8,128)S(1)} %get-tuple-element.23, f32[32,128]{1,0:T(8,128)S(1)} %collective-permute-done.7), kind=kLoop, calls=%fused_computation.1 | loop fusion | flops 12288 | bytes 81920 | tf_op jit(solution)/shard_map/add | solution.py:235
  (2 shorter events, 0.0 us)
Async XLA Ops:
  1.4 8.6 %collective-permute-start.1 = (bf16[1040,128]{1,0:T(8,128)(2,1)S(1)}, bf16[1040,128]{1,0:T(8,128)(2,1)S(1)}, u32[]{:S(2)}, u32[]{:S(2)}) collective-permute-start(bf16[1040,128]{1,0:T(8,128)(2,1)S(1)} %get-tuple-element.17), channel_id=1, source_target_pairs={{0,8},{8,0},{16,24},{24,16},{1,9},{9,1},{17,25},{25,17},{2,10},{10... | collective-permute-start | bytes 798728 | tf_op jit(solution)/shard_map/ppermute | solution.py:160
  2.0 8.1 %collective-permute-start = (bf16[144,256]{1,0:T(8,128)(2,1)S(1)}, bf16[144,256]{1,0:T(8,128)(2,1)S(1)}, u32[]{:S(2)}, u32[]{:S(2)}) collective-permute-start(bf16[144,256]{1,0:T(8,128)(2,1)S(1)} %get-tuple-element.16), channel_id=1, source_target_pairs={{0,4},{1,5},{2,6},{3,7},{4,0},{5,1},{6,2},{7,3},{8,12},{9,13},{10,... | collective-permute-start | bytes 221192 | tf_op jit(solution)/shard_map/ppermute | solution.py:163
  5.6 9.2 %collective-permute-start.5 = (bf16[1040,128]{1,0:T(8,128)(2,1)S(1)}, bf16[1040,128]{1,0:T(8,128)(2,1)S(1)}, u32[]{:S(2)}, u32[]{:S(2)}) collective-permute-start(bf16[1040,128]{1,0:T(8,128)(2,1)S(1)} %get-tuple-element.19), channel_id=1, source_target_pairs={{0,16},{8,24},{16,0},{24,8},{1,17},{9,25},{17,1},{25,9},{2,18},{10... | collective-permute-start | bytes 798728 | tf_op jit(solution)/shard_map/ppermute | solution.py:160
  7.1 11.9 %collective-permute-start.6 = (bf16[1040,128]{1,0:T(8,128)(2,1)S(1)}, bf16[1040,128]{1,0:T(8,128)(2,1)S(1)}, u32[]{:S(2)}, u32[]{:S(2)}) collective-permute-start(bf16[1040,128]{1,0:T(8,128)(2,1)S(1)} %get-tuple-element.20), channel_id=1, source_target_pairs={{0,24},{8,16},{16,8},{24,0},{1,25},{9,17},{17,9},{25,1},{2,26},{10... | collective-permute-start | bytes 798728 | tf_op jit(solution)/shard_map/ppermute | solution.py:160
  10.1 8.9 %collective-permute-start.4 = (bf16[288,256]{1,0:T(8,128)(2,1)S(1)}, bf16[288,256]{1,0:T(8,128)(2,1)S(1)}, u32[]{:S(2)}, u32[]{:S(2)}) collective-permute-start(bf16[288,256]{1,0:T(8,128)(2,1)S(1)} %pad_maximum_fusion.a_ref), channel_id=1, source_target_pairs={{0,3},{1,2},{2,1},{3,0},{4,7},{5,6},{6,5},{7,4},{8,11},{9,10},{10,... | collective-permute-start | bytes 442376 | tf_op jit(solution)/shard_map/ppermute | solution.py:163
  11.9 8.0 %collective-permute-start.3 = (bf16[288,256]{1,0:T(8,128)(2,1)S(1)}, bf16[288,256]{1,0:T(8,128)(2,1)S(1)}, u32[]{:S(2)}, u32[]{:S(2)}) collective-permute-start(bf16[288,256]{1,0:T(8,128)(2,1)S(1)} %pad_maximum_fusion.a_ref), channel_id=1, source_target_pairs={{0,1},{1,0},{2,3},{3,2},{4,5},{5,4},{6,7},{7,6},{8,9},{9,8},{10,11... | collective-permute-start | bytes 442376 | tf_op jit(solution)/shard_map/ppermute | solution.py:163
  12.4 7.4 %collective-permute-start.2 = (bf16[288,256]{1,0:T(8,128)(2,1)S(1)}, bf16[288,256]{1,0:T(8,128)(2,1)S(1)}, u32[]{:S(2)}, u32[]{:S(2)}) collective-permute-start(bf16[288,256]{1,0:T(8,128)(2,1)S(1)} %pad_maximum_fusion.a_ref), channel_id=1, source_target_pairs={{0,2},{1,3},{2,0},{3,1},{4,6},{5,7},{6,4},{7,5},{8,10},{9,11},{10,... | collective-permute-start | bytes 442376 | tf_op jit(solution)/shard_map/ppermute | solution.py:163
  21.3 3.8 %collective-permute-start.7 = (f32[32,128]{1,0:T(8,128)S(1)}, f32[32,128]{1,0:T(8,128)S(1)}, u32[]{:S(2)}, u32[]{:S(2)}) collective-permute-start(f32[32,128]{1,0:T(8,128)S(1)} %get-tuple-element.24), channel_id=1, source_target_pairs={{0,16},{8,24},{16,0},{24,8},{1,17},{9,25},{17,1},{25,9},{2,18},{10... | collective-permute-start | bytes 49160 | tf_op jit(solution)/shard_map/ppermute | solution.py:160
  22.8 3.3 %collective-permute-start.8 = (f32[32,128]{1,0:T(8,128)S(1)}, f32[32,128]{1,0:T(8,128)S(1)}, u32[]{:S(2)}, u32[]{:S(2)}) collective-permute-start(f32[32,128]{1,0:T(8,128)S(1)} %get-tuple-element.25), channel_id=1, source_target_pairs={{0,24},{8,16},{16,8},{24,0},{1,25},{9,17},{17,9},{25,1},{2,26},{10... | collective-permute-start | bytes 49160 | tf_op jit(solution)/shard_map/ppermute | solution.py:160
  22.8 3.3 %collective-permute-start.9 = (f32[32,128]{1,0:T(8,128)S(1)}, f32[32,128]{1,0:T(8,128)S(1)}, u32[]{:S(2)}, u32[]{:S(2)}) collective-permute-start(f32[32,128]{1,0:T(8,128)S(1)} %get-tuple-element.26), channel_id=1, source_target_pairs={{0,8},{8,0},{16,24},{24,16},{1,9},{9,1},{17,25},{25,17},{2,10},{10... | collective-permute-start | bytes 49160 | tf_op jit(solution)/shard_map/ppermute | solution.py:160

commit v3 on v2

--- a/solution.py
+++ b/solution.py
@@ -69,78 +69,59 @@
         copy.wait()
 
 
-def slot_kernel(n_panel, n_obs, cap, a_ref, b_ref, ya_ref, yb_ref, gate_ref, out_ref, slots_ref):
+def part_kernel(n_panel, n_obs, cap, quads, which, last, *refs):
+    buffers, pieces = dict(zip(which, refs)), refs[len(which) : len(which) + n_panel]
+    rest, acc_ref = refs[len(which) + n_panel : -1], refs[-1]
     count = n_panel * n_obs
     me_p = lax.axis_index("panel")
     me_o = lax.axis_index("obs")
-    rows = a_ref.shape[0] // (n_obs // 4) - EXTRA
-    steps = a_ref.shape[1] // 2
+    rows = refs[0].shape[0] // (n_obs // 4) - EXTRA
+    steps = refs[0].shape[1] // 2
     per = 16 // cap
+    width = n_obs * cap
+    depth = n_obs * width
+    acc_ref[...] = jnp.zeros_like(acc_ref)
+    if last:
+        acc_ref[0:steps] = rest[0][...]
     slot_ids = lax.broadcasted_iota(jnp.int32, (count * 16, per * rows), 0)
-    for quad in range(n_obs // per):
+    groups, starts = [], []
+    for quad in quads:
         values, places = [], []
         for i in range(per):
             j = quad * per + i
-            ref = (a_ref, ya_ref, b_ref, yb_ref)[j % 4]
-            base = (j // 4) * (rows + EXTRA)
+            ref, base = buffers[j % 4], (j // 4) * (rows + EXTRA)
             tail = ref[base + rows : base + rows + EXTRA, :].astype(jnp.float32)[0:1].astype(jnp.int32)
             dest, rank = tail[:, 0:rows], tail[:, steps : steps + rows]
             within = ((me_o % per) ^ i) * cap + rank
             places.append((dest ^ (me_p * n_obs)) * 16 + within)
             values.append(ref[base : base + rows, :])
-        value = jnp.concatenate(values, axis=0)
-        place = jnp.concatenate(places, axis=1)
-        pick = (slot_ids == place).astype(jnp.bfloat16)
-        got = dot(pick, value).astype(jnp.bfloat16)
-        start = pl.multiple_of(((me_o // per) ^ quad) * 16, 16)
-        slots_ref[:, pl.ds(start, 16), :] = got.reshape(count, 16, 2 * steps)
-    for k in range(out_ref.shape[0]):
-        block = slots_ref[2 * k : 2 * k + 2].reshape(2 * n_obs * cap, 2 * steps)
-        out_ref[k, :, 0 : 2 * n_obs * cap] = block[:, 0:steps].T
-        out_ref[k, :, 2 * n_obs * cap :] = block[:, steps:].T
-
-
-def add_term(acc_ref, source, weights, delay):
-    steps = source.shape[0]
-    acc_ref[pl.ds(delay, steps), :] += dot(source, weights)
-
-
-def late_kernel(depth, x_ref, xc_ref, out_ref):
-    for i, ref in enumerate((x_ref, xc_ref)):
-        out_ref[8 * i : 8 * i + 8] = ref[depth : depth + EXTRA, :].astype(jnp.float32)[0:8].astype(jnp.int32)
-
-
-def near_kernel(n_obs, width, s_ref, own_ref, c_ref, out_ref, acc_ref):
-    steps = out_ref.shape[0]
-    nblocks = n_obs // 2
-    acc_ref[...] = jnp.zeros_like(acc_ref)
-    piece_terms(nblocks, width, s_ref, 0, own_ref, acc_ref)
-    piece_terms(nblocks, width, s_ref, nblocks, c_ref, acc_ref)
-    out_ref[...] = acc_ref[0:steps]
-
-
-def piece_terms(nblocks, width, s_ref, first, w_ref, acc_ref):
-    depth = 2 * width * nblocks
-    delays = w_ref[2 * depth : 2 * depth + EXTRA, :].astype(jnp.float32)[0:1].astype(jnp.int32)
-    for b in range(nblocks):
-        lo, hi = 2 * width * b, 2 * width * (b + 1)
-        weights = jnp.concatenate([w_ref[lo:hi], w_ref[depth + lo : depth + hi]], axis=0)
-        add_term(acc_ref, s_ref[first + b], weights, delays[0, b])
-
-
-def far_kernel(n_panel, n_obs, width, s_ref, near_ref, x_ref, xc_ref, *refs):
-    outs, acc_ref = refs[:n_panel], refs[n_panel]
-    me_p = lax.axis_index("panel")
-    steps = near_ref.shape[0]
-    nblocks = n_obs // 2
-    acc_ref[0:steps] = near_ref[...]
-    acc_ref[steps:] = jnp.zeros_like(acc_ref[steps:])
-    piece_terms(nblocks, width, s_ref, 2 * nblocks, x_ref, acc_ref)
-    piece_terms(nblocks, width, s_ref, 3 * nblocks, xc_ref, acc_ref)
+        pick = (slot_ids == jnp.concatenate(places, axis=1)).astype(jnp.bfloat16)
+        groups.append(dot(pick, jnp.concatenate(values, axis=0)).astype(jnp.bfloat16))
+        starts.append(((me_o // per) ^ quad) * 16)
+    for k in range(n_panel):
+        delays = pieces[k][2 * depth : 2 * depth + EXTRA, :].astype(jnp.float32)[0:1].astype(jnp.int32)
+        for b in range(n_obs // 2):
+            row = 32 * (k * (n_obs // 2) + b)
+            source = jnp.concatenate(
+                [g[row : row + 32, c * steps : (c + 1) * steps] for c in range(2) for g in groups], axis=0
+            )
+            weights = jnp.concatenate(
+                [
+                    pieces[k][pl.ds(pl.multiple_of(c * depth + (2 * b + h) * width + start, 16), 16), :]
+                    for c in range(2)
+                    for start in starts
+                    for h in range(2)
+                ],
+                axis=0,
+            )
+            acc_ref[pl.ds(delays[0, b], steps), :] += dot(source.T, weights)
+    if not last:
+        rest[0][...] = acc_ref[0:steps]
+        return
     share = steps // n_panel
     for k in range(n_panel):
         start = pl.multiple_of((me_p ^ k) * share, share)
-        outs[k][...] = acc_ref[pl.ds(start, share), :]
+        rest[1 + k][...] = acc_ref[pl.ds(start, share), :]
 
 
 def per_device(les_rows, les_dest, loading_weight, thickness_weight, delays):
@@ -195,41 +176,21 @@
     a, from_c = lax.optimization_barrier((a, from_c))
     b, ya, yb = along_obs(a, 2), along_obs(a, 1), along_obs(a, 3)
 
-    late = pl.pallas_call(
-        functools.partial(late_kernel, 2 * n_obs * width),
-        out_shape=jax.ShapeDtypeStruct((16, observers), jnp.int32),
-        in_specs=[vmem] * 2,
-        out_specs=vmem,
-        compiler_params=params,
-        cost_estimate=pl.CostEstimate(flops=10**0, bytes_accessed=0, transcendentals=0),
-    )(from_x, from_xc)
-
-    sources = pl.pallas_call(
-        functools.partial(slot_kernel, n_panel, n_obs, cap),
-        out_shape=jax.ShapeDtypeStruct((count // 2, steps, 4 * width), jnp.bfloat16),
-        in_specs=[vmem] * 5,
-        out_specs=vmem,
-        scratch_shapes=[pltpu.VMEM((count, width, 2 * steps), jnp.bfloat16)],
-        compiler_params=params,
-    )(a, b, ya, yb, late)
-    acc = pltpu.VMEM((2 * steps, observers), jnp.float32)
-    near = pl.pallas_call(
-        functools.partial(near_kernel, n_obs, width),
-        out_shape=jax.ShapeDtypeStruct((steps, observers), jnp.float32),
-        in_specs=[vmem] * 3,
-        out_specs=vmem,
-        scratch_shapes=[acc],
-        compiler_params=params,
-    )(sources, own, from_c)
+    buffers, pieces = (a, ya, b, yb), (own, from_c, from_x, from_xc)
+    per = 16 // cap
     share = jax.ShapeDtypeStruct((steps // n_panel, observers), jnp.float32)
-    shares = pl.pallas_call(
-        functools.partial(far_kernel, n_panel, n_obs, width),
-        out_shape=[share] * n_panel,
-        in_specs=[vmem] * 4,
-        out_specs=[vmem] * n_panel,
-        scratch_shapes=[acc],
-        compiler_params=params,
-    )(sources, near, from_x, from_xc)
+    shares = []
+    for last in (False, True):
+        quads = [q for q in range(n_obs // per) if q % 2 == last]
+        which = sorted({j % 4 for q in quads for j in range(q * per, (q + 1) * per)})
+        shares = pl.pallas_call(
+            functools.partial(part_kernel, n_panel, n_obs, cap, quads, which, last),
+            out_shape=[share] * n_panel if last else [jax.ShapeDtypeStruct((steps, observers), jnp.float32)],
+            in_specs=[vmem] * (len(which) + n_panel + last),
+            out_specs=[vmem] * (n_panel if last else 1),
+            scratch_shapes=[pltpu.VMEM((2 * steps, observers), jnp.float32)],
+            compiler_params=params,
+        )(*(buffers[w] for w in which), *pieces, *shares)
     total = shares[0]
     for k in (2, 3, 1):
         total = total + along_panel(shares[k], k)

time: 26.8 us -> 26.1 us (0.974)
  waiting for transfers between devices: 11.7 us -> 11.2 us
    ppermute x4, waiting for transfers between devices: 3.71 us -> 3.39 us  [along_obs(): return lax.ppermute(value, 'obs', [(i, i ^ k) for i in range(n_obs)])]
    pallas_call x4 -> x2, Pallas kernels: 1.43 us -> 1.18 us  [per_device(): pl.pallas_call(functools.partial(part_kernel, n_panel, n_obs, cap, quads,...]
  transfers between devices with their start and end apart: 10 -> 10, of which waited for: 6 -> 6; matrix products, arithmetic and copies ran while one was open for 0% -> 0% of each run, Pallas kernels for 0% -> 2%
where the time goes in v3:
time: 26.1 us; the launch traced here: 25.9 us
  starting transfers between devices  11.5 us (44%)
  waiting for transfers between devices  11.2 us (43%)
  Pallas kernels  2.61 us (10%)
  other arithmetic  0.62 us (2%)
    ppermute x6, waiting for transfers between devices, along_panel(): return lax.ppermute(value, 'panel', [(i, i ^ k) for i in range(n_panel)])  7.77 us
    ppermute x4, starting transfers between devices, along_obs(): return lax.ppermute(value, 'obs', [(i, i ^ k) for i in range(n_obs)])  7.22 us
    ppermute x6, starting transfers between devices, along_panel(): return lax.ppermute(value, 'panel', [(i, i ^ k) for i in range(n_panel)])  4.26 us
    ppermute x4, waiting for transfers between devices, along_obs(): return lax.ppermute(value, 'obs', [(i, i ^ k) for i in range(n_obs)])  3.39 us
    pallas_call x1, Pallas kernels, per_device(): pl.pallas_call(functools.partial(pack_kernel, n_panel, n_obs, cap), out_s...  1.43 us
    pallas_call x2, Pallas kernels, per_device(): pl.pallas_call(functools.partial(part_kernel, n_panel, n_obs, cap, quads,...  1.18 us
    add x1, other arithmetic, per_device(): total = total + along_panel(shares[k], k)  0.61 us
  transfers between devices with their start and end apart: 10, of which 6 were waited for; matrix products, arithmetic and copies ran while one was open for 0% of the time, Pallas kernels for 2%

profile of v3, /device:TPU:0, one launch (start us, length us, event | category | flops | bytes accessed | tf_op | source)
XLA Modules:
  0.0 25.9 jit_solution(13470982653219210715)
XLA Ops:
  0.0 1.4 %shard_map.55 = (bf16[144,256]{1,0:T(8,128)(2,1)S(1)}, bf16[1040,128]{1,0:T(8,128)(2,1)S(1)}, bf16[1040,128]{1,0:T(8,128)(2,1)S(1)}, bf16[1040,128]{1,0:T(8,128)(2,1)S(1)}, bf16[1040,128]{1,0:T(8,128)(2,1)S(1)}) custom-call(bf16[256,128]{1,0:T(8,128)(2,1)} %bitcast.7, s32[1,128]{1,0:T(1,128)} %bitcast.8, s32[1,4]{1,0:T(1,128)} %bitcast.9, ...), custom_call_target="tpu_custom_call" | custom-call | tf_op jit(solution)/shard_map/pallas_call | solution.py:149
  1.4 0.5 %collective-permute-start.1 = (bf16[1040,128]{1,0:T(8,128)(2,1)S(1)}, bf16[1040,128]{1,0:T(8,128)(2,1)S(1)}, u32[]{:S(2)}, u32[]{:S(2)}) collective-permute-start(bf16[1040,128]{1,0:T(8,128)(2,1)S(1)} %get-tuple-element.17), channel_id=1, source_target_pairs={{0,8},{8,0},{16,24},{24,16},{1,9},{9,1},{17,25},{25,17},{2,10},{10... | collective-permute-start | bytes 798728 | tf_op jit(solution)/shard_map/ppermute | solution.py:141
  2.0 3.7 %collective-permute-start = (bf16[144,256]{1,0:T(8,128)(2,1)S(1)}, bf16[144,256]{1,0:T(8,128)(2,1)S(1)}, u32[]{:S(2)}, u32[]{:S(2)}) collective-permute-start(bf16[144,256]{1,0:T(8,128)(2,1)S(1)} %get-tuple-element.16), channel_id=1, source_target_pairs={{0,4},{1,5},{2,6},{3,7},{4,0},{5,1},{6,2},{7,3},{8,12},{9,13},{10,... | collective-permute-start | bytes 221192 | tf_op jit(solution)/shard_map/ppermute | solution.py:144
  5.6 1.5 %collective-permute-start.4 = (bf16[1040,128]{1,0:T(8,128)(2,1)S(1)}, bf16[1040,128]{1,0:T(8,128)(2,1)S(1)}, u32[]{:S(2)}, u32[]{:S(2)}) collective-permute-start(bf16[1040,128]{1,0:T(8,128)(2,1)S(1)} %get-tuple-element.21), channel_id=1, source_target_pairs={{0,16},{8,24},{16,0},{24,8},{1,17},{9,25},{17,1},{25,9},{2,18},{10... | collective-permute-start | bytes 798728 | tf_op jit(solution)/shard_map/ppermute | solution.py:141
  7.1 0.0 collective-permute-start.5
  7.1 2.9 %collective-permute-done = bf16[144,256]{1,0:T(8,128)(2,1)S(1)} collective-permute-done((bf16[144,256]{1,0:T(8,128)(2,1)S(1)}, bf16[144,256]{1,0:T(8,128)(2,1)S(1)}, u32[]{:S(2)}, u32[]{:S(2)}) %collective-permute-start) | collective-permute-done | bytes 73760 | tf_op jit(solution)/shard_map/ppermute | solution.py:144
  10.1 0.0 collective-permute-done.1.refs_3_
  10.1 1.7 %collective-permute-start.6 = (bf16[288,256]{1,0:T(8,128)(2,1)S(1)}, bf16[288,256]{1,0:T(8,128)(2,1)S(1)}, u32[]{:S(2)}, u32[]{:S(2)}) collective-permute-start(bf16[288,256]{1,0:T(8,128)(2,1)S(1)} %pad_maximum_fusion.refs_0_), channel_id=1, source_target_pairs={{0,1},{1,0},{2,3},{3,2},{4,5},{5,4},{6,7},{7,6},{8,9},{9,8},{10,11... | collective-permute-start | bytes 442376 | tf_op jit(solution)/shard_map/ppermute | solution.py:144
  11.7 0.7 %collective-permute-start.2 = (bf16[288,256]{1,0:T(8,128)(2,1)S(1)}, bf16[288,256]{1,0:T(8,128)(2,1)S(1)}, u32[]{:S(2)}, u32[]{:S(2)}) collective-permute-start(bf16[288,256]{1,0:T(8,128)(2,1)S(1)} %pad_maximum_fusion.refs_0_), channel_id=1, source_target_pairs={{0,2},{1,3},{2,0},{3,1},{4,6},{5,7},{6,4},{7,5},{8,10},{9,11},{10,... | collective-permute-start | bytes 442376 | tf_op jit(solution)/shard_map/ppermute | solution.py:144
  12.4 1.2 %collective-permute-start.3 = (bf16[288,256]{1,0:T(8,128)(2,1)S(1)}, bf16[288,256]{1,0:T(8,128)(2,1)S(1)}, u32[]{:S(2)}, u32[]{:S(2)}) collective-permute-start(bf16[288,256]{1,0:T(8,128)(2,1)S(1)} %pad_maximum_fusion.refs_0_), channel_id=1, source_target_pairs={{0,3},{1,2},{2,1},{3,0},{4,7},{5,6},{6,5},{7,4},{8,11},{9,10},{10,... | collective-permute-start | bytes 442376 | tf_op jit(solution)/shard_map/ppermute | solution.py:144
  13.6 1.2 %collective-permute-done.4.refs_4_ = bf16[1040,128]{1,0:T(8,128)(2,1)S(1)} collective-permute-done((bf16[1040,128]{1,0:T(8,128)(2,1)S(1)}, bf16[1040,128]{1,0:T(8,128)(2,1)S(1)}, u32[]{:S(2)}, u32[]{:S(2)}) %collective-permute-start.4) | collective-permute-done | bytes 266272 | tf_op jit(solution)/shard_map/ppermute | solution.py:141
  14.9 4.2 %collective-permute-done.5.refs_5_ = bf16[1040,128]{1,0:T(8,128)(2,1)S(1)} collective-permute-done((bf16[1040,128]{1,0:T(8,128)(2,1)S(1)}, bf16[1040,128]{1,0:T(8,128)(2,1)S(1)}, u32[]{:S(2)}, u32[]{:S(2)}) %collective-permute-start.5) | collective-permute-done | bytes 266272 | tf_op jit(solution)/shard_map/ppermute | solution.py:141
  19.0 0.0 collective-permute-done.6.refs_1_
  19.0 0.6 %shard_map.56.refs_6_ = f32[128,128]{1,0:T(8,128)S(1)} custom-call(bf16[288,256]{1,0:T(8,128)(2,1)S(1)} %pad_maximum_fusion.refs_0_, bf16[288,256]{1,0:T(8,128)(2,1)S(1)} %collective-permute-done.6.refs_1_, bf16[1040,128]{1,0:T(8,128)(2,1)S(1)} %get-tuple-element.19.refs_2_, bf16[1040,128]{1,0:T(8,128)(2,1)S(1)} %collective-permute-done.1.refs_3_, ...), custom_call_target="tpu_custom_call" | custom-call | tf_op jit(solution)/shard_map/pallas_call | solution.py:186
  19.6 0.0 collective-permute-done.2.refs_0_
  19.6 0.5 %collective-permute-done.3.refs_1_ = bf16[288,256]{1,0:T(8,128)(2,1)S(1)} collective-permute-done((bf16[288,256]{1,0:T(8,128)(2,1)S(1)}, bf16[288,256]{1,0:T(8,128)(2,1)S(1)}, u32[]{:S(2)}, u32[]{:S(2)}) %collective-permute-start.3) | collective-permute-done | bytes 147488 | tf_op jit(solution)/shard_map/ppermute | solution.py:144
  20.1 0.6 %shard_map.57 = (f32[32,128]{1,0:T(8,128)S(1)}, f32[32,128]{1,0:T(8,128)S(1)}, f32[32,128]{1,0:T(8,128)S(1)}, f32[32,128]{1,0:T(8,128)S(1)}) custom-call(bf16[288,256]{1,0:T(8,128)(2,1)S(1)} %collective-permute-done.2.refs_0_, bf16[288,256]{1,0:T(8,128)(2,1)S(1)} %collective-permute-done.3.refs_1_, bf16[1040,128]{1,0:T(8,128)(2,1)S(1)} %get-tuple-element.19.refs_2_, ...), custom_call_target="tpu_custom_call" | custom-call | tf_op jit(solution)/shard_map/pallas_call | solution.py:186
  20.7 1.4 %collective-permute-start.7 = (f32[32,128]{1,0:T(8,128)S(1)}, f32[32,128]{1,0:T(8,128)S(1)}, u32[]{:S(2)}, u32[]{:S(2)}) collective-permute-start(f32[32,128]{1,0:T(8,128)S(1)} %get-tuple-element.24), channel_id=1, source_target_pairs={{0,16},{8,24},{16,0},{24,8},{1,17},{9,25},{17,1},{25,9},{2,18},{10... | collective-permute-start | bytes 49160 | tf_op jit(solution)/shard_map/ppermute | solution.py:141
  22.1 0.4 %collective-permute-start.8 = (f32[32,128]{1,0:T(8,128)S(1)}, f32[32,128]{1,0:T(8,128)S(1)}, u32[]{:S(2)}, u32[]{:S(2)}) collective-permute-start(f32[32,128]{1,0:T(8,128)S(1)} %get-tuple-element.25), channel_id=1, source_target_pairs={{0,24},{8,16},{16,8},{24,0},{1,25},{9,17},{17,9},{25,1},{2,26},{10... | collective-permute-start | bytes 49160 | tf_op jit(solution)/shard_map/ppermute | solution.py:141
  22.5 0.3 %collective-permute-start.9 = (f32[32,128]{1,0:T(8,128)S(1)}, f32[32,128]{1,0:T(8,128)S(1)}, u32[]{:S(2)}, u32[]{:S(2)}) collective-permute-start(f32[32,128]{1,0:T(8,128)S(1)} %get-tuple-element.26), channel_id=1, source_target_pairs={{0,8},{8,0},{16,24},{24,16},{1,9},{9,1},{17,25},{25,17},{2,10},{10... | collective-permute-start | bytes 49160 | tf_op jit(solution)/shard_map/ppermute | solution.py:141
  22.9 1.6 %collective-permute-done.7 = f32[32,128]{1,0:T(8,128)S(1)} collective-permute-done((f32[32,128]{1,0:T(8,128)S(1)}, f32[32,128]{1,0:T(8,128)S(1)}, u32[]{:S(2)}, u32[]{:S(2)}) %collective-permute-start.7) | collective-permute-done | bytes 16416 | tf_op jit(solution)/shard_map/ppermute | solution.py:141
  24.5 0.8 %collective-permute-done.8 = f32[32,128]{1,0:T(8,128)S(1)} collective-permute-done((f32[32,128]{1,0:T(8,128)S(1)}, f32[32,128]{1,0:T(8,128)S(1)}, u32[]{:S(2)}, u32[]{:S(2)}) %collective-permute-start.8) | collective-permute-done | bytes 16416 | tf_op jit(solution)/shard_map/ppermute | solution.py:141
  25.3 0.0 collective-permute-done.9
  25.3 0.6 %add_add_fusion = f32[32,128]{1,0:T(8,128)} fusion(f32[32,128]{1,0:T(8,128)S(1)} %collective-permute-done.9, f32[32,128]{1,0:T(8,128)S(1)} %collective-permute-done.8, f32[32,128]{1,0:T(8,128)S(1)} %get-tuple-element.23, f32[32,128]{1,0:T(8,128)S(1)} %collective-permute-done.7), kind=kLoop, calls=%fused_computation.1 | loop fusion | flops 12288 | bytes 81920 | tf_op jit(solution)/shard_map/add | solution.py:196
  (1 shorter events, 0.0 us)
Async XLA Ops:
  1.4 8.6 %collective-permute-start.1 = (bf16[1040,128]{1,0:T(8,128)(2,1)S(1)}, bf16[1040,128]{1,0:T(8,128)(2,1)S(1)}, u32[]{:S(2)}, u32[]{:S(2)}) collective-permute-start(bf16[1040,128]{1,0:T(8,128)(2,1)S(1)} %get-tuple-element.17), channel_id=1, source_target_pairs={{0,8},{8,0},{16,24},{24,16},{1,9},{9,1},{17,25},{25,17},{2,10},{10... | collective-permute-start | bytes 798728 | tf_op jit(solution)/shard_map/ppermute | solution.py:141
  2.0 8.1 %collective-permute-start = (bf16[144,256]{1,0:T(8,128)(2,1)S(1)}, bf16[144,256]{1,0:T(8,128)(2,1)S(1)}, u32[]{:S(2)}, u32[]{:S(2)}) collective-permute-start(bf16[144,256]{1,0:T(8,128)(2,1)S(1)} %get-tuple-element.16), channel_id=1, source_target_pairs={{0,4},{1,5},{2,6},{3,7},{4,0},{5,1},{6,2},{7,3},{8,12},{9,13},{10,... | collective-permute-start | bytes 221192 | tf_op jit(solution)/shard_map/ppermute | solution.py:144
  5.6 9.2 %collective-permute-start.4 = (bf16[1040,128]{1,0:T(8,128)(2,1)S(1)}, bf16[1040,128]{1,0:T(8,128)(2,1)S(1)}, u32[]{:S(2)}, u32[]{:S(2)}) collective-permute-start(bf16[1040,128]{1,0:T(8,128)(2,1)S(1)} %get-tuple-element.21), channel_id=1, source_target_pairs={{0,16},{8,24},{16,0},{24,8},{1,17},{9,25},{17,1},{25,9},{2,18},{10... | collective-permute-start | bytes 798728 | tf_op jit(solution)/shard_map/ppermute | solution.py:141
  7.1 11.9 %collective-permute-start.5 = (bf16[1040,128]{1,0:T(8,128)(2,1)S(1)}, bf16[1040,128]{1,0:T(8,128)(2,1)S(1)}, u32[]{:S(2)}, u32[]{:S(2)}) collective-permute-start(bf16[1040,128]{1,0:T(8,128)(2,1)S(1)} %get-tuple-element.22), channel_id=1, source_target_pairs={{0,24},{8,16},{16,8},{24,0},{1,25},{9,17},{17,9},{25,1},{2,26},{10... | collective-permute-start | bytes 798728 | tf_op jit(solution)/shard_map/ppermute | solution.py:141
  10.1 8.9 %collective-permute-start.6 = (bf16[288,256]{1,0:T(8,128)(2,1)S(1)}, bf16[288,256]{1,0:T(8,128)(2,1)S(1)}, u32[]{:S(2)}, u32[]{:S(2)}) collective-permute-start(bf16[288,256]{1,0:T(8,128)(2,1)S(1)} %pad_maximum_fusion.refs_0_), channel_id=1, source_target_pairs={{0,1},{1,0},{2,3},{3,2},{4,5},{5,4},{6,7},{7,6},{8,9},{9,8},{10,11... | collective-permute-start | bytes 442376 | tf_op jit(solution)/shard_map/ppermute | solution.py:144
  11.7 7.9 %collective-permute-start.2 = (bf16[288,256]{1,0:T(8,128)(2,1)S(1)}, bf16[288,256]{1,0:T(8,128)(2,1)S(1)}, u32[]{:S(2)}, u32[]{:S(2)}) collective-permute-start(bf16[288,256]{1,0:T(8,128)(2,1)S(1)} %pad_maximum_fusion.refs_0_), channel_id=1, source_target_pairs={{0,2},{1,3},{2,0},{3,1},{4,6},{5,7},{6,4},{7,5},{8,10},{9,11},{10,... | collective-permute-start | bytes 442376 | tf_op jit(solution)/shard_map/ppermute | solution.py:144
  12.4 7.7 %collective-permute-start.3 = (bf16[288,256]{1,0:T(8,128)(2,1)S(1)}, bf16[288,256]{1,0:T(8,128)(2,1)S(1)}, u32[]{:S(2)}, u32[]{:S(2)}) collective-permute-start(bf16[288,256]{1,0:T(8,128)(2,1)S(1)} %pad_maximum_fusion.refs_0_), channel_id=1, source_target_pairs={{0,3},{1,2},{2,1},{3,0},{4,7},{5,6},{6,5},{7,4},{8,11},{9,10},{10,... | collective-permute-start | bytes 442376 | tf_op jit(solution)/shard_map/ppermute | solution.py:144
  20.7 3.8 %collective-permute-start.7 = (f32[32,128]{1,0:T(8,128)S(1)}, f32[32,128]{1,0:T(8,128)S(1)}, u32[]{:S(2)}, u32[]{:S(2)}) collective-permute-start(f32[32,128]{1,0:T(8,128)S(1)} %get-tuple-element.24), channel_id=1, source_target_pairs={{0,16},{8,24},{16,0},{24,8},{1,17},{9,25},{17,1},{25,9},{2,18},{10... | collective-permute-start | bytes 49160 | tf_op jit(solution)/shard_map/ppermute | solution.py:141
  22.1 3.2 %collective-permute-start.8 = (f32[32,128]{1,0:T(8,128)S(1)}, f32[32,128]{1,0:T(8,128)S(1)}, u32[]{:S(2)}, u32[]{:S(2)}) collective-permute-start(f32[32,128]{1,0:T(8,128)S(1)} %get-tuple-element.25), channel_id=1, source_target_pairs={{0,24},{8,16},{16,8},{24,0},{1,25},{9,17},{17,9},{25,1},{2,26},{10... | collective-permute-start | bytes 49160 | tf_op jit(solution)/shard_map/ppermute | solution.py:141
  22.5 2.7 %collective-permute-start.9 = (f32[32,128]{1,0:T(8,128)S(1)}, f32[32,128]{1,0:T(8,128)S(1)}, u32[]{:S(2)}, u32[]{:S(2)}) collective-permute-start(f32[32,128]{1,0:T(8,128)S(1)} %get-tuple-element.26), channel_id=1, source_target_pairs={{0,8},{8,0},{16,24},{24,16},{1,9},{9,1},{17,25},{25,17},{2,10},{10... | collective-permute-start | bytes 49160 | tf_op jit(solution)/shard_map/ppermute | solution.py:141

commit v4 on v2

--- a/solution.py
+++ b/solution.py
@@ -9,6 +9,7 @@
 
 PBLK = 512
 PACK_ORDER = (2, 3, 1, 0)
+F_JOIN, F_LATE, F_NEAR = 4000000000, 10000000000, 2000000000
 EXTRA = 16
 VMEM_LIMIT = 48 * 1024 * 1024
 
@@ -69,74 +70,80 @@
         copy.wait()
 
 
-def slot_kernel(n_panel, n_obs, cap, a_ref, b_ref, ya_ref, yb_ref, gate_ref, out_ref, slots_ref):
+def late_kernel(*refs):
+    for i, ref in enumerate(refs[:-1]):
+        tail = ref[ref.shape[0] - EXTRA :, :].astype(jnp.float32)[0:8]
+        refs[-1][8 * i : 8 * i + 8] = tail.astype(jnp.int32)
+
+
+def join_kernel(*refs):
+    at = 0
+    for ref in refs[:-1]:
+        refs[-1][at : at + ref.shape[0]] = ref[...]
+        at += ref.shape[0]
+
+
+def add_terms(n_obs, width, sources, pieces, delays, acc_ref):
+    steps = sources[0].shape[1]
+    depth = n_obs * width
+    for source, piece, late in zip(sources, pieces, delays):
+        for b in range(n_obs // 2):
+            lo, hi = 2 * width * b, 2 * width * (b + 1)
+            weights = jnp.concatenate([piece[lo:hi], piece[depth + lo : depth + hi]], axis=0)
+            acc_ref[pl.ds(late[0, b], steps), :] += dot(source[b], weights)
+
+
+def late_row(piece):
+    return piece[piece.shape[0] - EXTRA :, :].astype(jnp.float32)[0:1].astype(jnp.int32)
+
+
+def near_kernel(n_panel, n_obs, cap, a_ref, ya_ref, b_ref, yb_ref, own_ref, c_ref, near_ref, *refs):
+    outs, (slots_ref, mine_ref, acc_ref) = refs[: n_panel - 2], refs[n_panel - 2 :]
     count = n_panel * n_obs
     me_p = lax.axis_index("panel")
     me_o = lax.axis_index("obs")
     rows = a_ref.shape[0] // (n_obs // 4) - EXTRA
     steps = a_ref.shape[1] // 2
     per = 16 // cap
+    width = n_obs * cap
     slot_ids = lax.broadcasted_iota(jnp.int32, (count * 16, per * rows), 0)
     for quad in range(n_obs // per):
         values, places = [], []
         for i in range(per):
             j = quad * per + i
-            ref = (a_ref, ya_ref, b_ref, yb_ref)[j % 4]
-            base = (j // 4) * (rows + EXTRA)
+            ref, base = (a_ref, ya_ref, b_ref, yb_ref)[j % 4], (j // 4) * (rows + EXTRA)
             tail = ref[base + rows : base + rows + EXTRA, :].astype(jnp.float32)[0:1].astype(jnp.int32)
             dest, rank = tail[:, 0:rows], tail[:, steps : steps + rows]
             within = ((me_o % per) ^ i) * cap + rank
             places.append((dest ^ (me_p * n_obs)) * 16 + within)
             values.append(ref[base : base + rows, :])
-        value = jnp.concatenate(values, axis=0)
-        place = jnp.concatenate(places, axis=1)
-        pick = (slot_ids == place).astype(jnp.bfloat16)
-        got = dot(pick, value).astype(jnp.bfloat16)
+        pick = (slot_ids == jnp.concatenate(places, axis=1)).astype(jnp.bfloat16)
+        got = dot(pick, jnp.concatenate(values, axis=0)).astype(jnp.bfloat16)
         start = pl.multiple_of(((me_o // per) ^ quad) * 16, 16)
         slots_ref[:, pl.ds(start, 16), :] = got.reshape(count, 16, 2 * steps)
-    for k in range(out_ref.shape[0]):
-        block = slots_ref[2 * k : 2 * k + 2].reshape(2 * n_obs * cap, 2 * steps)
-        out_ref[k, :, 0 : 2 * n_obs * cap] = block[:, 0:steps].T
-        out_ref[k, :, 2 * n_obs * cap :] = block[:, steps:].T
-
-
-def add_term(acc_ref, source, weights, delay):
-    steps = source.shape[0]
-    acc_ref[pl.ds(delay, steps), :] += dot(source, weights)
-
-
-def late_kernel(depth, x_ref, xc_ref, out_ref):
-    for i, ref in enumerate((x_ref, xc_ref)):
-        out_ref[8 * i : 8 * i + 8] = ref[depth : depth + EXTRA, :].astype(jnp.float32)[0:8].astype(jnp.int32)
-
-
-def near_kernel(n_obs, width, s_ref, own_ref, c_ref, out_ref, acc_ref):
-    steps = out_ref.shape[0]
-    nblocks = n_obs // 2
+    for k in range(n_panel):
+        for b in range(n_obs // 2):
+            at = k * n_obs + 2 * b
+            block = slots_ref[at : at + 2].reshape(2 * width, 2 * steps)
+            into = mine_ref.at[k * (n_obs // 2) + b] if k < 2 else outs[k - 2].at[b]
+            into[:, 0 : 2 * width] = block[:, 0:steps].T
+            into[:, 2 * width :] = block[:, steps:].T
     acc_ref[...] = jnp.zeros_like(acc_ref)
-    piece_terms(nblocks, width, s_ref, 0, own_ref, acc_ref)
-    piece_terms(nblocks, width, s_ref, nblocks, c_ref, acc_ref)
-    out_ref[...] = acc_ref[0:steps]
-
-
-def piece_terms(nblocks, width, s_ref, first, w_ref, acc_ref):
-    depth = 2 * width * nblocks
-    delays = w_ref[2 * depth : 2 * depth + EXTRA, :].astype(jnp.float32)[0:1].astype(jnp.int32)
-    for b in range(nblocks):
-        lo, hi = 2 * width * b, 2 * width * (b + 1)
-        weights = jnp.concatenate([w_ref[lo:hi], w_ref[depth + lo : depth + hi]], axis=0)
-        add_term(acc_ref, s_ref[first + b], weights, delays[0, b])
-
-
-def far_kernel(n_panel, n_obs, width, s_ref, near_ref, x_ref, xc_ref, *refs):
-    outs, acc_ref = refs[:n_panel], refs[n_panel]
+    mine = [mine_ref.at[k * (n_obs // 2) : (k + 1) * (n_obs // 2)] for k in range(2)]
+    add_terms(n_obs, width, mine, (own_ref, c_ref), (late_row(own_ref), late_row(c_ref)), acc_ref)
+    near_ref[...] = acc_ref[0:steps]
+
+
+def far_kernel(n_panel, n_obs, width, near_ref, *refs):
+    far = n_panel - 2
+    sources, pieces, late_ref = refs[:far], refs[far : 2 * far], refs[2 * far]
+    outs, acc_ref = refs[2 * far + 1 : -1], refs[-1]
     me_p = lax.axis_index("panel")
     steps = near_ref.shape[0]
-    nblocks = n_obs // 2
     acc_ref[0:steps] = near_ref[...]
     acc_ref[steps:] = jnp.zeros_like(acc_ref[steps:])
-    piece_terms(nblocks, width, s_ref, 2 * nblocks, x_ref, acc_ref)
-    piece_terms(nblocks, width, s_ref, 3 * nblocks, xc_ref, acc_ref)
+    delays = [late_ref[8 * k : 8 * k + 8][0:1] for k in range(far)]
+    add_terms(n_obs, width, sources, pieces, delays, acc_ref)
     share = steps // n_panel
     for k in range(n_panel):
         start = pl.multiple_of((me_p ^ k) * share, share)
@@ -191,45 +198,54 @@
         )
     )
     from_x, from_xc, from_c = along_panel(to_x, 2), along_panel(to_xc, 3), along_panel(to_c, 1)
-    a = jnp.concatenate([message] + [along_obs(message, k) for k in range(4, n_obs, 4)], axis=0)
-    a, from_c = lax.optimization_barrier((a, from_c))
-    b, ya, yb = along_obs(a, 2), along_obs(a, 1), along_obs(a, 3)
-
+    ranges = range(4, n_obs, 4)
+    far = [along_obs(message, k) for k in ranges]
+    later, from_c = lax.optimization_barrier((message, from_c))
+    near = along_obs(later, 3)
+    a = pl.pallas_call(
+        join_kernel,
+        out_shape=jax.ShapeDtypeStruct((n_obs // 4 * (rows + EXTRA), 2 * steps), jnp.bfloat16),
+        in_specs=[vmem] * (n_obs // 4),
+        out_specs=vmem,
+        compiler_params=params,
+        cost_estimate=pl.CostEstimate(flops=F_JOIN, bytes_accessed=0, transcendentals=0),
+    )(message, *far)
+    ya, b = along_obs(a, 1), along_obs(a, 2)
+    again, near = lax.optimization_barrier((jnp.concatenate(far, axis=0), near))
+    yb = jnp.concatenate([near, along_obs(again, 3)], axis=0)
+
+    acc = pltpu.VMEM((2 * steps, observers), jnp.float32)
+    source = jax.ShapeDtypeStruct((nblocks, steps, 4 * width), jnp.bfloat16)
+    near, *sources = pl.pallas_call(
+        functools.partial(near_kernel, n_panel, n_obs, cap),
+        out_shape=[jax.ShapeDtypeStruct((steps, observers), jnp.float32)] + [source] * (n_panel - 2),
+        in_specs=[vmem] * 6,
+        out_specs=[vmem] * (n_panel - 1),
+        scratch_shapes=[
+            pltpu.VMEM((count, width, 2 * steps), jnp.bfloat16),
+            pltpu.VMEM((2 * nblocks, steps, 4 * width), jnp.bfloat16),
+            acc,
+        ],
+        compiler_params=params,
+        cost_estimate=pl.CostEstimate(flops=F_NEAR, bytes_accessed=0, transcendentals=0),
+    )(a, ya, b, yb, own, from_c)
+    pieces = (from_x, from_xc)
     late = pl.pallas_call(
-        functools.partial(late_kernel, 2 * n_obs * width),
-        out_shape=jax.ShapeDtypeStruct((16, observers), jnp.int32),
-        in_specs=[vmem] * 2,
+        late_kernel,
+        out_shape=jax.ShapeDtypeStruct((8 * len(pieces), observers), jnp.int32),
+        in_specs=[vmem] * len(pieces),
         out_specs=vmem,
         compiler_params=params,
-        cost_estimate=pl.CostEstimate(flops=10**0, bytes_accessed=0, transcendentals=0),
-    )(from_x, from_xc)
-
-    sources = pl.pallas_call(
-        functools.partial(slot_kernel, n_panel, n_obs, cap),
-        out_shape=jax.ShapeDtypeStruct((count // 2, steps, 4 * width), jnp.bfloat16),
-        in_specs=[vmem] * 5,
-        out_specs=vmem,
-        scratch_shapes=[pltpu.VMEM((count, width, 2 * steps), jnp.bfloat16)],
-        compiler_params=params,
-    )(a, b, ya, yb, late)
-    acc = pltpu.VMEM((2 * steps, observers), jnp.float32)
-    near = pl.pallas_call(
-        functools.partial(near_kernel, n_obs, width),
-        out_shape=jax.ShapeDtypeStruct((steps, observers), jnp.float32),
-        in_specs=[vmem] * 3,
-        out_specs=vmem,
-        scratch_shapes=[acc],
-        compiler_params=params,
-    )(sources, own, from_c)
-    share = jax.ShapeDtypeStruct((steps // n_panel, observers), jnp.float32)
+        cost_estimate=pl.CostEstimate(flops=F_LATE, bytes_accessed=0, transcendentals=0),
+    )(*pieces)
     shares = pl.pallas_call(
         functools.partial(far_kernel, n_panel, n_obs, width),
-        out_shape=[share] * n_panel,
-        in_specs=[vmem] * 4,
+        out_shape=[jax.ShapeDtypeStruct((steps // n_panel, observers), jnp.float32)] * n_panel,
+        in_specs=[vmem] * (2 + 2 * len(pieces)),
         out_specs=[vmem] * n_panel,
         scratch_shapes=[acc],
         compiler_params=params,
-    )(sources, near, from_x, from_xc)
+    )(near, *sources, *pieces, late)
     total = shares[0]
     for k in (2, 3, 1):
         total = total + along_panel(shares[k], k)

time: 26.8 us -> 25.8 us (0.963)
  waiting for transfers between devices: 11.7 us -> 6.65 us
  starting transfers between devices: 11.5 us -> 15.6 us
    ppermute x4 -> x5, starting transfers between devices: 7.22 us -> 11.4 us  [along_obs(): return lax.ppermute(value, 'obs', [(i, i ^ k) for i in range(n_obs)])]
    ppermute x4 -> x5, waiting for transfers between devices: 3.71 us -> 0.76 us  [along_obs(): return lax.ppermute(value, 'obs', [(i, i ^ k) for i in range(n_obs)])]
    ppermute x6, waiting for transfers between devices: 7.99 us -> 5.89 us  [along_panel(): return lax.ppermute(value, 'panel', [(i, i ^ k) for i in range(n_panel)])]
  transfers between devices with their start and end apart: 10 -> 11, of which waited for: 6 -> 5; matrix products, arithmetic and copies ran while one was open for 0% -> 0% of each run, Pallas kernels for 0% -> 0%
where the time goes in v4:
time: 25.8 us; the launch traced here: 25.6 us
  starting transfers between devices  15.6 us (60%)
  waiting for transfers between devices  6.65 us (26%)
  Pallas kernels  2.65 us (10%)
  other arithmetic  0.62 us (2%)
    ppermute x5, starting transfers between devices, along_obs(): return lax.ppermute(value, 'obs', [(i, i ^ k) for i in range(n_obs)])  11.4 us
    ppermute x6, waiting for transfers between devices, along_panel(): return lax.ppermute(value, 'panel', [(i, i ^ k) for i in range(n_panel)])  5.89 us
    ppermute x6, starting transfers between devices, along_panel(): return lax.ppermute(value, 'panel', [(i, i ^ k) for i in range(n_panel)])  4.26 us
    pallas_call x1, Pallas kernels, per_device(): pl.pallas_call(functools.partial(pack_kernel, n_panel, n_obs, cap), out_s...  1.43 us
    pallas_call x1, Pallas kernels, per_device(): pl.pallas_call(functools.partial(near_kernel, n_panel, n_obs, cap), out_s...  0.88 us
    ppermute x5, waiting for transfers between devices, along_obs(): return lax.ppermute(value, 'obs', [(i, i ^ k) for i in range(n_obs)])  0.76 us
    add x1, other arithmetic, per_device(): total = total + along_panel(shares[k], k)  0.61 us
  transfers between devices with their start and end apart: 11, of which 5 were waited for; matrix products, arithmetic and copies ran while one was open for 0% of the time, Pallas kernels for 0%

profile of v4, /device:TPU:0, one launch (start us, length us, event | category | flops | bytes accessed | tf_op | source)
XLA Modules:
  0.0 25.6 jit_solution(6077129903394724330)
XLA Ops:
  0.0 1.4 %shard_map.55 = (bf16[144,256]{1,0:T(8,128)(2,1)S(1)}, bf16[1040,128]{1,0:T(8,128)(2,1)S(1)}, bf16[1040,128]{1,0:T(8,128)(2,1)S(1)}, bf16[1040,128]{1,0:T(8,128)(2,1)S(1)}, bf16[1040,128]{1,0:T(8,128)(2,1)S(1)}) custom-call(bf16[256,128]{1,0:T(8,128)(2,1)} %bitcast.7, s32[1,128]{1,0:T(1,128)} %bitcast.8, s32[1,4]{1,0:T(1,128)} %bitcast.9, ...), custom_call_target="tpu_custom_call" | custom-call | tf_op jit(solution)/shard_map/pallas_call | solution.py:175
  1.4 0.5 %collective-permute-start.3 = (bf16[1040,128]{1,0:T(8,128)(2,1)S(1)}, bf16[1040,128]{1,0:T(8,128)(2,1)S(1)}, u32[]{:S(2)}, u32[]{:S(2)}) collective-permute-start(bf16[1040,128]{1,0:T(8,128)(2,1)S(1)} %get-tuple-element.22), channel_id=1, source_target_pairs={{0,8},{8,0},{16,24},{24,16},{1,9},{9,1},{17,25},{25,17},{2,10},{10... | collective-permute-start | bytes 798728 | tf_op jit(solution)/shard_map/ppermute | solution.py:167
  2.0 3.7 %collective-permute-start = (bf16[144,256]{1,0:T(8,128)(2,1)S(1)}, bf16[144,256]{1,0:T(8,128)(2,1)S(1)}, u32[]{:S(2)}, u32[]{:S(2)}) collective-permute-start(bf16[144,256]{1,0:T(8,128)(2,1)S(1)} %get-tuple-element.23.refs_0_), channel_id=1, source_target_pairs={{0,4},{1,5},{2,6},{3,7},{4,0},{5,1},{6,2},{7,3},{8,12},{9,13},{10,... | collective-permute-start | bytes 221192 | tf_op jit(solution)/shard_map/ppermute | solution.py:170
  5.6 1.5 %collective-permute-start.6 = (bf16[1040,128]{1,0:T(8,128)(2,1)S(1)}, bf16[1040,128]{1,0:T(8,128)(2,1)S(1)}, u32[]{:S(2)}, u32[]{:S(2)}) collective-permute-start(bf16[1040,128]{1,0:T(8,128)(2,1)S(1)} %get-tuple-element.31), channel_id=1, source_target_pairs={{0,16},{8,24},{16,0},{24,8},{1,17},{9,25},{17,1},{25,9},{2,18},{10... | collective-permute-start | bytes 798728 | tf_op jit(solution)/shard_map/ppermute | solution.py:167
  7.1 0.0 collective-permute-start.7
  7.1 0.0 collective-permute-done.3.c_ref
  7.2 2.5 %collective-permute-start.4 = (bf16[144,256]{1,0:T(8,128)(2,1)S(1)}, bf16[144,256]{1,0:T(8,128)(2,1)S(1)}, u32[]{:S(2)}, u32[]{:S(2)}) collective-permute-start(bf16[144,256]{1,0:T(8,128)(2,1)S(1)} %get-tuple-element.23.refs_0_), channel_id=1, source_target_pairs={{0,3},{1,2},{2,1},{3,0},{4,7},{5,6},{6,5},{7,4},{8,11},{9,10},{10,... | collective-permute-start | bytes 221192 | tf_op jit(solution)/shard_map/ppermute | solution.py:170
  9.7 0.4 %collective-permute-done.refs_1_ = bf16[144,256]{1,0:T(8,128)(2,1)S(1)} collective-permute-done((bf16[144,256]{1,0:T(8,128)(2,1)S(1)}, bf16[144,256]{1,0:T(8,128)(2,1)S(1)}, u32[]{:S(2)}, u32[]{:S(2)}) %collective-permute-start) | collective-permute-done | bytes 73760 | tf_op jit(solution)/shard_map/ppermute | solution.py:170
  10.1 0.8 %collective-permute-start.2 = (bf16[288,256]{1,0:T(8,128)(2,1)S(1)}, bf16[288,256]{1,0:T(8,128)(2,1)S(1)}, u32[]{:S(2)}, u32[]{:S(2)}) collective-permute-start(bf16[288,256]{1,0:T(8,128)(2,1)S(1)} %shard_map.56.a_ref), channel_id=1, source_target_pairs={{0,2},{1,3},{2,0},{3,1},{4,6},{5,7},{6,4},{7,5},{8,10},{9,11},{10,... | collective-permute-start | bytes 442376 | tf_op jit(solution)/shard_map/ppermute | solution.py:170
  10.9 1.6 %collective-permute-start.1 = (bf16[288,256]{1,0:T(8,128)(2,1)S(1)}, bf16[288,256]{1,0:T(8,128)(2,1)S(1)}, u32[]{:S(2)}, u32[]{:S(2)}) collective-permute-start(bf16[288,256]{1,0:T(8,128)(2,1)S(1)} %shard_map.56.a_ref), channel_id=1, source_target_pairs={{0,1},{1,0},{2,3},{3,2},{4,5},{5,4},{6,7},{7,6},{8,9},{9,8},{10,11... | collective-permute-start | bytes 442376 | tf_op jit(solution)/shard_map/ppermute | solution.py:170
  12.5 0.4 %collective-permute-done.4 = bf16[144,256]{1,0:T(8,128)(2,1)S(1)} collective-permute-done((bf16[144,256]{1,0:T(8,128)(2,1)S(1)}, bf16[144,256]{1,0:T(8,128)(2,1)S(1)}, u32[]{:S(2)}, u32[]{:S(2)}) %collective-permute-start.4) | collective-permute-done | bytes 73760 | tf_op jit(solution)/shard_map/ppermute | solution.py:170
  12.8 2.8 %collective-permute-start.5 = (bf16[144,256]{1,0:T(8,128)(2,1)S(1)}, bf16[144,256]{1,0:T(8,128)(2,1)S(1)}, u32[]{:S(2)}, u32[]{:S(2)}) collective-permute-start(bf16[144,256]{1,0:T(8,128)(2,1)S(1)} %collective-permute-done.refs_1_), channel_id=1, source_target_pairs={{0,3},{1,2},{2,1},{3,0},{4,7},{5,6},{6,5},{7,4},{8,11},{9,10},{10,... | collective-permute-start | bytes 221192 | tf_op jit(solution)/shard_map/ppermute | solution.py:170
  15.6 0.0 collective-permute-done.6.refs_0_.refs_2_
  15.6 3.4 %collective-permute-done.7.refs_1_.refs_3_ = bf16[1040,128]{1,0:T(8,128)(2,1)S(1)} collective-permute-done((bf16[1040,128]{1,0:T(8,128)(2,1)S(1)}, bf16[1040,128]{1,0:T(8,128)(2,1)S(1)}, u32[]{:S(2)}, u32[]{:S(2)}) %collective-permute-start.7) | collective-permute-done | bytes 266272 | tf_op jit(solution)/shard_map/ppermute | solution.py:167
  19.0 0.0 collective-permute-done.5
  19.0 0.0 collective-permute-done.2.b_ref
  19.1 0.0 collective-permute-done.1.ya_ref
  19.1 0.9 %shard_map.57 = (f32[128,128]{1,0:T(8,128)S(1)}, bf16[4,128,256]{2,1,0:T(8,128)(2,1)S(1)}, bf16[4,128,256]{2,1,0:T(8,128)(2,1)S(1)}) custom-call(bf16[288,256]{1,0:T(8,128)(2,1)S(1)} %shard_map.56.a_ref, bf16[288,256]{1,0:T(8,128)(2,1)S(1)} %collective-permute-done.1.ya_ref, bf16[288,256]{1,0:T(8,128)(2,1)S(1)} %collective-permute-done.2.b_ref, ...), custom_call_target="tpu_custom_call" | custom-call | flops 2000000000 | tf_op jit(solution)/shard_map/pallas_call | solution.py:219
  20.0 0.3 %shard_map.59 = (f32[32,128]{1,0:T(8,128)S(1)}, f32[32,128]{1,0:T(8,128)S(1)}, f32[32,128]{1,0:T(8,128)S(1)}, f32[32,128]{1,0:T(8,128)S(1)}) custom-call(f32[128,128]{1,0:T(8,128)S(1)} %get-tuple-element.28.near_ref, bf16[4,128,256]{2,1,0:T(8,128)(2,1)S(1)} %get-tuple-element.29.refs_0_, bf16[4,128,256]{2,1,0:T(8,128)(2,1)S(1)} %get-tuple-element.30.refs_1_, ...), custom_call_target="tpu_custom_call" | custom-call | tf_op jit(solution)/shard_map/pallas_call | solution.py:241
  20.3 1.6 %collective-permute-start.8 = (f32[32,128]{1,0:T(8,128)S(1)}, f32[32,128]{1,0:T(8,128)S(1)}, u32[]{:S(2)}, u32[]{:S(2)}) collective-permute-start(f32[32,128]{1,0:T(8,128)S(1)} %get-tuple-element.34), channel_id=1, source_target_pairs={{0,16},{8,24},{16,0},{24,8},{1,17},{9,25},{17,1},{25,9},{2,18},{10... | collective-permute-start | bytes 49160 | tf_op jit(solution)/shard_map/ppermute | solution.py:167
  21.8 0.5 %collective-permute-start.9 = (f32[32,128]{1,0:T(8,128)S(1)}, f32[32,128]{1,0:T(8,128)S(1)}, u32[]{:S(2)}, u32[]{:S(2)}) collective-permute-start(f32[32,128]{1,0:T(8,128)S(1)} %get-tuple-element.35), channel_id=1, source_target_pairs={{0,24},{8,16},{16,8},{24,0},{1,25},{9,17},{17,9},{25,1},{2,26},{10... | collective-permute-start | bytes 49160 | tf_op jit(solution)/shard_map/ppermute | solution.py:167
  22.3 0.2 collective-permute-start.10
  22.5 1.6 %collective-permute-done.8 = f32[32,128]{1,0:T(8,128)S(1)} collective-permute-done((f32[32,128]{1,0:T(8,128)S(1)}, f32[32,128]{1,0:T(8,128)S(1)}, u32[]{:S(2)}, u32[]{:S(2)}) %collective-permute-start.8) | collective-permute-done | bytes 16416 | tf_op jit(solution)/shard_map/ppermute | solution.py:167
  24.1 0.9 %collective-permute-done.9 = f32[32,128]{1,0:T(8,128)S(1)} collective-permute-done((f32[32,128]{1,0:T(8,128)S(1)}, f32[32,128]{1,0:T(8,128)S(1)}, u32[]{:S(2)}, u32[]{:S(2)}) %collective-permute-start.9) | collective-permute-done | bytes 16416 | tf_op jit(solution)/shard_map/ppermute | solution.py:167
  25.0 0.0 collective-permute-done.10
  25.0 0.6 %add_add_fusion = f32[32,128]{1,0:T(8,128)} fusion(f32[32,128]{1,0:T(8,128)S(1)} %collective-permute-done.10, f32[32,128]{1,0:T(8,128)S(1)} %collective-permute-done.9, f32[32,128]{1,0:T(8,128)S(1)} %get-tuple-element.33, f32[32,128]{1,0:T(8,128)S(1)} %collective-permute-done.8), kind=kLoop, calls=%fused_computation.1 | loop fusion | flops 12288 | bytes 81920 | tf_op jit(solution)/shard_map/add | solution.py:251
  (3 shorter events, 0.0 us)
Async XLA Ops:
  1.4 5.7 %collective-permute-start.3 = (bf16[1040,128]{1,0:T(8,128)(2,1)S(1)}, bf16[1040,128]{1,0:T(8,128)(2,1)S(1)}, u32[]{:S(2)}, u32[]{:S(2)}) collective-permute-start(bf16[1040,128]{1,0:T(8,128)(2,1)S(1)} %get-tuple-element.22), channel_id=1, source_target_pairs={{0,8},{8,0},{16,24},{24,16},{1,9},{9,1},{17,25},{25,17},{2,10},{10... | collective-permute-start | bytes 798728 | tf_op jit(solution)/shard_map/ppermute | solution.py:167
  2.0 8.1 %collective-permute-start = (bf16[144,256]{1,0:T(8,128)(2,1)S(1)}, bf16[144,256]{1,0:T(8,128)(2,1)S(1)}, u32[]{:S(2)}, u32[]{:S(2)}) collective-permute-start(bf16[144,256]{1,0:T(8,128)(2,1)S(1)} %get-tuple-element.23.refs_0_), channel_id=1, source_target_pairs={{0,4},{1,5},{2,6},{3,7},{4,0},{5,1},{6,2},{7,3},{8,12},{9,13},{10,... | collective-permute-start | bytes 221192 | tf_op jit(solution)/shard_map/ppermute | solution.py:170
  5.6 10.0 %collective-permute-start.6 = (bf16[1040,128]{1,0:T(8,128)(2,1)S(1)}, bf16[1040,128]{1,0:T(8,128)(2,1)S(1)}, u32[]{:S(2)}, u32[]{:S(2)}) collective-permute-start(bf16[1040,128]{1,0:T(8,128)(2,1)S(1)} %get-tuple-element.31), channel_id=1, source_target_pairs={{0,16},{8,24},{16,0},{24,8},{1,17},{9,25},{17,1},{25,9},{2,18},{10... | collective-permute-start | bytes 798728 | tf_op jit(solution)/shard_map/ppermute | solution.py:167
  7.1 11.9 %collective-permute-start.7 = (bf16[1040,128]{1,0:T(8,128)(2,1)S(1)}, bf16[1040,128]{1,0:T(8,128)(2,1)S(1)}, u32[]{:S(2)}, u32[]{:S(2)}) collective-permute-start(bf16[1040,128]{1,0:T(8,128)(2,1)S(1)} %get-tuple-element.32), channel_id=1, source_target_pairs={{0,24},{8,16},{16,8},{24,0},{1,25},{9,17},{17,9},{25,1},{2,26},{10... | collective-permute-start | bytes 798728 | tf_op jit(solution)/shard_map/ppermute | solution.py:167
  7.2 5.7 %collective-permute-start.4 = (bf16[144,256]{1,0:T(8,128)(2,1)S(1)}, bf16[144,256]{1,0:T(8,128)(2,1)S(1)}, u32[]{:S(2)}, u32[]{:S(2)}) collective-permute-start(bf16[144,256]{1,0:T(8,128)(2,1)S(1)} %get-tuple-element.23.refs_0_), channel_id=1, source_target_pairs={{0,3},{1,2},{2,1},{3,0},{4,7},{5,6},{6,5},{7,4},{8,11},{9,10},{10,... | collective-permute-start | bytes 221192 | tf_op jit(solution)/shard_map/ppermute | solution.py:170
  10.1 9.0 %collective-permute-start.2 = (bf16[288,256]{1,0:T(8,128)(2,1)S(1)}, bf16[288,256]{1,0:T(8,128)(2,1)S(1)}, u32[]{:S(2)}, u32[]{:S(2)}) collective-permute-start(bf16[288,256]{1,0:T(8,128)(2,1)S(1)} %shard_map.56.a_ref), channel_id=1, source_target_pairs={{0,2},{1,3},{2,0},{3,1},{4,6},{5,7},{6,4},{7,5},{8,10},{9,11},{10,... | collective-permute-start | bytes 442376 | tf_op jit(solution)/shard_map/ppermute | solution.py:170
  10.9 8.2 %collective-permute-start.1 = (bf16[288,256]{1,0:T(8,128)(2,1)S(1)}, bf16[288,256]{1,0:T(8,128)(2,1)S(1)}, u32[]{:S(2)}, u32[]{:S(2)}) collective-permute-start(bf16[288,256]{1,0:T(8,128)(2,1)S(1)} %shard_map.56.a_ref), channel_id=1, source_target_pairs={{0,1},{1,0},{2,3},{3,2},{4,5},{5,4},{6,7},{7,6},{8,9},{9,8},{10,11... | collective-permute-start | bytes 442376 | tf_op jit(solution)/shard_map/ppermute | solution.py:170
  12.8 6.2 %collective-permute-start.5 = (bf16[144,256]{1,0:T(8,128)(2,1)S(1)}, bf16[144,256]{1,0:T(8,128)(2,1)S(1)}, u32[]{:S(2)}, u32[]{:S(2)}) collective-permute-start(bf16[144,256]{1,0:T(8,128)(2,1)S(1)} %collective-permute-done.refs_1_), channel_id=1, source_target_pairs={{0,3},{1,2},{2,1},{3,0},{4,7},{5,6},{6,5},{7,4},{8,11},{9,10},{10,... | collective-permute-start | bytes 221192 | tf_op jit(solution)/shard_map/ppermute | solution.py:170
  20.3 3.8 %collective-permute-start.8 = (f32[32,128]{1,0:T(8,128)S(1)}, f32[32,128]{1,0:T(8,128)S(1)}, u32[]{:S(2)}, u32[]{:S(2)}) collective-permute-start(f32[32,128]{1,0:T(8,128)S(1)} %get-tuple-element.34), channel_id=1, source_target_pairs={{0,16},{8,24},{16,0},{24,8},{1,17},{9,25},{17,1},{25,9},{2,18},{10... | collective-permute-start | bytes 49160 | tf_op jit(solution)/shard_map/ppermute | solution.py:167
  21.8 3.2 %collective-permute-start.9 = (f32[32,128]{1,0:T(8,128)S(1)}, f32[32,128]{1,0:T(8,128)S(1)}, u32[]{:S(2)}, u32[]{:S(2)}) collective-permute-start(f32[32,128]{1,0:T(8,128)S(1)} %get-tuple-element.35), channel_id=1, source_target_pairs={{0,24},{8,16},{16,8},{24,0},{1,25},{9,17},{17,9},{25,1},{2,26},{10... | collective-permute-start | bytes 49160 | tf_op jit(solution)/shard_map/ppermute | solution.py:167
  22.3 2.7 %collective-permute-start.10 = (f32[32,128]{1,0:T(8,128)S(1)}, f32[32,128]{1,0:T(8,128)S(1)}, u32[]{:S(2)}, u32[]{:S(2)}) collective-permute-start(f32[32,128]{1,0:T(8,128)S(1)} %get-tuple-element.36), channel_id=1, source_target_pairs={{0,8},{8,0},{16,24},{24,16},{1,9},{9,1},{17,25},{25,17},{2,10},{10... | collective-permute-start | bytes 49160 | tf_op jit(solution)/shard_map/ppermute | solution.py:167

commit v5 on v3

--- a/solution.py
+++ b/solution.py
@@ -69,9 +69,22 @@
         copy.wait()
 
 
+def late_kernel(*refs):
+    for i, ref in enumerate(refs[:-1]):
+        tail = ref[ref.shape[0] - EXTRA :, :].astype(jnp.float32)[0:8]
+        refs[-1][8 * i : 8 * i + 8] = tail.astype(jnp.int32)
+
+
+def join_kernel(*refs):
+    at = 0
+    for ref in refs[:-1]:
+        refs[-1][at : at + ref.shape[0]] = ref[...]
+        at += ref.shape[0]
+
+
 def part_kernel(n_panel, n_obs, cap, quads, which, last, *refs):
     buffers, pieces = dict(zip(which, refs)), refs[len(which) : len(which) + n_panel]
-    rest, acc_ref = refs[len(which) + n_panel : -1], refs[-1]
+    late_ref, rest, acc_ref = refs[len(which) + n_panel], refs[len(which) + n_panel + 1 : -1], refs[-1]
     count = n_panel * n_obs
     me_p = lax.axis_index("panel")
     me_o = lax.axis_index("obs")
@@ -99,7 +112,7 @@
         groups.append(dot(pick, jnp.concatenate(values, axis=0)).astype(jnp.bfloat16))
         starts.append(((me_o // per) ^ quad) * 16)
     for k in range(n_panel):
-        delays = pieces[k][2 * depth : 2 * depth + EXTRA, :].astype(jnp.float32)[0:1].astype(jnp.int32)
+        delays = late_ref[8 * k : 8 * k + 8][0:1]
         for b in range(n_obs // 2):
             row = 32 * (k * (n_obs // 2) + b)
             source = jnp.concatenate(
@@ -172,12 +185,32 @@
         )
     )
     from_x, from_xc, from_c = along_panel(to_x, 2), along_panel(to_xc, 3), along_panel(to_c, 1)
-    a = jnp.concatenate([message] + [along_obs(message, k) for k in range(4, n_obs, 4)], axis=0)
-    a, from_c = lax.optimization_barrier((a, from_c))
-    b, ya, yb = along_obs(a, 2), along_obs(a, 1), along_obs(a, 3)
+    ranges = range(4, n_obs, 4)
+    far = [along_obs(message, k) for k in ranges]
+    later, from_c = lax.optimization_barrier((message, from_c))
+    near = along_obs(later, 3)
+    a = pl.pallas_call(
+        join_kernel,
+        out_shape=jax.ShapeDtypeStruct((n_obs // 4 * (rows + EXTRA), 2 * steps), jnp.bfloat16),
+        in_specs=[vmem] * (n_obs // 4),
+        out_specs=vmem,
+        compiler_params=params,
+        cost_estimate=pl.CostEstimate(flops=4*10**9, bytes_accessed=0, transcendentals=0),
+    )(message, *far)
+    ya, b = along_obs(a, 1), along_obs(a, 2)
+    again, near = lax.optimization_barrier((jnp.concatenate(far, axis=0), near))
+    yb = jnp.concatenate([near, along_obs(again, 3)], axis=0)
 
     buffers, pieces = (a, ya, b, yb), (own, from_c, from_x, from_xc)
     per = 16 // cap
+    late = pl.pallas_call(
+        late_kernel,
+        out_shape=jax.ShapeDtypeStruct((8 * n_panel, observers), jnp.int32),
+        in_specs=[vmem] * n_panel,
+        out_specs=vmem,
+        compiler_params=params,
+        cost_estimate=pl.CostEstimate(flops=2*10**9, bytes_accessed=0, transcendentals=0),
+    )(*pieces)
     share = jax.ShapeDtypeStruct((steps // n_panel, observers), jnp.float32)
     shares = []
     for last in (False, True):
@@ -186,13 +219,13 @@
         shares = pl.pallas_call(
             functools.partial(part_kernel, n_panel, n_obs, cap, quads, which, last),
             out_shape=[share] * n_panel if last else [jax.ShapeDtypeStruct((steps, observers), jnp.float32)],
-            in_specs=[vmem] * (len(which) + n_panel + last),
+            in_specs=[vmem] * (len(which) + n_panel + 1 + last),
             out_specs=[vmem] * (n_panel if last else 1),
             scratch_shapes=[pltpu.VMEM((2 * steps, observers), jnp.float32)],
             compiler_params=params,
-        )(*(buffers[w] for w in which), *pieces, *shares)
+        )(*(buffers[w] for w in which), *pieces, late, *shares)
     total = shares[0]
-    for k in (2, 3, 1):
+    for k in (3, 1, 2):
         total = total + along_panel(shares[k], k)
     return total
 

time: 26.1 us -> 25.7 us (0.985)
  waiting for transfers between devices: 11.2 us -> 6.83 us
  starting transfers between devices: 11.5 us -> 15.4 us
    ppermute x4 -> x5, starting transfers between devices: 7.22 us -> 11.2 us  [along_obs(): return lax.ppermute(value, 'obs', [(i, i ^ k) for i in range(n_obs)])]
    ppermute x4 -> x5, waiting for transfers between devices: 3.39 us -> 0.77 us  [along_obs(): return lax.ppermute(value, 'obs', [(i, i ^ k) for i in range(n_obs)])]
    ppermute x6, waiting for transfers between devices: 7.77 us -> 6.07 us  [along_panel(): return lax.ppermute(value, 'panel', [(i, i ^ k) for i in range(n_panel)])]
  transfers between devices with their start and end apart: 10 -> 11, of which waited for: 6 -> 5; matrix products, arithmetic and copies ran while one was open for 0% -> 0% of each run, Pallas kernels for 2% -> 2%
where the time goes in v5:
time: 25.7 us; the launch traced here: 25.6 us
  starting transfers between devices  15.4 us (60%)
  waiting for transfers between devices  6.83 us (27%)
  Pallas kernels  2.63 us (10%)
  other arithmetic  0.62 us (2%)
    ppermute x5, starting transfers between devices, along_obs(): return lax.ppermute(value, 'obs', [(i, i ^ k) for i in range(n_obs)])  11.2 us
    ppermute x6, waiting for transfers between devices, along_panel(): return lax.ppermute(value, 'panel', [(i, i ^ k) for i in range(n_panel)])  6.07 us
    ppermute x6, starting transfers between devices, along_panel(): return lax.ppermute(value, 'panel', [(i, i ^ k) for i in range(n_panel)])  4.26 us
    pallas_call x1, Pallas kernels, per_device(): pl.pallas_call(functools.partial(pack_kernel, n_panel, n_obs, cap), out_s...  1.43 us
    pallas_call x2, Pallas kernels, per_device(): pl.pallas_call(functools.partial(part_kernel, n_panel, n_obs, cap, quads,...  1.18 us
    ppermute x5, waiting for transfers between devices, along_obs(): return lax.ppermute(value, 'obs', [(i, i ^ k) for i in range(n_obs)])  0.77 us
    add x1, other arithmetic, per_device(): total = total + along_panel(shares[k], k)  0.61 us
  transfers between devices with their start and end apart: 11, of which 5 were waited for; matrix products, arithmetic and copies ran while one was open for 0% of the time, Pallas kernels for 2%

profile of v5, /device:TPU:0, one launch (start us, length us, event | category | flops | bytes accessed | tf_op | source)
XLA Modules:
  0.0 25.6 jit_solution(2775939722403957925)
XLA Ops:
  0.0 1.4 %shard_map.55 = (bf16[144,256]{1,0:T(8,128)(2,1)S(1)}, bf16[1040,128]{1,0:T(8,128)(2,1)S(1)}, bf16[1040,128]{1,0:T(8,128)(2,1)S(1)}, bf16[1040,128]{1,0:T(8,128)(2,1)S(1)}, bf16[1040,128]{1,0:T(8,128)(2,1)S(1)}) custom-call(bf16[256,128]{1,0:T(8,128)(2,1)} %bitcast.7, s32[1,128]{1,0:T(1,128)} %bitcast.8, s32[1,4]{1,0:T(1,128)} %bitcast.9, ...), custom_call_target="tpu_custom_call" | custom-call | tf_op jit(solution)/shard_map/pallas_call | solution.py:162
  1.4 0.5 %collective-permute-start.2 = (bf16[1040,128]{1,0:T(8,128)(2,1)S(1)}, bf16[1040,128]{1,0:T(8,128)(2,1)S(1)}, u32[]{:S(2)}, u32[]{:S(2)}) collective-permute-start(bf16[1040,128]{1,0:T(8,128)(2,1)S(1)} %get-tuple-element.19), channel_id=1, source_target_pairs={{0,8},{8,0},{16,24},{24,16},{1,9},{9,1},{17,25},{25,17},{2,10},{10... | collective-permute-start | bytes 798728 | tf_op jit(solution)/shard_map/ppermute | solution.py:154
  2.0 3.7 %collective-permute-start = (bf16[144,256]{1,0:T(8,128)(2,1)S(1)}, bf16[144,256]{1,0:T(8,128)(2,1)S(1)}, u32[]{:S(2)}, u32[]{:S(2)}) collective-permute-start(bf16[144,256]{1,0:T(8,128)(2,1)S(1)} %get-tuple-element.20.refs_0_), channel_id=1, source_target_pairs={{0,4},{1,5},{2,6},{3,7},{4,0},{5,1},{6,2},{7,3},{8,12},{9,13},{10,... | collective-permute-start | bytes 221192 | tf_op jit(solution)/shard_map/ppermute | solution.py:157
  5.6 1.5 %collective-permute-start.5 = (bf16[1040,128]{1,0:T(8,128)(2,1)S(1)}, bf16[1040,128]{1,0:T(8,128)(2,1)S(1)}, u32[]{:S(2)}, u32[]{:S(2)}) collective-permute-start(bf16[1040,128]{1,0:T(8,128)(2,1)S(1)} %get-tuple-element.25), channel_id=1, source_target_pairs={{0,16},{8,24},{16,0},{24,8},{1,17},{9,25},{17,1},{25,9},{2,18},{10... | collective-permute-start | bytes 798728 | tf_op jit(solution)/shard_map/ppermute | solution.py:154
  7.1 0.0 collective-permute-start.6
  7.1 0.0 collective-permute-done.2.refs_1_.refs_3_
  7.2 2.5 %collective-permute-start.3 = (bf16[144,256]{1,0:T(8,128)(2,1)S(1)}, bf16[144,256]{1,0:T(8,128)(2,1)S(1)}, u32[]{:S(2)}, u32[]{:S(2)}) collective-permute-start(bf16[144,256]{1,0:T(8,128)(2,1)S(1)} %get-tuple-element.20.refs_0_), channel_id=1, source_target_pairs={{0,3},{1,2},{2,1},{3,0},{4,7},{5,6},{6,5},{7,4},{8,11},{9,10},{10,... | collective-permute-start | bytes 221192 | tf_op jit(solution)/shard_map/ppermute | solution.py:157
  9.7 0.4 %collective-permute-done.refs_1_ = bf16[144,256]{1,0:T(8,128)(2,1)S(1)} collective-permute-done((bf16[144,256]{1,0:T(8,128)(2,1)S(1)}, bf16[144,256]{1,0:T(8,128)(2,1)S(1)}, u32[]{:S(2)}, u32[]{:S(2)}) %collective-permute-start) | collective-permute-done | bytes 73760 | tf_op jit(solution)/shard_map/ppermute | solution.py:157
  10.1 1.7 %collective-permute-start.7 = (bf16[288,256]{1,0:T(8,128)(2,1)S(1)}, bf16[288,256]{1,0:T(8,128)(2,1)S(1)}, u32[]{:S(2)}, u32[]{:S(2)}) collective-permute-start(bf16[288,256]{1,0:T(8,128)(2,1)S(1)} %shard_map.56.refs_0_), channel_id=1, source_target_pairs={{0,1},{1,0},{2,3},{3,2},{4,5},{5,4},{6,7},{7,6},{8,9},{9,8},{10,11... | collective-permute-start | bytes 442376 | tf_op jit(solution)/shard_map/ppermute | solution.py:157
  11.7 0.7 %collective-permute-start.1 = (bf16[288,256]{1,0:T(8,128)(2,1)S(1)}, bf16[288,256]{1,0:T(8,128)(2,1)S(1)}, u32[]{:S(2)}, u32[]{:S(2)}) collective-permute-start(bf16[288,256]{1,0:T(8,128)(2,1)S(1)} %shard_map.56.refs_0_), channel_id=1, source_target_pairs={{0,2},{1,3},{2,0},{3,1},{4,6},{5,7},{6,4},{7,5},{8,10},{9,11},{10,... | collective-permute-start | bytes 442376 | tf_op jit(solution)/shard_map/ppermute | solution.py:157
  12.5 0.4 %collective-permute-done.3 = bf16[144,256]{1,0:T(8,128)(2,1)S(1)} collective-permute-done((bf16[144,256]{1,0:T(8,128)(2,1)S(1)}, bf16[144,256]{1,0:T(8,128)(2,1)S(1)}, u32[]{:S(2)}, u32[]{:S(2)}) %collective-permute-start.3) | collective-permute-done | bytes 73760 | tf_op jit(solution)/shard_map/ppermute | solution.py:157
  12.8 2.6 %collective-permute-start.4 = (bf16[144,256]{1,0:T(8,128)(2,1)S(1)}, bf16[144,256]{1,0:T(8,128)(2,1)S(1)}, u32[]{:S(2)}, u32[]{:S(2)}) collective-permute-start(bf16[144,256]{1,0:T(8,128)(2,1)S(1)} %collective-permute-done.refs_1_), channel_id=1, source_target_pairs={{0,3},{1,2},{2,1},{3,0},{4,7},{5,6},{6,5},{7,4},{8,11},{9,10},{10,... | collective-permute-start | bytes 221192 | tf_op jit(solution)/shard_map/ppermute | solution.py:157
  15.5 0.0 collective-permute-done.5.refs_2_.refs_4_
  15.5 3.5 %collective-permute-done.6.refs_3_.refs_5_ = bf16[1040,128]{1,0:T(8,128)(2,1)S(1)} collective-permute-done((bf16[1040,128]{1,0:T(8,128)(2,1)S(1)}, bf16[1040,128]{1,0:T(8,128)(2,1)S(1)}, u32[]{:S(2)}, u32[]{:S(2)}) %collective-permute-start.6) | collective-permute-done | bytes 266272 | tf_op jit(solution)/shard_map/ppermute | solution.py:154
  19.0 0.0 collective-permute-done.7.refs_1_
  19.0 0.6 %shard_map.58.refs_7_ = f32[128,128]{1,0:T(8,128)S(1)} custom-call(bf16[288,256]{1,0:T(8,128)(2,1)S(1)} %shard_map.56.refs_0_, bf16[288,256]{1,0:T(8,128)(2,1)S(1)} %collective-permute-done.7.refs_1_, bf16[1040,128]{1,0:T(8,128)(2,1)S(1)} %get-tuple-element.23.refs_0_.refs_2_, bf16[1040,128]{1,0:T(8,128)(2,1)S(1)} %collective-permute-done.2.refs_1_.refs_3_, ...), custom_call_target="tpu_custom_call" | custom-call | tf_op jit(solution)/shard_map/pallas_call | solution.py:219
  19.6 0.0 collective-permute-done.4
  19.6 0.0 collective-permute-done.1.refs_0_
  19.7 0.6 %shard_map.59 = (f32[32,128]{1,0:T(8,128)S(1)}, f32[32,128]{1,0:T(8,128)S(1)}, f32[32,128]{1,0:T(8,128)S(1)}, f32[32,128]{1,0:T(8,128)S(1)}) custom-call(bf16[288,256]{1,0:T(8,128)(2,1)S(1)} %collective-permute-done.1.refs_0_, bf16[288,256]{1,0:T(8,128)(2,1)S(1)} %pad_maximum_fusion.refs_1_, bf16[1040,128]{1,0:T(8,128)(2,1)S(1)} %get-tuple-element.23.refs_0_.refs_2_, ...), custom_call_target="tpu_custom_call" | custom-call | tf_op jit(solution)/shard_map/pallas_call | solution.py:219
  20.3 1.6 %collective-permute-start.10 = (f32[32,128]{1,0:T(8,128)S(1)}, f32[32,128]{1,0:T(8,128)S(1)}, u32[]{:S(2)}, u32[]{:S(2)}) collective-permute-start(f32[32,128]{1,0:T(8,128)S(1)} %get-tuple-element.30), channel_id=1, source_target_pairs={{0,16},{8,24},{16,0},{24,8},{1,17},{9,25},{17,1},{25,9},{2,18},{10... | collective-permute-start | bytes 49160 | tf_op jit(solution)/shard_map/ppermute | solution.py:154
  21.8 0.5 %collective-permute-start.8 = (f32[32,128]{1,0:T(8,128)S(1)}, f32[32,128]{1,0:T(8,128)S(1)}, u32[]{:S(2)}, u32[]{:S(2)}) collective-permute-start(f32[32,128]{1,0:T(8,128)S(1)} %get-tuple-element.28), channel_id=1, source_target_pairs={{0,24},{8,16},{16,8},{24,0},{1,25},{9,17},{17,9},{25,1},{2,26},{10... | collective-permute-start | bytes 49160 | tf_op jit(solution)/shard_map/ppermute | solution.py:154
  22.3 0.2 collective-permute-start.9
  22.5 1.6 %collective-permute-done.10 = f32[32,128]{1,0:T(8,128)S(1)} collective-permute-done((f32[32,128]{1,0:T(8,128)S(1)}, f32[32,128]{1,0:T(8,128)S(1)}, u32[]{:S(2)}, u32[]{:S(2)}) %collective-permute-start.10) | collective-permute-done | bytes 16416 | tf_op jit(solution)/shard_map/ppermute | solution.py:154
  24.1 0.9 %collective-permute-done.8 = f32[32,128]{1,0:T(8,128)S(1)} collective-permute-done((f32[32,128]{1,0:T(8,128)S(1)}, f32[32,128]{1,0:T(8,128)S(1)}, u32[]{:S(2)}, u32[]{:S(2)}) %collective-permute-start.8) | collective-permute-done | bytes 16416 | tf_op jit(solution)/shard_map/ppermute | solution.py:154
  25.0 0.0 collective-permute-done.9
  25.0 0.6 %add_add_fusion = f32[32,128]{1,0:T(8,128)} fusion(f32[32,128]{1,0:T(8,128)S(1)} %collective-permute-done.10, f32[32,128]{1,0:T(8,128)S(1)} %collective-permute-done.9, f32[32,128]{1,0:T(8,128)S(1)} %get-tuple-element.27, f32[32,128]{1,0:T(8,128)S(1)} %collective-permute-done.8), kind=kLoop, calls=%fused_computation.1 | loop fusion | flops 12288 | bytes 81920 | tf_op jit(solution)/shard_map/add | solution.py:229
  (3 shorter events, 0.0 us)
Async XLA Ops:
  1.4 5.7 %collective-permute-start.2 = (bf16[1040,128]{1,0:T(8,128)(2,1)S(1)}, bf16[1040,128]{1,0:T(8,128)(2,1)S(1)}, u32[]{:S(2)}, u32[]{:S(2)}) collective-permute-start(bf16[1040,128]{1,0:T(8,128)(2,1)S(1)} %get-tuple-element.19), channel_id=1, source_target_pairs={{0,8},{8,0},{16,24},{24,16},{1,9},{9,1},{17,25},{25,17},{2,10},{10... | collective-permute-start | bytes 798728 | tf_op jit(solution)/shard_map/ppermute | solution.py:154
  2.0 8.1 %collective-permute-start = (bf16[144,256]{1,0:T(8,128)(2,1)S(1)}, bf16[144,256]{1,0:T(8,128)(2,1)S(1)}, u32[]{:S(2)}, u32[]{:S(2)}) collective-permute-start(bf16[144,256]{1,0:T(8,128)(2,1)S(1)} %get-tuple-element.20.refs_0_), channel_id=1, source_target_pairs={{0,4},{1,5},{2,6},{3,7},{4,0},{5,1},{6,2},{7,3},{8,12},{9,13},{10,... | collective-permute-start | bytes 221192 | tf_op jit(solution)/shard_map/ppermute | solution.py:157
  5.6 9.8 %collective-permute-start.5 = (bf16[1040,128]{1,0:T(8,128)(2,1)S(1)}, bf16[1040,128]{1,0:T(8,128)(2,1)S(1)}, u32[]{:S(2)}, u32[]{:S(2)}) collective-permute-start(bf16[1040,128]{1,0:T(8,128)(2,1)S(1)} %get-tuple-element.25), channel_id=1, source_target_pairs={{0,16},{8,24},{16,0},{24,8},{1,17},{9,25},{17,1},{25,9},{2,18},{10... | collective-permute-start | bytes 798728 | tf_op jit(solution)/shard_map/ppermute | solution.py:154
  7.1 11.9 %collective-permute-start.6 = (bf16[1040,128]{1,0:T(8,128)(2,1)S(1)}, bf16[1040,128]{1,0:T(8,128)(2,1)S(1)}, u32[]{:S(2)}, u32[]{:S(2)}) collective-permute-start(bf16[1040,128]{1,0:T(8,128)(2,1)S(1)} %get-tuple-element.26), channel_id=1, source_target_pairs={{0,24},{8,16},{16,8},{24,0},{1,25},{9,17},{17,9},{25,1},{2,26},{10... | collective-permute-start | bytes 798728 | tf_op jit(solution)/shard_map/ppermute | solution.py:154
  7.2 5.7 %collective-permute-start.3 = (bf16[144,256]{1,0:T(8,128)(2,1)S(1)}, bf16[144,256]{1,0:T(8,128)(2,1)S(1)}, u32[]{:S(2)}, u32[]{:S(2)}) collective-permute-start(bf16[144,256]{1,0:T(8,128)(2,1)S(1)} %get-tuple-element.20.refs_0_), channel_id=1, source_target_pairs={{0,3},{1,2},{2,1},{3,0},{4,7},{5,6},{6,5},{7,4},{8,11},{9,10},{10,... | collective-permute-start | bytes 221192 | tf_op jit(solution)/shard_map/ppermute | solution.py:157
  10.1 8.9 %collective-permute-start.7 = (bf16[288,256]{1,0:T(8,128)(2,1)S(1)}, bf16[288,256]{1,0:T(8,128)(2,1)S(1)}, u32[]{:S(2)}, u32[]{:S(2)}) collective-permute-start(bf16[288,256]{1,0:T(8,128)(2,1)S(1)} %shard_map.56.refs_0_), channel_id=1, source_target_pairs={{0,1},{1,0},{2,3},{3,2},{4,5},{5,4},{6,7},{7,6},{8,9},{9,8},{10,11... | collective-permute-start | bytes 442376 | tf_op jit(solution)/shard_map/ppermute | solution.py:157
  11.7 7.9 %collective-permute-start.1 = (bf16[288,256]{1,0:T(8,128)(2,1)S(1)}, bf16[288,256]{1,0:T(8,128)(2,1)S(1)}, u32[]{:S(2)}, u32[]{:S(2)}) collective-permute-start(bf16[288,256]{1,0:T(8,128)(2,1)S(1)} %shard_map.56.refs_0_), channel_id=1, source_target_pairs={{0,2},{1,3},{2,0},{3,1},{4,6},{5,7},{6,4},{7,5},{8,10},{9,11},{10,... | collective-permute-start | bytes 442376 | tf_op jit(solution)/shard_map/ppermute | solution.py:157
  12.8 6.8 %collective-permute-start.4 = (bf16[144,256]{1,0:T(8,128)(2,1)S(1)}, bf16[144,256]{1,0:T(8,128)(2,1)S(1)}, u32[]{:S(2)}, u32[]{:S(2)}) collective-permute-start(bf16[144,256]{1,0:T(8,128)(2,1)S(1)} %collective-permute-done.refs_1_), channel_id=1, source_target_pairs={{0,3},{1,2},{2,1},{3,0},{4,7},{5,6},{6,5},{7,4},{8,11},{9,10},{10,... | collective-permute-start | bytes 221192 | tf_op jit(solution)/shard_map/ppermute | solution.py:157
  20.3 3.8 %collective-permute-start.10 = (f32[32,128]{1,0:T(8,128)S(1)}, f32[32,128]{1,0:T(8,128)S(1)}, u32[]{:S(2)}, u32[]{:S(2)}) collective-permute-start(f32[32,128]{1,0:T(8,128)S(1)} %get-tuple-element.30), channel_id=1, source_target_pairs={{0,16},{8,24},{16,0},{24,8},{1,17},{9,25},{17,1},{25,9},{2,18},{10... | collective-permute-start | bytes 49160 | tf_op jit(solution)/shard_map/ppermute | solution.py:154
  21.8 3.2 %collective-permute-start.8 = (f32[32,128]{1,0:T(8,128)S(1)}, f32[32,128]{1,0:T(8,128)S(1)}, u32[]{:S(2)}, u32[]{:S(2)}) collective-permute-start(f32[32,128]{1,0:T(8,128)S(1)} %get-tuple-element.28), channel_id=1, source_target_pairs={{0,24},{8,16},{16,8},{24,0},{1,25},{9,17},{17,9},{25,1},{2,26},{10... | collective-permute-start | bytes 49160 | tf_op jit(solution)/shard_map/ppermute | solution.py:154
  22.3 2.7 %collective-permute-start.9 = (f32[32,128]{1,0:T(8,128)S(1)}, f32[32,128]{1,0:T(8,128)S(1)}, u32[]{:S(2)}, u32[]{:S(2)}) collective-permute-start(f32[32,128]{1,0:T(8,128)S(1)} %get-tuple-element.29), channel_id=1, source_target_pairs={{0,8},{8,0},{16,24},{24,16},{1,9},{9,1},{17,25},{25,17},{2,10},{10... | collective-permute-start | bytes 49160 | tf_op jit(solution)/shard_map/ppermute | solution.py:154

commit v6 on v5

--- a/solution.py
+++ b/solution.py
@@ -82,9 +82,9 @@
         at += ref.shape[0]
 
 
-def part_kernel(n_panel, n_obs, cap, quads, which, last, *refs):
-    buffers, pieces = dict(zip(which, refs)), refs[len(which) : len(which) + n_panel]
-    late_ref, rest, acc_ref = refs[len(which) + n_panel], refs[len(which) + n_panel + 1 : -1], refs[-1]
+def part_kernel(n_panel, n_obs, cap, *refs):
+    buffers, pieces, late_ref = refs[:4], refs[4 : 4 + n_panel], refs[4 + n_panel]
+    outs, acc_ref = refs[5 + n_panel : -1], refs[-1]
     count = n_panel * n_obs
     me_p = lax.axis_index("panel")
     me_o = lax.axis_index("obs")
@@ -94,11 +94,9 @@
     width = n_obs * cap
     depth = n_obs * width
     acc_ref[...] = jnp.zeros_like(acc_ref)
-    if last:
-        acc_ref[0:steps] = rest[0][...]
     slot_ids = lax.broadcasted_iota(jnp.int32, (count * 16, per * rows), 0)
     groups, starts = [], []
-    for quad in quads:
+    for quad in range(n_obs // per):
         values, places = [], []
         for i in range(per):
             j = quad * per + i
@@ -128,13 +126,10 @@
                 axis=0,
             )
             acc_ref[pl.ds(delays[0, b], steps), :] += dot(source.T, weights)
-    if not last:
-        rest[0][...] = acc_ref[0:steps]
-        return
     share = steps // n_panel
     for k in range(n_panel):
         start = pl.multiple_of((me_p ^ k) * share, share)
-        rest[1 + k][...] = acc_ref[pl.ds(start, share), :]
+        outs[k][...] = acc_ref[pl.ds(start, share), :]
 
 
 def per_device(les_rows, les_dest, loading_weight, thickness_weight, delays):
@@ -202,7 +197,6 @@
     yb = jnp.concatenate([near, along_obs(again, 3)], axis=0)
 
     buffers, pieces = (a, ya, b, yb), (own, from_c, from_x, from_xc)
-    per = 16 // cap
     late = pl.pallas_call(
         late_kernel,
         out_shape=jax.ShapeDtypeStruct((8 * n_panel, observers), jnp.int32),
@@ -212,18 +206,15 @@
         cost_estimate=pl.CostEstimate(flops=2*10**9, bytes_accessed=0, transcendentals=0),
     )(*pieces)
     share = jax.ShapeDtypeStruct((steps // n_panel, observers), jnp.float32)
-    shares = []
-    for last in (False, True):
-        quads = [q for q in range(n_obs // per) if q % 2 == last]
-        which = sorted({j % 4 for q in quads for j in range(q * per, (q + 1) * per)})
-        shares = pl.pallas_call(
-            functools.partial(part_kernel, n_panel, n_obs, cap, quads, which, last),
-            out_shape=[share] * n_panel if last else [jax.ShapeDtypeStruct((steps, observers), jnp.float32)],
-            in_specs=[vmem] * (len(which) + n_panel + 1 + last),
-            out_specs=[vmem] * (n_panel if last else 1),
-            scratch_shapes=[pltpu.VMEM((2 * steps, observers), jnp.float32)],
-            compiler_params=params,
-        )(*(buffers[w] for w in which), *pieces, late, *shares)
+    shares = pl.pallas_call(
+        functools.partial(part_kernel, n_panel, n_obs, cap),
+        out_shape=[share] * n_panel,
+        in_specs=[vmem] * (5 + n_panel),
+        out_specs=[vmem] * n_panel,
+        scratch_shapes=[pltpu.VMEM((2 * steps, observers), jnp.float32)],
+        compiler_params=params,
+        cost_estimate=pl.CostEstimate(flops=1, bytes_accessed=0, transcendentals=0),
+    )(*buffers, *pieces, late)
     total = shares[0]
     for k in (3, 1, 2):
         total = total + along_panel(shares[k], k)

time: 25.7 us -> 25.4 us (0.988)
  Pallas kernels: 2.63 us -> 2.33 us
    pallas_call x2 -> x1, Pallas kernels: 1.18 us -> 0.89 us  [per_device(): pl.pallas_call(functools.partial(part_kernel, n_panel, n_obs, cap), out_s...]
  transfers between devices with their start and end apart: 11 -> 11, of which waited for: 5 -> 5; matrix products, arithmetic and copies ran while one was open for 0% -> 0% of each run, Pallas kernels for 2% -> 0%
where the time goes in v6:
time: 25.4 us; the launch traced here: 25.3 us
  starting transfers between devices  15.4 us (61%)
  waiting for transfers between devices  6.83 us (27%)
  Pallas kernels  2.33 us (9%)
  other arithmetic  0.62 us (2%)
    ppermute x5, starting transfers between devices, along_obs(): return lax.ppermute(value, 'obs', [(i, i ^ k) for i in range(n_obs)])  11.2 us
    ppermute x6, waiting for transfers between devices, along_panel(): return lax.ppermute(value, 'panel', [(i, i ^ k) for i in range(n_panel)])  6.06 us
    ppermute x6, starting transfers between devices, along_panel(): return lax.ppermute(value, 'panel', [(i, i ^ k) for i in range(n_panel)])  4.26 us
    pallas_call x1, Pallas kernels, per_device(): pl.pallas_call(functools.partial(pack_kernel, n_panel, n_obs, cap), out_s...  1.43 us
    pallas_call x1, Pallas kernels, per_device(): pl.pallas_call(functools.partial(part_kernel, n_panel, n_obs, cap), out_s...  0.89 us
    ppermute x5, waiting for transfers between devices, along_obs(): return lax.ppermute(value, 'obs', [(i, i ^ k) for i in range(n_obs)])  0.77 us
    add x1, other arithmetic, per_device(): total = total + along_panel(shares[k], k)  0.61 us
  transfers between devices with their start and end apart: 11, of which 5 were waited for; matrix products, arithmetic and copies ran while one was open for 0% of the time, Pallas kernels for 0%

profile of v6, /device:TPU:0, one launch (start us, length us, event | category | flops | bytes accessed | tf_op | source)
XLA Modules:
  0.0 25.3 jit_solution(8547227014931118911)
XLA Ops:
  0.0 1.4 %shard_map.55 = (bf16[144,256]{1,0:T(8,128)(2,1)S(1)}, bf16[1040,128]{1,0:T(8,128)(2,1)S(1)}, bf16[1040,128]{1,0:T(8,128)(2,1)S(1)}, bf16[1040,128]{1,0:T(8,128)(2,1)S(1)}, bf16[1040,128]{1,0:T(8,128)(2,1)S(1)}) custom-call(bf16[256,128]{1,0:T(8,128)(2,1)} %bitcast.7, s32[1,128]{1,0:T(1,128)} %bitcast.8, s32[1,4]{1,0:T(1,128)} %bitcast.9, ...), custom_call_target="tpu_custom_call" | custom-call | tf_op jit(solution)/shard_map/pallas_call | solution.py:157
  1.4 0.5 %collective-permute-start.3 = (bf16[1040,128]{1,0:T(8,128)(2,1)S(1)}, bf16[1040,128]{1,0:T(8,128)(2,1)S(1)}, u32[]{:S(2)}, u32[]{:S(2)}) collective-permute-start(bf16[1040,128]{1,0:T(8,128)(2,1)S(1)} %get-tuple-element.19), channel_id=1, source_target_pairs={{0,8},{8,0},{16,24},{24,16},{1,9},{9,1},{17,25},{25,17},{2,10},{10... | collective-permute-start | bytes 798728 | tf_op jit(solution)/shard_map/ppermute | solution.py:149
  2.0 3.7 %collective-permute-start = (bf16[144,256]{1,0:T(8,128)(2,1)S(1)}, bf16[144,256]{1,0:T(8,128)(2,1)S(1)}, u32[]{:S(2)}, u32[]{:S(2)}) collective-permute-start(bf16[144,256]{1,0:T(8,128)(2,1)S(1)} %get-tuple-element.20.refs_0_), channel_id=1, source_target_pairs={{0,4},{1,5},{2,6},{3,7},{4,0},{5,1},{6,2},{7,3},{8,12},{9,13},{10,... | collective-permute-start | bytes 221192 | tf_op jit(solution)/shard_map/ppermute | solution.py:152
  5.6 1.5 %collective-permute-start.6 = (bf16[1040,128]{1,0:T(8,128)(2,1)S(1)}, bf16[1040,128]{1,0:T(8,128)(2,1)S(1)}, u32[]{:S(2)}, u32[]{:S(2)}) collective-permute-start(bf16[1040,128]{1,0:T(8,128)(2,1)S(1)} %get-tuple-element.25), channel_id=1, source_target_pairs={{0,16},{8,24},{16,0},{24,8},{1,17},{9,25},{17,1},{25,9},{2,18},{10... | collective-permute-start | bytes 798728 | tf_op jit(solution)/shard_map/ppermute | solution.py:149
  7.1 0.0 collective-permute-start.7
  7.1 0.0 collective-permute-done.3.refs_1_.refs_5_
  7.2 2.5 %collective-permute-start.4 = (bf16[144,256]{1,0:T(8,128)(2,1)S(1)}, bf16[144,256]{1,0:T(8,128)(2,1)S(1)}, u32[]{:S(2)}, u32[]{:S(2)}) collective-permute-start(bf16[144,256]{1,0:T(8,128)(2,1)S(1)} %get-tuple-element.20.refs_0_), channel_id=1, source_target_pairs={{0,3},{1,2},{2,1},{3,0},{4,7},{5,6},{6,5},{7,4},{8,11},{9,10},{10,... | collective-permute-start | bytes 221192 | tf_op jit(solution)/shard_map/ppermute | solution.py:152
  9.7 0.4 %collective-permute-done.refs_1_ = bf16[144,256]{1,0:T(8,128)(2,1)S(1)} collective-permute-done((bf16[144,256]{1,0:T(8,128)(2,1)S(1)}, bf16[144,256]{1,0:T(8,128)(2,1)S(1)}, u32[]{:S(2)}, u32[]{:S(2)}) %collective-permute-start) | collective-permute-done | bytes 73760 | tf_op jit(solution)/shard_map/ppermute | solution.py:152
  10.1 1.7 %collective-permute-start.1 = (bf16[288,256]{1,0:T(8,128)(2,1)S(1)}, bf16[288,256]{1,0:T(8,128)(2,1)S(1)}, u32[]{:S(2)}, u32[]{:S(2)}) collective-permute-start(bf16[288,256]{1,0:T(8,128)(2,1)S(1)} %shard_map.56.refs_0_), channel_id=1, source_target_pairs={{0,1},{1,0},{2,3},{3,2},{4,5},{5,4},{6,7},{7,6},{8,9},{9,8},{10,11... | collective-permute-start | bytes 442376 | tf_op jit(solution)/shard_map/ppermute | solution.py:152
  11.7 0.7 %collective-permute-start.2 = (bf16[288,256]{1,0:T(8,128)(2,1)S(1)}, bf16[288,256]{1,0:T(8,128)(2,1)S(1)}, u32[]{:S(2)}, u32[]{:S(2)}) collective-permute-start(bf16[288,256]{1,0:T(8,128)(2,1)S(1)} %shard_map.56.refs_0_), channel_id=1, source_target_pairs={{0,2},{1,3},{2,0},{3,1},{4,6},{5,7},{6,4},{7,5},{8,10},{9,11},{10,... | collective-permute-start | bytes 442376 | tf_op jit(solution)/shard_map/ppermute | solution.py:152
  12.5 0.4 %collective-permute-done.4 = bf16[144,256]{1,0:T(8,128)(2,1)S(1)} collective-permute-done((bf16[144,256]{1,0:T(8,128)(2,1)S(1)}, bf16[144,256]{1,0:T(8,128)(2,1)S(1)}, u32[]{:S(2)}, u32[]{:S(2)}) %collective-permute-start.4) | collective-permute-done | bytes 73760 | tf_op jit(solution)/shard_map/ppermute | solution.py:152
  12.8 2.6 %collective-permute-start.5 = (bf16[144,256]{1,0:T(8,128)(2,1)S(1)}, bf16[144,256]{1,0:T(8,128)(2,1)S(1)}, u32[]{:S(2)}, u32[]{:S(2)}) collective-permute-start(bf16[144,256]{1,0:T(8,128)(2,1)S(1)} %collective-permute-done.refs_1_), channel_id=1, source_target_pairs={{0,3},{1,2},{2,1},{3,0},{4,7},{5,6},{6,5},{7,4},{8,11},{9,10},{10,... | collective-permute-start | bytes 221192 | tf_op jit(solution)/shard_map/ppermute | solution.py:152
  15.5 0.0 collective-permute-done.6.refs_2_.refs_6_
  15.5 3.5 %collective-permute-done.7.refs_3_.refs_7_ = bf16[1040,128]{1,0:T(8,128)(2,1)S(1)} collective-permute-done((bf16[1040,128]{1,0:T(8,128)(2,1)S(1)}, bf16[1040,128]{1,0:T(8,128)(2,1)S(1)}, u32[]{:S(2)}, u32[]{:S(2)}) %collective-permute-start.7) | collective-permute-done | bytes 266272 | tf_op jit(solution)/shard_map/ppermute | solution.py:149
  19.0 0.0 collective-permute-done.5
  19.0 0.0 collective-permute-done.1.refs_1_
  19.1 0.0 collective-permute-done.2.refs_2_
  19.1 0.9 %shard_map.58 = (f32[32,128]{1,0:T(8,128)S(1)}, f32[32,128]{1,0:T(8,128)S(1)}, f32[32,128]{1,0:T(8,128)S(1)}, f32[32,128]{1,0:T(8,128)S(1)}) custom-call(bf16[288,256]{1,0:T(8,128)(2,1)S(1)} %shard_map.56.refs_0_, bf16[288,256]{1,0:T(8,128)(2,1)S(1)} %collective-permute-done.1.refs_1_, bf16[288,256]{1,0:T(8,128)(2,1)S(1)} %collective-permute-done.2.refs_2_, ...), custom_call_target="tpu_custom_call" | custom-call | flops 1 | tf_op jit(solution)/shard_map/pallas_call | solution.py:209
  20.0 1.5 %collective-permute-start.10 = (f32[32,128]{1,0:T(8,128)S(1)}, f32[32,128]{1,0:T(8,128)S(1)}, u32[]{:S(2)}, u32[]{:S(2)}) collective-permute-start(f32[32,128]{1,0:T(8,128)S(1)} %get-tuple-element.30), channel_id=1, source_target_pairs={{0,16},{8,24},{16,0},{24,8},{1,17},{9,25},{17,1},{25,9},{2,18},{10... | collective-permute-start | bytes 49160 | tf_op jit(solution)/shard_map/ppermute | solution.py:149
  21.5 0.5 %collective-permute-start.8 = (f32[32,128]{1,0:T(8,128)S(1)}, f32[32,128]{1,0:T(8,128)S(1)}, u32[]{:S(2)}, u32[]{:S(2)}) collective-permute-start(f32[32,128]{1,0:T(8,128)S(1)} %get-tuple-element.28), channel_id=1, source_target_pairs={{0,24},{8,16},{16,8},{24,0},{1,25},{9,17},{17,9},{25,1},{2,26},{10... | collective-permute-start | bytes 49160 | tf_op jit(solution)/shard_map/ppermute | solution.py:149
  22.0 0.2 collective-permute-start.9
  22.2 1.6 %collective-permute-done.10 = f32[32,128]{1,0:T(8,128)S(1)} collective-permute-done((f32[32,128]{1,0:T(8,128)S(1)}, f32[32,128]{1,0:T(8,128)S(1)}, u32[]{:S(2)}, u32[]{:S(2)}) %collective-permute-start.10) | collective-permute-done | bytes 16416 | tf_op jit(solution)/shard_map/ppermute | solution.py:149
  23.8 0.9 %collective-permute-done.8 = f32[32,128]{1,0:T(8,128)S(1)} collective-permute-done((f32[32,128]{1,0:T(8,128)S(1)}, f32[32,128]{1,0:T(8,128)S(1)}, u32[]{:S(2)}, u32[]{:S(2)}) %collective-permute-start.8) | collective-permute-done | bytes 16416 | tf_op jit(solution)/shard_map/ppermute | solution.py:149
  24.7 0.0 collective-permute-done.9
  24.7 0.6 %add_add_fusion = f32[32,128]{1,0:T(8,128)} fusion(f32[32,128]{1,0:T(8,128)S(1)} %collective-permute-done.10, f32[32,128]{1,0:T(8,128)S(1)} %collective-permute-done.9, f32[32,128]{1,0:T(8,128)S(1)} %get-tuple-element.27, f32[32,128]{1,0:T(8,128)S(1)} %collective-permute-done.8), kind=kLoop, calls=%fused_computation.1 | loop fusion | flops 12288 | bytes 81920 | tf_op jit(solution)/shard_map/add | solution.py:220
  (3 shorter events, 0.0 us)
Async XLA Ops:
  1.4 5.7 %collective-permute-start.3 = (bf16[1040,128]{1,0:T(8,128)(2,1)S(1)}, bf16[1040,128]{1,0:T(8,128)(2,1)S(1)}, u32[]{:S(2)}, u32[]{:S(2)}) collective-permute-start(bf16[1040,128]{1,0:T(8,128)(2,1)S(1)} %get-tuple-element.19), channel_id=1, source_target_pairs={{0,8},{8,0},{16,24},{24,16},{1,9},{9,1},{17,25},{25,17},{2,10},{10... | collective-permute-start | bytes 798728 | tf_op jit(solution)/shard_map/ppermute | solution.py:149
  2.0 8.1 %collective-permute-start = (bf16[144,256]{1,0:T(8,128)(2,1)S(1)}, bf16[144,256]{1,0:T(8,128)(2,1)S(1)}, u32[]{:S(2)}, u32[]{:S(2)}) collective-permute-start(bf16[144,256]{1,0:T(8,128)(2,1)S(1)} %get-tuple-element.20.refs_0_), channel_id=1, source_target_pairs={{0,4},{1,5},{2,6},{3,7},{4,0},{5,1},{6,2},{7,3},{8,12},{9,13},{10,... | collective-permute-start | bytes 221192 | tf_op jit(solution)/shard_map/ppermute | solution.py:152
  5.6 9.8 %collective-permute-start.6 = (bf16[1040,128]{1,0:T(8,128)(2,1)S(1)}, bf16[1040,128]{1,0:T(8,128)(2,1)S(1)}, u32[]{:S(2)}, u32[]{:S(2)}) collective-permute-start(bf16[1040,128]{1,0:T(8,128)(2,1)S(1)} %get-tuple-element.25), channel_id=1, source_target_pairs={{0,16},{8,24},{16,0},{24,8},{1,17},{9,25},{17,1},{25,9},{2,18},{10... | collective-permute-start | bytes 798728 | tf_op jit(solution)/shard_map/ppermute | solution.py:149
  7.1 11.9 %collective-permute-start.7 = (bf16[1040,128]{1,0:T(8,128)(2,1)S(1)}, bf16[1040,128]{1,0:T(8,128)(2,1)S(1)}, u32[]{:S(2)}, u32[]{:S(2)}) collective-permute-start(bf16[1040,128]{1,0:T(8,128)(2,1)S(1)} %get-tuple-element.26), channel_id=1, source_target_pairs={{0,24},{8,16},{16,8},{24,0},{1,25},{9,17},{17,9},{25,1},{2,26},{10... | collective-permute-start | bytes 798728 | tf_op jit(solution)/shard_map/ppermute | solution.py:149
  7.2 5.7 %collective-permute-start.4 = (bf16[144,256]{1,0:T(8,128)(2,1)S(1)}, bf16[144,256]{1,0:T(8,128)(2,1)S(1)}, u32[]{:S(2)}, u32[]{:S(2)}) collective-permute-start(bf16[144,256]{1,0:T(8,128)(2,1)S(1)} %get-tuple-element.20.refs_0_), channel_id=1, source_target_pairs={{0,3},{1,2},{2,1},{3,0},{4,7},{5,6},{6,5},{7,4},{8,11},{9,10},{10,... | collective-permute-start | bytes 221192 | tf_op jit(solution)/shard_map/ppermute | solution.py:152
  10.1 9.0 %collective-permute-start.1 = (bf16[288,256]{1,0:T(8,128)(2,1)S(1)}, bf16[288,256]{1,0:T(8,128)(2,1)S(1)}, u32[]{:S(2)}, u32[]{:S(2)}) collective-permute-start(bf16[288,256]{1,0:T(8,128)(2,1)S(1)} %shard_map.56.refs_0_), channel_id=1, source_target_pairs={{0,1},{1,0},{2,3},{3,2},{4,5},{5,4},{6,7},{7,6},{8,9},{9,8},{10,11... | collective-permute-start | bytes 442376 | tf_op jit(solution)/shard_map/ppermute | solution.py:152
  11.7 7.3 %collective-permute-start.2 = (bf16[288,256]{1,0:T(8,128)(2,1)S(1)}, bf16[288,256]{1,0:T(8,128)(2,1)S(1)}, u32[]{:S(2)}, u32[]{:S(2)}) collective-permute-start(bf16[288,256]{1,0:T(8,128)(2,1)S(1)} %shard_map.56.refs_0_), channel_id=1, source_target_pairs={{0,2},{1,3},{2,0},{3,1},{4,6},{5,7},{6,4},{7,5},{8,10},{9,11},{10,... | collective-permute-start | bytes 442376 | tf_op jit(solution)/shard_map/ppermute | solution.py:152
  12.8 6.2 %collective-permute-start.5 = (bf16[144,256]{1,0:T(8,128)(2,1)S(1)}, bf16[144,256]{1,0:T(8,128)(2,1)S(1)}, u32[]{:S(2)}, u32[]{:S(2)}) collective-permute-start(bf16[144,256]{1,0:T(8,128)(2,1)S(1)} %collective-permute-done.refs_1_), channel_id=1, source_target_pairs={{0,3},{1,2},{2,1},{3,0},{4,7},{5,6},{6,5},{7,4},{8,11},{9,10},{10,... | collective-permute-start | bytes 221192 | tf_op jit(solution)/shard_map/ppermute | solution.py:152
  20.0 3.8 %collective-permute-start.10 = (f32[32,128]{1,0:T(8,128)S(1)}, f32[32,128]{1,0:T(8,128)S(1)}, u32[]{:S(2)}, u32[]{:S(2)}) collective-permute-start(f32[32,128]{1,0:T(8,128)S(1)} %get-tuple-element.30), channel_id=1, source_target_pairs={{0,16},{8,24},{16,0},{24,8},{1,17},{9,25},{17,1},{25,9},{2,18},{10... | collective-permute-start | bytes 49160 | tf_op jit(solution)/shard_map/ppermute | solution.py:149
  21.5 3.2 %collective-permute-start.8 = (f32[32,128]{1,0:T(8,128)S(1)}, f32[32,128]{1,0:T(8,128)S(1)}, u32[]{:S(2)}, u32[]{:S(2)}) collective-permute-start(f32[32,128]{1,0:T(8,128)S(1)} %get-tuple-element.28), channel_id=1, source_target_pairs={{0,24},{8,16},{16,8},{24,0},{1,25},{9,17},{17,9},{25,1},{2,26},{10... | collective-permute-start | bytes 49160 | tf_op jit(solution)/shard_map/ppermute | solution.py:149
  22.0 2.7 %collective-permute-start.9 = (f32[32,128]{1,0:T(8,128)S(1)}, f32[32,128]{1,0:T(8,128)S(1)}, u32[]{:S(2)}, u32[]{:S(2)}) collective-permute-start(f32[32,128]{1,0:T(8,128)S(1)} %get-tuple-element.29), channel_id=1, source_target_pairs={{0,8},{8,0},{16,24},{24,16},{1,9},{9,1},{17,25},{25,17},{2,10},{10... | collective-permute-start | bytes 49160 | tf_op jit(solution)/shard_map/ppermute | solution.py:149

commit v7 on v6

--- a/solution.py
+++ b/solution.py
@@ -110,7 +110,10 @@
         groups.append(dot(pick, jnp.concatenate(values, axis=0)).astype(jnp.bfloat16))
         starts.append(((me_o // per) ^ quad) * 16)
     for k in range(n_panel):
-        delays = late_ref[8 * k : 8 * k + 8][0:1]
+        if k < 2:
+            delays = pieces[k][2 * depth : 2 * depth + EXTRA, :].astype(jnp.float32)[0:1].astype(jnp.int32)
+        else:
+            delays = late_ref[8 * (k - 2) : 8 * (k - 1)][0:1]
         for b in range(n_obs // 2):
             row = 32 * (k * (n_obs // 2) + b)
             source = jnp.concatenate(
@@ -199,12 +202,12 @@
     buffers, pieces = (a, ya, b, yb), (own, from_c, from_x, from_xc)
     late = pl.pallas_call(
         late_kernel,
-        out_shape=jax.ShapeDtypeStruct((8 * n_panel, observers), jnp.int32),
-        in_specs=[vmem] * n_panel,
+        out_shape=jax.ShapeDtypeStruct((8 * (n_panel - 2), observers), jnp.int32),
+        in_specs=[vmem] * (n_panel - 2),
         out_specs=vmem,
         compiler_params=params,
         cost_estimate=pl.CostEstimate(flops=2*10**9, bytes_accessed=0, transcendentals=0),
-    )(*pieces)
+    )(*pieces[2:])
     share = jax.ShapeDtypeStruct((steps // n_panel, observers), jnp.float32)
     shares = pl.pallas_call(
         functools.partial(part_kernel, n_panel, n_obs, cap),
@@ -216,7 +219,7 @@
         cost_estimate=pl.CostEstimate(flops=1, bytes_accessed=0, transcendentals=0),
     )(*buffers, *pieces, late)
     total = shares[0]
-    for k in (3, 1, 2):
+    for k in (2, 3, 1):
         total = total + along_panel(shares[k], k)
     return total
 

time: 25.4 us -> 25.4 us (level)
  no operation moved by 1% of the time
where the time goes in v7:
time: 25.4 us; the launch traced here: 25.3 us
  starting transfers between devices  15.6 us (61%)
  waiting for transfers between devices  6.65 us (26%)
  Pallas kernels  2.32 us (9%)
  other arithmetic  0.63 us (2%)
    ppermute x5, starting transfers between devices, along_obs(): return lax.ppermute(value, 'obs', [(i, i ^ k) for i in range(n_obs)])  11.4 us
    ppermute x6, waiting for transfers between devices, along_panel(): return lax.ppermute(value, 'panel', [(i, i ^ k) for i in range(n_panel)])  5.9 us
    ppermute x6, starting transfers between devices, along_panel(): return lax.ppermute(value, 'panel', [(i, i ^ k) for i in range(n_panel)])  4.26 us
    pallas_call x1, Pallas kernels, per_device(): pl.pallas_call(functools.partial(pack_kernel, n_panel, n_obs, cap), out_s...  1.43 us
    pallas_call x1, Pallas kernels, per_device(): pl.pallas_call(functools.partial(part_kernel, n_panel, n_obs, cap), out_s...  0.88 us
    ppermute x5, waiting for transfers between devices, along_obs(): return lax.ppermute(value, 'obs', [(i, i ^ k) for i in range(n_obs)])  0.76 us
    add x1, other arithmetic, per_device(): total = total + along_panel(shares[k], k)  0.61 us
  transfers between devices with their start and end apart: 11, of which 5 were waited for; matrix products, arithmetic and copies ran while one was open for 0% of the time, Pallas kernels for 0%

profile of v7, /device:TPU:0, one launch (start us, length us, event | category | flops | bytes accessed | tf_op | source)
XLA Modules:
  0.0 25.3 jit_solution(1246067236140864978)
XLA Ops:
  0.0 1.4 %shard_map.55 = (bf16[144,256]{1,0:T(8,128)(2,1)S(1)}, bf16[1040,128]{1,0:T(8,128)(2,1)S(1)}, bf16[1040,128]{1,0:T(8,128)(2,1)S(1)}, bf16[1040,128]{1,0:T(8,128)(2,1)S(1)}, bf16[1040,128]{1,0:T(8,128)(2,1)S(1)}) custom-call(bf16[256,128]{1,0:T(8,128)(2,1)} %bitcast.7, s32[1,128]{1,0:T(1,128)} %bitcast.8, s32[1,4]{1,0:T(1,128)} %bitcast.9, ...), custom_call_target="tpu_custom_call" | custom-call | tf_op jit(solution)/shard_map/pallas_call | solution.py:160
  1.4 0.5 %collective-permute-start.3 = (bf16[1040,128]{1,0:T(8,128)(2,1)S(1)}, bf16[1040,128]{1,0:T(8,128)(2,1)S(1)}, u32[]{:S(2)}, u32[]{:S(2)}) collective-permute-start(bf16[1040,128]{1,0:T(8,128)(2,1)S(1)} %get-tuple-element.19), channel_id=1, source_target_pairs={{0,8},{8,0},{16,24},{24,16},{1,9},{9,1},{17,25},{25,17},{2,10},{10... | collective-permute-start | bytes 798728 | tf_op jit(solution)/shard_map/ppermute | solution.py:152
  2.0 3.7 %collective-permute-start = (bf16[144,256]{1,0:T(8,128)(2,1)S(1)}, bf16[144,256]{1,0:T(8,128)(2,1)S(1)}, u32[]{:S(2)}, u32[]{:S(2)}) collective-permute-start(bf16[144,256]{1,0:T(8,128)(2,1)S(1)} %get-tuple-element.20.refs_0_), channel_id=1, source_target_pairs={{0,4},{1,5},{2,6},{3,7},{4,0},{5,1},{6,2},{7,3},{8,12},{9,13},{10,... | collective-permute-start | bytes 221192 | tf_op jit(solution)/shard_map/ppermute | solution.py:155
  5.6 1.5 %collective-permute-start.6 = (bf16[1040,128]{1,0:T(8,128)(2,1)S(1)}, bf16[1040,128]{1,0:T(8,128)(2,1)S(1)}, u32[]{:S(2)}, u32[]{:S(2)}) collective-permute-start(bf16[1040,128]{1,0:T(8,128)(2,1)S(1)} %get-tuple-element.25), channel_id=1, source_target_pairs={{0,16},{8,24},{16,0},{24,8},{1,17},{9,25},{17,1},{25,9},{2,18},{10... | collective-permute-start | bytes 798728 | tf_op jit(solution)/shard_map/ppermute | solution.py:152
  7.1 0.0 collective-permute-start.7
  7.1 0.0 collective-permute-done.3.refs_5_
  7.2 2.5 %collective-permute-start.4 = (bf16[144,256]{1,0:T(8,128)(2,1)S(1)}, bf16[144,256]{1,0:T(8,128)(2,1)S(1)}, u32[]{:S(2)}, u32[]{:S(2)}) collective-permute-start(bf16[144,256]{1,0:T(8,128)(2,1)S(1)} %get-tuple-element.20.refs_0_), channel_id=1, source_target_pairs={{0,3},{1,2},{2,1},{3,0},{4,7},{5,6},{6,5},{7,4},{8,11},{9,10},{10,... | collective-permute-start | bytes 221192 | tf_op jit(solution)/shard_map/ppermute | solution.py:155
  9.7 0.4 %collective-permute-done.refs_1_ = bf16[144,256]{1,0:T(8,128)(2,1)S(1)} collective-permute-done((bf16[144,256]{1,0:T(8,128)(2,1)S(1)}, bf16[144,256]{1,0:T(8,128)(2,1)S(1)}, u32[]{:S(2)}, u32[]{:S(2)}) %collective-permute-start) | collective-permute-done | bytes 73760 | tf_op jit(solution)/shard_map/ppermute | solution.py:155
  10.1 0.8 %collective-permute-start.2 = (bf16[288,256]{1,0:T(8,128)(2,1)S(1)}, bf16[288,256]{1,0:T(8,128)(2,1)S(1)}, u32[]{:S(2)}, u32[]{:S(2)}) collective-permute-start(bf16[288,256]{1,0:T(8,128)(2,1)S(1)} %shard_map.56.refs_0_), channel_id=1, source_target_pairs={{0,2},{1,3},{2,0},{3,1},{4,6},{5,7},{6,4},{7,5},{8,10},{9,11},{10,... | collective-permute-start | bytes 442376 | tf_op jit(solution)/shard_map/ppermute | solution.py:155
  10.9 1.6 %collective-permute-start.1 = (bf16[288,256]{1,0:T(8,128)(2,1)S(1)}, bf16[288,256]{1,0:T(8,128)(2,1)S(1)}, u32[]{:S(2)}, u32[]{:S(2)}) collective-permute-start(bf16[288,256]{1,0:T(8,128)(2,1)S(1)} %shard_map.56.refs_0_), channel_id=1, source_target_pairs={{0,1},{1,0},{2,3},{3,2},{4,5},{5,4},{6,7},{7,6},{8,9},{9,8},{10,11... | collective-permute-start | bytes 442376 | tf_op jit(solution)/shard_map/ppermute | solution.py:155
  12.5 0.4 %collective-permute-done.4 = bf16[144,256]{1,0:T(8,128)(2,1)S(1)} collective-permute-done((bf16[144,256]{1,0:T(8,128)(2,1)S(1)}, bf16[144,256]{1,0:T(8,128)(2,1)S(1)}, u32[]{:S(2)}, u32[]{:S(2)}) %collective-permute-start.4) | collective-permute-done | bytes 73760 | tf_op jit(solution)/shard_map/ppermute | solution.py:155
  12.8 2.8 %collective-permute-start.5 = (bf16[144,256]{1,0:T(8,128)(2,1)S(1)}, bf16[144,256]{1,0:T(8,128)(2,1)S(1)}, u32[]{:S(2)}, u32[]{:S(2)}) collective-permute-start(bf16[144,256]{1,0:T(8,128)(2,1)S(1)} %collective-permute-done.refs_1_), channel_id=1, source_target_pairs={{0,3},{1,2},{2,1},{3,0},{4,7},{5,6},{6,5},{7,4},{8,11},{9,10},{10,... | collective-permute-start | bytes 221192 | tf_op jit(solution)/shard_map/ppermute | solution.py:155
  15.6 0.0 collective-permute-done.6.refs_0_.refs_6_
  15.6 3.4 %collective-permute-done.7.refs_1_.refs_7_ = bf16[1040,128]{1,0:T(8,128)(2,1)S(1)} collective-permute-done((bf16[1040,128]{1,0:T(8,128)(2,1)S(1)}, bf16[1040,128]{1,0:T(8,128)(2,1)S(1)}, u32[]{:S(2)}, u32[]{:S(2)}) %collective-permute-start.7) | collective-permute-done | bytes 266272 | tf_op jit(solution)/shard_map/ppermute | solution.py:152
  19.0 0.0 collective-permute-done.5
  19.0 0.0 collective-permute-done.2.refs_2_
  19.1 0.0 collective-permute-done.1.refs_1_
  19.1 0.9 %shard_map.58 = (f32[32,128]{1,0:T(8,128)S(1)}, f32[32,128]{1,0:T(8,128)S(1)}, f32[32,128]{1,0:T(8,128)S(1)}, f32[32,128]{1,0:T(8,128)S(1)}) custom-call(bf16[288,256]{1,0:T(8,128)(2,1)S(1)} %shard_map.56.refs_0_, bf16[288,256]{1,0:T(8,128)(2,1)S(1)} %collective-permute-done.1.refs_1_, bf16[288,256]{1,0:T(8,128)(2,1)S(1)} %collective-permute-done.2.refs_2_, ...), custom_call_target="tpu_custom_call" | custom-call | flops 1 | tf_op jit(solution)/shard_map/pallas_call | solution.py:212
  19.9 1.6 %collective-permute-start.8 = (f32[32,128]{1,0:T(8,128)S(1)}, f32[32,128]{1,0:T(8,128)S(1)}, u32[]{:S(2)}, u32[]{:S(2)}) collective-permute-start(f32[32,128]{1,0:T(8,128)S(1)} %get-tuple-element.28), channel_id=1, source_target_pairs={{0,16},{8,24},{16,0},{24,8},{1,17},{9,25},{17,1},{25,9},{2,18},{10... | collective-permute-start | bytes 49160 | tf_op jit(solution)/shard_map/ppermute | solution.py:152
  21.5 0.5 %collective-permute-start.9 = (f32[32,128]{1,0:T(8,128)S(1)}, f32[32,128]{1,0:T(8,128)S(1)}, u32[]{:S(2)}, u32[]{:S(2)}) collective-permute-start(f32[32,128]{1,0:T(8,128)S(1)} %get-tuple-element.29), channel_id=1, source_target_pairs={{0,24},{8,16},{16,8},{24,0},{1,25},{9,17},{17,9},{25,1},{2,26},{10... | collective-permute-start | bytes 49160 | tf_op jit(solution)/shard_map/ppermute | solution.py:152
  22.0 0.2 collective-permute-start.10
  22.2 1.6 %collective-permute-done.8 = f32[32,128]{1,0:T(8,128)S(1)} collective-permute-done((f32[32,128]{1,0:T(8,128)S(1)}, f32[32,128]{1,0:T(8,128)S(1)}, u32[]{:S(2)}, u32[]{:S(2)}) %collective-permute-start.8) | collective-permute-done | bytes 16416 | tf_op jit(solution)/shard_map/ppermute | solution.py:152
  23.7 0.9 %collective-permute-done.9 = f32[32,128]{1,0:T(8,128)S(1)} collective-permute-done((f32[32,128]{1,0:T(8,128)S(1)}, f32[32,128]{1,0:T(8,128)S(1)}, u32[]{:S(2)}, u32[]{:S(2)}) %collective-permute-start.9) | collective-permute-done | bytes 16416 | tf_op jit(solution)/shard_map/ppermute | solution.py:152
  24.7 0.0 collective-permute-done.10
  24.7 0.6 %add_add_fusion = f32[32,128]{1,0:T(8,128)} fusion(f32[32,128]{1,0:T(8,128)S(1)} %collective-permute-done.10, f32[32,128]{1,0:T(8,128)S(1)} %collective-permute-done.9, f32[32,128]{1,0:T(8,128)S(1)} %get-tuple-element.27, f32[32,128]{1,0:T(8,128)S(1)} %collective-permute-done.8), kind=kLoop, calls=%fused_computation.1 | loop fusion | flops 12288 | bytes 81920 | tf_op jit(solution)/shard_map/add | solution.py:223
  (3 shorter events, 0.0 us)
Async XLA Ops:
  1.4 5.7 %collective-permute-start.3 = (bf16[1040,128]{1,0:T(8,128)(2,1)S(1)}, bf16[1040,128]{1,0:T(8,128)(2,1)S(1)}, u32[]{:S(2)}, u32[]{:S(2)}) collective-permute-start(bf16[1040,128]{1,0:T(8,128)(2,1)S(1)} %get-tuple-element.19), channel_id=1, source_target_pairs={{0,8},{8,0},{16,24},{24,16},{1,9},{9,1},{17,25},{25,17},{2,10},{10... | collective-permute-start | bytes 798728 | tf_op jit(solution)/shard_map/ppermute | solution.py:152
  2.0 8.1 %collective-permute-start = (bf16[144,256]{1,0:T(8,128)(2,1)S(1)}, bf16[144,256]{1,0:T(8,128)(2,1)S(1)}, u32[]{:S(2)}, u32[]{:S(2)}) collective-permute-start(bf16[144,256]{1,0:T(8,128)(2,1)S(1)} %get-tuple-element.20.refs_0_), channel_id=1, source_target_pairs={{0,4},{1,5},{2,6},{3,7},{4,0},{5,1},{6,2},{7,3},{8,12},{9,13},{10,... | collective-permute-start | bytes 221192 | tf_op jit(solution)/shard_map/ppermute | solution.py:155
  5.6 10.0 %collective-permute-start.6 = (bf16[1040,128]{1,0:T(8,128)(2,1)S(1)}, bf16[1040,128]{1,0:T(8,128)(2,1)S(1)}, u32[]{:S(2)}, u32[]{:S(2)}) collective-permute-start(bf16[1040,128]{1,0:T(8,128)(2,1)S(1)} %get-tuple-element.25), channel_id=1, source_target_pairs={{0,16},{8,24},{16,0},{24,8},{1,17},{9,25},{17,1},{25,9},{2,18},{10... | collective-permute-start | bytes 798728 | tf_op jit(solution)/shard_map/ppermute | solution.py:152
  7.1 11.9 %collective-permute-start.7 = (bf16[1040,128]{1,0:T(8,128)(2,1)S(1)}, bf16[1040,128]{1,0:T(8,128)(2,1)S(1)}, u32[]{:S(2)}, u32[]{:S(2)}) collective-permute-start(bf16[1040,128]{1,0:T(8,128)(2,1)S(1)} %get-tuple-element.26), channel_id=1, source_target_pairs={{0,24},{8,16},{16,8},{24,0},{1,25},{9,17},{17,9},{25,1},{2,26},{10... | collective-permute-start | bytes 798728 | tf_op jit(solution)/shard_map/ppermute | solution.py:152
  7.2 5.7 %collective-permute-start.4 = (bf16[144,256]{1,0:T(8,128)(2,1)S(1)}, bf16[144,256]{1,0:T(8,128)(2,1)S(1)}, u32[]{:S(2)}, u32[]{:S(2)}) collective-permute-start(bf16[144,256]{1,0:T(8,128)(2,1)S(1)} %get-tuple-element.20.refs_0_), channel_id=1, source_target_pairs={{0,3},{1,2},{2,1},{3,0},{4,7},{5,6},{6,5},{7,4},{8,11},{9,10},{10,... | collective-permute-start | bytes 221192 | tf_op jit(solution)/shard_map/ppermute | solution.py:155
  10.1 9.0 %collective-permute-start.2 = (bf16[288,256]{1,0:T(8,128)(2,1)S(1)}, bf16[288,256]{1,0:T(8,128)(2,1)S(1)}, u32[]{:S(2)}, u32[]{:S(2)}) collective-permute-start(bf16[288,256]{1,0:T(8,128)(2,1)S(1)} %shard_map.56.refs_0_), channel_id=1, source_target_pairs={{0,2},{1,3},{2,0},{3,1},{4,6},{5,7},{6,4},{7,5},{8,10},{9,11},{10,... | collective-permute-start | bytes 442376 | tf_op jit(solution)/shard_map/ppermute | solution.py:155
  10.9 8.2 %collective-permute-start.1 = (bf16[288,256]{1,0:T(8,128)(2,1)S(1)}, bf16[288,256]{1,0:T(8,128)(2,1)S(1)}, u32[]{:S(2)}, u32[]{:S(2)}) collective-permute-start(bf16[288,256]{1,0:T(8,128)(2,1)S(1)} %shard_map.56.refs_0_), channel_id=1, source_target_pairs={{0,1},{1,0},{2,3},{3,2},{4,5},{5,4},{6,7},{7,6},{8,9},{9,8},{10,11... | collective-permute-start | bytes 442376 | tf_op jit(solution)/shard_map/ppermute | solution.py:155
  12.8 6.2 %collective-permute-start.5 = (bf16[144,256]{1,0:T(8,128)(2,1)S(1)}, bf16[144,256]{1,0:T(8,128)(2,1)S(1)}, u32[]{:S(2)}, u32[]{:S(2)}) collective-permute-start(bf16[144,256]{1,0:T(8,128)(2,1)S(1)} %collective-permute-done.refs_1_), channel_id=1, source_target_pairs={{0,3},{1,2},{2,1},{3,0},{4,7},{5,6},{6,5},{7,4},{8,11},{9,10},{10,... | collective-permute-start | bytes 221192 | tf_op jit(solution)/shard_map/ppermute | solution.py:155
  19.9 3.8 %collective-permute-start.8 = (f32[32,128]{1,0:T(8,128)S(1)}, f32[32,128]{1,0:T(8,128)S(1)}, u32[]{:S(2)}, u32[]{:S(2)}) collective-permute-start(f32[32,128]{1,0:T(8,128)S(1)} %get-tuple-element.28), channel_id=1, source_target_pairs={{0,16},{8,24},{16,0},{24,8},{1,17},{9,25},{17,1},{25,9},{2,18},{10... | collective-permute-start | bytes 49160 | tf_op jit(solution)/shard_map/ppermute | solution.py:152
  21.5 3.2 %collective-permute-start.9 = (f32[32,128]{1,0:T(8,128)S(1)}, f32[32,128]{1,0:T(8,128)S(1)}, u32[]{:S(2)}, u32[]{:S(2)}) collective-permute-start(f32[32,128]{1,0:T(8,128)S(1)} %get-tuple-element.29), channel_id=1, source_target_pairs={{0,24},{8,16},{16,8},{24,0},{1,25},{9,17},{17,9},{25,1},{2,26},{10... | collective-permute-start | bytes 49160 | tf_op jit(solution)/shard_map/ppermute | solution.py:152
  22.0 2.7 %collective-permute-start.10 = (f32[32,128]{1,0:T(8,128)S(1)}, f32[32,128]{1,0:T(8,128)S(1)}, u32[]{:S(2)}, u32[]{:S(2)}) collective-permute-start(f32[32,128]{1,0:T(8,128)S(1)} %get-tuple-element.30), channel_id=1, source_target_pairs={{0,8},{8,0},{16,24},{24,16},{1,9},{9,1},{17,25},{25,17},{2,10},{10... | collective-permute-start | bytes 49160 | tf_op jit(solution)/shard_map/ppermute | solution.py:152

commit v8 on v6

--- a/solution.py
+++ b/solution.py
@@ -8,7 +8,7 @@
 from jax.sharding import PartitionSpec as P
 
 PBLK = 512
-PACK_ORDER = (2, 3, 1, 0)
+FAR = (2, 3)
 EXTRA = 16
 VMEM_LIMIT = 48 * 1024 * 1024
 
@@ -18,8 +18,8 @@
 
 
 def pack_kernel(n_panel, n_obs, cap, rows_ref, dest_ref, delay_ref, load_ref, thick_ref, *refs):
-    message_ref, pieces = refs[0], refs[1 : 1 + n_panel]
-    rows_in, dest_in, delay_in, sems, few = refs[1 + n_panel :]
+    message_ref, chip_ref, *pieces = refs[:4]
+    rows_in, dest_in, delay_in, sems, few = refs[4:]
     count = n_panel * n_obs
     me_p = lax.axis_index("panel")
     width = n_obs * cap
@@ -31,11 +31,15 @@
     for copy in small:
         copy.start()
     copies = []
-    for k in PACK_ORDER:
+    for at, k in enumerate(FAR):
         for i, ref in enumerate((load_ref, thick_ref)):
-            there = pieces[k].at[pl.ds(i * depth, depth)].reshape(n_obs, width, ref.shape[3])
-            copies.append(pltpu.make_async_copy(ref.at[:, me_p ^ k], there, sems.at[k, i]))
+            there = pieces[at].at[pl.ds(i * depth, depth)].reshape(n_obs, width, ref.shape[3])
+            copies.append(pltpu.make_async_copy(ref.at[:, me_p ^ k], there, sems.at[at, i]))
             copies[-1].start()
+    for i, ref in enumerate((load_ref, thick_ref)):
+        there = chip_ref.at[pl.ds(2 * i * depth, 2 * depth)].reshape(n_obs, 2, width, ref.shape[3])
+        copies.append(pltpu.make_async_copy(ref.at[:, pl.ds(me_p // 2 * 2, 2)], there, sems.at[2, i]))
+        copies[-1].start()
     rows, steps = rows_ref.shape[0] // 2, rows_ref.shape[1]
     nblocks = delay_ref.shape[1]
     for copy in small:
@@ -44,8 +48,8 @@
     late = jnp.zeros(lane.shape, jnp.int32)
     for b in range(nblocks):
         late = jnp.where(lane == b, delay_in[0, b], late)
-    for k in range(n_panel):
-        pieces[k][2 * depth : 2 * depth + EXTRA, :] = late.astype(jnp.float32).astype(jnp.bfloat16)
+    for ref in (chip_ref, *pieces):
+        ref[ref.shape[0] - EXTRA :, :] = late.astype(jnp.float32).astype(jnp.bfloat16)
     r0 = lax.broadcasted_iota(jnp.int32, (rows, 2 * rows), 0)
     r1 = lax.broadcasted_iota(jnp.int32, (rows, 2 * rows), 1)
     value = rows_in[...]
@@ -111,6 +115,7 @@
         starts.append(((me_o // per) ^ quad) * 16)
     for k in range(n_panel):
         delays = late_ref[8 * k : 8 * k + 8][0:1]
+        scale, shift = (2, me_p % 2 * width) if k < 2 else (1, 0)
         for b in range(n_obs // 2):
             row = 32 * (k * (n_obs // 2) + b)
             source = jnp.concatenate(
@@ -118,7 +123,7 @@
             )
             weights = jnp.concatenate(
                 [
-                    pieces[k][pl.ds(pl.multiple_of(c * depth + (2 * b + h) * width + start, 16), 16), :]
+                    pieces[k][pl.ds(pl.multiple_of(scale * (c * depth + (2 * b + h) * width) + shift + start, 16), 16), :]
                     for c in range(2)
                     for start in starts
                     for h in range(2)
@@ -154,11 +159,12 @@
     load = loading_weight.reshape(n_obs, n_panel, width, observers)
     thick = thickness_weight.reshape(n_obs, n_panel, width, observers)
     piece = jax.ShapeDtypeStruct((2 * n_obs * width + EXTRA, observers), jnp.bfloat16)
-    message, own, to_c, to_x, to_xc = pl.pallas_call(
+    chip = jax.ShapeDtypeStruct((4 * n_obs * width + EXTRA, observers), jnp.bfloat16)
+    message, own, to_x, to_xc = pl.pallas_call(
         functools.partial(pack_kernel, n_panel, n_obs, cap),
-        out_shape=[jax.ShapeDtypeStruct((rows + EXTRA, 2 * steps), jnp.bfloat16)] + [piece] * n_panel,
+        out_shape=[jax.ShapeDtypeStruct((rows + EXTRA, 2 * steps), jnp.bfloat16)] + [chip, piece, piece],
         in_specs=[hbm] * 5,
-        out_specs=[vmem] * (1 + n_panel),
+        out_specs=[vmem] * 4,
         scratch_shapes=[
             pltpu.VMEM((2 * rows, steps), jnp.bfloat16),
             pltpu.VMEM((1, rows), jnp.int32),
@@ -179,7 +185,7 @@
             )
         )
     )
-    from_x, from_xc, from_c = along_panel(to_x, 2), along_panel(to_xc, 3), along_panel(to_c, 1)
+    from_x, from_xc, from_c = along_panel(to_x, 2), along_panel(to_xc, 3), along_panel(own, 1)
     ranges = range(4, n_obs, 4)
     far = [along_obs(message, k) for k in ranges]
     later, from_c = lax.optimization_barrier((message, from_c))

time: 25.4 us -> 25.5 us (level)
  no operation moved by 1% of the time
where the time goes in v8:
time: 25.5 us; the launch traced here: 25.3 us
  starting transfers between devices  15.4 us (60%)
  waiting for transfers between devices  6.83 us (27%)
  Pallas kernels  2.35 us (9%)
  other arithmetic  0.62 us (2%)
    ppermute x5, starting transfers between devices, along_obs(): return lax.ppermute(value, 'obs', [(i, i ^ k) for i in range(n_obs)])  11.2 us
    ppermute x6, waiting for transfers between devices, along_panel(): return lax.ppermute(value, 'panel', [(i, i ^ k) for i in range(n_panel)])  6.07 us
    ppermute x6, starting transfers between devices, along_panel(): return lax.ppermute(value, 'panel', [(i, i ^ k) for i in range(n_panel)])  4.25 us
    pallas_call x1, Pallas kernels, per_device(): pl.pallas_call(functools.partial(pack_kernel, n_panel, n_obs, cap), out_s...  1.43 us
    pallas_call x1, Pallas kernels, per_device(): pl.pallas_call(functools.partial(part_kernel, n_panel, n_obs, cap), out_s...  0.9 us
    ppermute x5, waiting for transfers between devices, along_obs(): return lax.ppermute(value, 'obs', [(i, i ^ k) for i in range(n_obs)])  0.77 us
    add x1, other arithmetic, per_device(): total = total + along_panel(shares[k], k)  0.61 us
  transfers between devices with their start and end apart: 11, of which 5 were waited for; matrix products, arithmetic and copies ran while one was open for 0% of the time, Pallas kernels for 0%

profile of v8, /device:TPU:0, one launch (start us, length us, event | category | flops | bytes accessed | tf_op | source)
XLA Modules:
  0.0 25.3 jit_solution(4391996978660678731)
XLA Ops:
  0.0 1.4 %shard_map.55 = (bf16[144,256]{1,0:T(8,128)(2,1)S(1)}, bf16[2064,128]{1,0:T(8,128)(2,1)S(1)}, bf16[1040,128]{1,0:T(8,128)(2,1)S(1)}, bf16[1040,128]{1,0:T(8,128)(2,1)S(1)}) custom-call(bf16[256,128]{1,0:T(8,128)(2,1)} %bitcast.7, s32[1,128]{1,0:T(1,128)} %bitcast.8, s32[1,4]{1,0:T(1,128)} %bitcast.9, bf16[8,4,64,128]{3,2,1,0:T(8,128)(2,1)} %bitcast.5, ...), custom_call_target="tpu_custom_call" | custom-call | tf_op jit(solution)/shard_map/pallas_call | solution.py:163
  1.4 0.5 %collective-permute-start.3 = (bf16[2064,128]{1,0:T(8,128)(2,1)S(1)}, bf16[2064,128]{1,0:T(8,128)(2,1)S(1)}, u32[]{:S(2)}, u32[]{:S(2)}) collective-permute-start(bf16[2064,128]{1,0:T(8,128)(2,1)S(1)} %get-tuple-element.18.refs_0_.refs_4_), channel_id=1, source_target_pairs={{0,8},{8,0},{16,24},{24,16},{1,9},{9,1},{17,25},{25,17},{2,10},{10... | collective-permute-start | bytes 1585160 | tf_op jit(solution)/shard_map/ppermute | solution.py:154
  2.0 3.7 %collective-permute-start = (bf16[144,256]{1,0:T(8,128)(2,1)S(1)}, bf16[144,256]{1,0:T(8,128)(2,1)S(1)}, u32[]{:S(2)}, u32[]{:S(2)}) collective-permute-start(bf16[144,256]{1,0:T(8,128)(2,1)S(1)} %get-tuple-element.19.refs_0_), channel_id=1, source_target_pairs={{0,4},{1,5},{2,6},{3,7},{4,0},{5,1},{6,2},{7,3},{8,12},{9,13},{10,... | collective-permute-start | bytes 221192 | tf_op jit(solution)/shard_map/ppermute | solution.py:157
  5.6 1.5 %collective-permute-start.6 = (bf16[1040,128]{1,0:T(8,128)(2,1)S(1)}, bf16[1040,128]{1,0:T(8,128)(2,1)S(1)}, u32[]{:S(2)}, u32[]{:S(2)}) collective-permute-start(bf16[1040,128]{1,0:T(8,128)(2,1)S(1)} %get-tuple-element.23), channel_id=1, source_target_pairs={{0,16},{8,24},{16,0},{24,8},{1,17},{9,25},{17,1},{25,9},{2,18},{10... | collective-permute-start | bytes 798728 | tf_op jit(solution)/shard_map/ppermute | solution.py:154
  7.1 0.0 collective-permute-start.7
  7.2 0.0 collective-permute-done.3.refs_1_.refs_5_
  7.2 2.5 %collective-permute-start.4 = (bf16[144,256]{1,0:T(8,128)(2,1)S(1)}, bf16[144,256]{1,0:T(8,128)(2,1)S(1)}, u32[]{:S(2)}, u32[]{:S(2)}) collective-permute-start(bf16[144,256]{1,0:T(8,128)(2,1)S(1)} %get-tuple-element.19.refs_0_), channel_id=1, source_target_pairs={{0,3},{1,2},{2,1},{3,0},{4,7},{5,6},{6,5},{7,4},{8,11},{9,10},{10,... | collective-permute-start | bytes 221192 | tf_op jit(solution)/shard_map/ppermute | solution.py:157
  9.7 0.4 %collective-permute-done.refs_1_ = bf16[144,256]{1,0:T(8,128)(2,1)S(1)} collective-permute-done((bf16[144,256]{1,0:T(8,128)(2,1)S(1)}, bf16[144,256]{1,0:T(8,128)(2,1)S(1)}, u32[]{:S(2)}, u32[]{:S(2)}) %collective-permute-start) | collective-permute-done | bytes 73760 | tf_op jit(solution)/shard_map/ppermute | solution.py:157
  10.1 1.7 %collective-permute-start.1 = (bf16[288,256]{1,0:T(8,128)(2,1)S(1)}, bf16[288,256]{1,0:T(8,128)(2,1)S(1)}, u32[]{:S(2)}, u32[]{:S(2)}) collective-permute-start(bf16[288,256]{1,0:T(8,128)(2,1)S(1)} %shard_map.56.refs_0_), channel_id=1, source_target_pairs={{0,1},{1,0},{2,3},{3,2},{4,5},{5,4},{6,7},{7,6},{8,9},{9,8},{10,11... | collective-permute-start | bytes 442376 | tf_op jit(solution)/shard_map/ppermute | solution.py:157
  11.7 0.7 %collective-permute-start.2 = (bf16[288,256]{1,0:T(8,128)(2,1)S(1)}, bf16[288,256]{1,0:T(8,128)(2,1)S(1)}, u32[]{:S(2)}, u32[]{:S(2)}) collective-permute-start(bf16[288,256]{1,0:T(8,128)(2,1)S(1)} %shard_map.56.refs_0_), channel_id=1, source_target_pairs={{0,2},{1,3},{2,0},{3,1},{4,6},{5,7},{6,4},{7,5},{8,10},{9,11},{10,... | collective-permute-start | bytes 442376 | tf_op jit(solution)/shard_map/ppermute | solution.py:157
  12.5 0.4 %collective-permute-done.4 = bf16[144,256]{1,0:T(8,128)(2,1)S(1)} collective-permute-done((bf16[144,256]{1,0:T(8,128)(2,1)S(1)}, bf16[144,256]{1,0:T(8,128)(2,1)S(1)}, u32[]{:S(2)}, u32[]{:S(2)}) %collective-permute-start.4) | collective-permute-done | bytes 73760 | tf_op jit(solution)/shard_map/ppermute | solution.py:157
  12.9 2.6 %collective-permute-start.5 = (bf16[144,256]{1,0:T(8,128)(2,1)S(1)}, bf16[144,256]{1,0:T(8,128)(2,1)S(1)}, u32[]{:S(2)}, u32[]{:S(2)}) collective-permute-start(bf16[144,256]{1,0:T(8,128)(2,1)S(1)} %collective-permute-done.refs_1_), channel_id=1, source_target_pairs={{0,3},{1,2},{2,1},{3,0},{4,7},{5,6},{6,5},{7,4},{8,11},{9,10},{10,... | collective-permute-start | bytes 221192 | tf_op jit(solution)/shard_map/ppermute | solution.py:157
  15.5 0.0 collective-permute-done.6.refs_2_.refs_6_
  15.5 3.5 %collective-permute-done.7.refs_3_.refs_7_ = bf16[1040,128]{1,0:T(8,128)(2,1)S(1)} collective-permute-done((bf16[1040,128]{1,0:T(8,128)(2,1)S(1)}, bf16[1040,128]{1,0:T(8,128)(2,1)S(1)}, u32[]{:S(2)}, u32[]{:S(2)}) %collective-permute-start.7) | collective-permute-done | bytes 266272 | tf_op jit(solution)/shard_map/ppermute | solution.py:154
  19.0 0.0 collective-permute-done.5
  19.0 0.0 collective-permute-done.1.refs_1_
  19.1 0.0 collective-permute-done.2.refs_2_
  19.1 0.9 %shard_map.58 = (f32[32,128]{1,0:T(8,128)S(1)}, f32[32,128]{1,0:T(8,128)S(1)}, f32[32,128]{1,0:T(8,128)S(1)}, f32[32,128]{1,0:T(8,128)S(1)}) custom-call(bf16[288,256]{1,0:T(8,128)(2,1)S(1)} %shard_map.56.refs_0_, bf16[288,256]{1,0:T(8,128)(2,1)S(1)} %collective-permute-done.1.refs_1_, bf16[288,256]{1,0:T(8,128)(2,1)S(1)} %collective-permute-done.2.refs_2_, ...), custom_call_target="tpu_custom_call" | custom-call | flops 1 | tf_op jit(solution)/shard_map/pallas_call | solution.py:215
  20.0 1.6 %collective-permute-start.10 = (f32[32,128]{1,0:T(8,128)S(1)}, f32[32,128]{1,0:T(8,128)S(1)}, u32[]{:S(2)}, u32[]{:S(2)}) collective-permute-start(f32[32,128]{1,0:T(8,128)S(1)} %get-tuple-element.28), channel_id=1, source_target_pairs={{0,16},{8,24},{16,0},{24,8},{1,17},{9,25},{17,1},{25,9},{2,18},{10... | collective-permute-start | bytes 49160 | tf_op jit(solution)/shard_map/ppermute | solution.py:154
  21.5 0.5 %collective-permute-start.8 = (f32[32,128]{1,0:T(8,128)S(1)}, f32[32,128]{1,0:T(8,128)S(1)}, u32[]{:S(2)}, u32[]{:S(2)}) collective-permute-start(f32[32,128]{1,0:T(8,128)S(1)} %get-tuple-element.26), channel_id=1, source_target_pairs={{0,24},{8,16},{16,8},{24,0},{1,25},{9,17},{17,9},{25,1},{2,26},{10... | collective-permute-start | bytes 49160 | tf_op jit(solution)/shard_map/ppermute | solution.py:154
  22.0 0.2 collective-permute-start.9
  22.2 1.6 %collective-permute-done.10 = f32[32,128]{1,0:T(8,128)S(1)} collective-permute-done((f32[32,128]{1,0:T(8,128)S(1)}, f32[32,128]{1,0:T(8,128)S(1)}, u32[]{:S(2)}, u32[]{:S(2)}) %collective-permute-start.10) | collective-permute-done | bytes 16416 | tf_op jit(solution)/shard_map/ppermute | solution.py:154
  23.8 0.9 %collective-permute-done.8 = f32[32,128]{1,0:T(8,128)S(1)} collective-permute-done((f32[32,128]{1,0:T(8,128)S(1)}, f32[32,128]{1,0:T(8,128)S(1)}, u32[]{:S(2)}, u32[]{:S(2)}) %collective-permute-start.8) | collective-permute-done | bytes 16416 | tf_op jit(solution)/shard_map/ppermute | solution.py:154
  24.7 0.0 collective-permute-done.9
  24.7 0.6 %add_add_fusion = f32[32,128]{1,0:T(8,128)} fusion(f32[32,128]{1,0:T(8,128)S(1)} %collective-permute-done.10, f32[32,128]{1,0:T(8,128)S(1)} %collective-permute-done.9, f32[32,128]{1,0:T(8,128)S(1)} %get-tuple-element.25, f32[32,128]{1,0:T(8,128)S(1)} %collective-permute-done.8), kind=kLoop, calls=%fused_computation.1 | loop fusion | flops 12288 | bytes 81920 | tf_op jit(solution)/shard_map/add | solution.py:226
  (3 shorter events, 0.0 us)
Async XLA Ops:
  1.4 5.7 %collective-permute-start.3 = (bf16[2064,128]{1,0:T(8,128)(2,1)S(1)}, bf16[2064,128]{1,0:T(8,128)(2,1)S(1)}, u32[]{:S(2)}, u32[]{:S(2)}) collective-permute-start(bf16[2064,128]{1,0:T(8,128)(2,1)S(1)} %get-tuple-element.18.refs_0_.refs_4_), channel_id=1, source_target_pairs={{0,8},{8,0},{16,24},{24,16},{1,9},{9,1},{17,25},{25,17},{2,10},{10... | collective-permute-start | bytes 1585160 | tf_op jit(solution)/shard_map/ppermute | solution.py:154
  2.0 8.1 %collective-permute-start = (bf16[144,256]{1,0:T(8,128)(2,1)S(1)}, bf16[144,256]{1,0:T(8,128)(2,1)S(1)}, u32[]{:S(2)}, u32[]{:S(2)}) collective-permute-start(bf16[144,256]{1,0:T(8,128)(2,1)S(1)} %get-tuple-element.19.refs_0_), channel_id=1, source_target_pairs={{0,4},{1,5},{2,6},{3,7},{4,0},{5,1},{6,2},{7,3},{8,12},{9,13},{10,... | collective-permute-start | bytes 221192 | tf_op jit(solution)/shard_map/ppermute | solution.py:157
  5.6 9.8 %collective-permute-start.6 = (bf16[1040,128]{1,0:T(8,128)(2,1)S(1)}, bf16[1040,128]{1,0:T(8,128)(2,1)S(1)}, u32[]{:S(2)}, u32[]{:S(2)}) collective-permute-start(bf16[1040,128]{1,0:T(8,128)(2,1)S(1)} %get-tuple-element.23), channel_id=1, source_target_pairs={{0,16},{8,24},{16,0},{24,8},{1,17},{9,25},{17,1},{25,9},{2,18},{10... | collective-permute-start | bytes 798728 | tf_op jit(solution)/shard_map/ppermute | solution.py:154
  7.1 11.9 %collective-permute-start.7 = (bf16[1040,128]{1,0:T(8,128)(2,1)S(1)}, bf16[1040,128]{1,0:T(8,128)(2,1)S(1)}, u32[]{:S(2)}, u32[]{:S(2)}) collective-permute-start(bf16[1040,128]{1,0:T(8,128)(2,1)S(1)} %get-tuple-element.24), channel_id=1, source_target_pairs={{0,24},{8,16},{16,8},{24,0},{1,25},{9,17},{17,9},{25,1},{2,26},{10... | collective-permute-start | bytes 798728 | tf_op jit(solution)/shard_map/ppermute | solution.py:154
  7.2 5.7 %collective-permute-start.4 = (bf16[144,256]{1,0:T(8,128)(2,1)S(1)}, bf16[144,256]{1,0:T(8,128)(2,1)S(1)}, u32[]{:S(2)}, u32[]{:S(2)}) collective-permute-start(bf16[144,256]{1,0:T(8,128)(2,1)S(1)} %get-tuple-element.19.refs_0_), channel_id=1, source_target_pairs={{0,3},{1,2},{2,1},{3,0},{4,7},{5,6},{6,5},{7,4},{8,11},{9,10},{10,... | collective-permute-start | bytes 221192 | tf_op jit(solution)/shard_map/ppermute | solution.py:157
  10.1 9.0 %collective-permute-start.1 = (bf16[288,256]{1,0:T(8,128)(2,1)S(1)}, bf16[288,256]{1,0:T(8,128)(2,1)S(1)}, u32[]{:S(2)}, u32[]{:S(2)}) collective-permute-start(bf16[288,256]{1,0:T(8,128)(2,1)S(1)} %shard_map.56.refs_0_), channel_id=1, source_target_pairs={{0,1},{1,0},{2,3},{3,2},{4,5},{5,4},{6,7},{7,6},{8,9},{9,8},{10,11... | collective-permute-start | bytes 442376 | tf_op jit(solution)/shard_map/ppermute | solution.py:157
  11.7 7.3 %collective-permute-start.2 = (bf16[288,256]{1,0:T(8,128)(2,1)S(1)}, bf16[288,256]{1,0:T(8,128)(2,1)S(1)}, u32[]{:S(2)}, u32[]{:S(2)}) collective-permute-start(bf16[288,256]{1,0:T(8,128)(2,1)S(1)} %shard_map.56.refs_0_), channel_id=1, source_target_pairs={{0,2},{1,3},{2,0},{3,1},{4,6},{5,7},{6,4},{7,5},{8,10},{9,11},{10,... | collective-permute-start | bytes 442376 | tf_op jit(solution)/shard_map/ppermute | solution.py:157
  12.9 6.2 %collective-permute-start.5 = (bf16[144,256]{1,0:T(8,128)(2,1)S(1)}, bf16[144,256]{1,0:T(8,128)(2,1)S(1)}, u32[]{:S(2)}, u32[]{:S(2)}) collective-permute-start(bf16[144,256]{1,0:T(8,128)(2,1)S(1)} %collective-permute-done.refs_1_), channel_id=1, source_target_pairs={{0,3},{1,2},{2,1},{3,0},{4,7},{5,6},{6,5},{7,4},{8,11},{9,10},{10,... | collective-permute-start | bytes 221192 | tf_op jit(solution)/shard_map/ppermute | solution.py:157
  20.0 3.8 %collective-permute-start.10 = (f32[32,128]{1,0:T(8,128)S(1)}, f32[32,128]{1,0:T(8,128)S(1)}, u32[]{:S(2)}, u32[]{:S(2)}) collective-permute-start(f32[32,128]{1,0:T(8,128)S(1)} %get-tuple-element.28), channel_id=1, source_target_pairs={{0,16},{8,24},{16,0},{24,8},{1,17},{9,25},{17,1},{25,9},{2,18},{10... | collective-permute-start | bytes 49160 | tf_op jit(solution)/shard_map/ppermute | solution.py:154
  21.5 3.2 %collective-permute-start.8 = (f32[32,128]{1,0:T(8,128)S(1)}, f32[32,128]{1,0:T(8,128)S(1)}, u32[]{:S(2)}, u32[]{:S(2)}) collective-permute-start(f32[32,128]{1,0:T(8,128)S(1)} %get-tuple-element.26), channel_id=1, source_target_pairs={{0,24},{8,16},{16,8},{24,0},{1,25},{9,17},{17,9},{25,1},{2,26},{10... | collective-permute-start | bytes 49160 | tf_op jit(solution)/shard_map/ppermute | solution.py:154
  22.0 2.7 %collective-permute-start.9 = (f32[32,128]{1,0:T(8,128)S(1)}, f32[32,128]{1,0:T(8,128)S(1)}, u32[]{:S(2)}, u32[]{:S(2)}) collective-permute-start(f32[32,128]{1,0:T(8,128)S(1)} %get-tuple-element.27), channel_id=1, source_target_pairs={{0,8},{8,0},{16,24},{24,16},{1,9},{9,1},{17,25},{25,17},{2,10},{10... | collective-permute-start | bytes 49160 | tf_op jit(solution)/shard_map/ppermute | solution.py:154
